TPU v7x, 32 devices: a whole 2x2x4 slice. The times are simulated.
32 devices in a mesh: dp: 4 (over z), expert: 8 (over y, x, core).
Axes of the slice: x: 2, y: 2, z: 4, core: 2. Of those that a mesh axis runs over, the one named last changes fastest.
Arguments:
- tokens: bfloat16 [4096, 2048], P(('dp', 'expert')), may hold values from -6 to 6
- routes: int32 [4096, 8], P(('dp', 'expert')), may hold values from 0 to 15, all different within a row; in each aligned block of 128 rows (0 to 127, 128 to 255, ...) at most 96 rows name the same one
- route_weights: float32 [4096, 8], P(('dp', 'expert')), may hold values from 0.05 to 0.3
- cotangent: bfloat16 [4096, 2048], P(('dp', 'expert')), may hold values from -6 to 6
- gate_proj: bfloat16 [16, 2048, 640], P('expert'), may hold values from -0.125 to 0.125
- up_proj: bfloat16 [16, 2048, 640], P('expert'), may hold values from -0.125 to 0.125
- down_proj: bfloat16 [16, 640, 2048], P('expert'), may hold values from -0.25 to 0.25
Outputs:
- layer_output: bfloat16 [4096, 2048], P(('dp', 'expert'))
- input_grad: bfloat16 [4096, 2048], P(('dp', 'expert'))
- route_weight_grad: float32 [4096, 8], P(('dp', 'expert'))
- gate_grad: float32 [2048, 16, 640], P('dp', 'expert')
- up_grad: float32 [2048, 16, 640], P('dp', 'expert')
- down_grad: float32 [2048, 16, 640], P('dp', 'expert')
Inputs may be any that keep to these rules, and one draw needn't show every extreme that they name: `routes`: each row names 8 different experts. Among the 128 rows of one device, no expert is named by more than 96 rows, a bound that some block reaches.
All inputs are finite; a program needn't handle non-finite values.
Results may differ from a plain program's by a relative error of at most 0.0095.
Values may be sent and summed in bfloat16 or wider, within the bound.
No kernel may reach another device: no remote copies, remote signals or barrier semaphores. Data moves between devices by JAX's collectives and lax.ppermute only.
A program may use at most 192 MiB of HBM per device.

v0:
```python
import jax
import jax.numpy as jnp
from jax import lax
from jax.sharding import PartitionSpec as P


def swish_parts(gate_pre):
    sig_value = jax.nn.sigmoid(gate_pre)
    return (gate_pre * sig_value, sig_value * (1.0 + gate_pre * (1.0 - sig_value)))


def project_in(arrived, gate_proj, up_proj):
    gate_pre = jnp.einsum("secd,edh->sech", arrived, gate_proj, preferred_element_type=jnp.float32)
    up_pre = jnp.einsum("secd,edh->sech", arrived, up_proj, preferred_element_type=jnp.float32)
    return (gate_pre, up_pre)


def project_out(gate_pre, up_pre, down_proj):
    swish = swish_parts(gate_pre)[0]
    hidden = (swish * up_pre).astype(jnp.bfloat16)
    return jnp.einsum(
        "sech,ehd->secd", hidden, down_proj, preferred_element_type=jnp.float32
    ).astype(jnp.bfloat16)


def three_terms(feat_rows, cot_rows, d_gate, d_up, hidden):
    return jnp.stack(
        [
            jnp.einsum("secd,sech->deh", feat_rows, d_gate, preferred_element_type=jnp.float32),
            jnp.einsum("secd,sech->deh", feat_rows, d_up, preferred_element_type=jnp.float32),
            jnp.einsum("secd,sech->deh", cot_rows, hidden, preferred_element_type=jnp.float32),
        ],
        axis=1,
    )


def on_device(tokens, routes, route_weights, cotangent, gate_proj, up_proj, down_proj):
    tok_dev, model_width = tokens.shape
    top_count = routes.shape[1]
    exp_dev = gate_proj.shape[0]
    groups = lax.axis_size("expert")
    experts = exp_dev * groups
    capacity = 3 * tok_dev * top_count // (2 * experts)
    n_routes = tok_dev * top_count
    flat_expert = routes.reshape(-1)
    onehot = (flat_expert[:, None] == jnp.arange(experts, dtype=jnp.int32)[None, :]).astype(
        jnp.int32
    )
    before = jnp.cumsum(onehot, axis=0) - onehot
    position = jnp.sum(before * onehot, axis=1)
    slot_index = flat_expert * capacity + position
    slot_source = (
        jnp.full((experts * capacity,), n_routes, jnp.int32)
        .at[slot_index]
        .set(jnp.arange(n_routes, dtype=jnp.int32))
    )
    token_of = slot_source // top_count
    padded_x = jnp.concatenate([tokens, jnp.zeros((1, model_width), tokens.dtype)], 0)
    outgoing = padded_x[token_of].reshape(groups, exp_dev, capacity, model_width)
    arrived = lax.all_to_all(outgoing, "expert", split_axis=0, concat_axis=0, tiled=True)
    gate_pre, up_pre = project_in(arrived, gate_proj, up_proj)
    expert_out, arrived, gate_pre, up_pre = (
        project_out(gate_pre, up_pre, down_proj),
        arrived,
        gate_pre,
        up_pre,
    )
    returned = lax.all_to_all(expert_out, "expert", split_axis=0, concat_axis=0, tiled=True)
    route_out = returned.reshape(experts * capacity, model_width)[slot_index].reshape(
        tok_dev, top_count, model_width
    )
    layer_output = jnp.sum(
        route_out.astype(jnp.float32) * route_weights[:, :, None], axis=1
    ).astype(jnp.bfloat16)
    route_weight_grad = jnp.einsum(
        "tkd,td->tk", route_out, cotangent, preferred_element_type=jnp.float32
    )
    route_cot = (route_weights[:, :, None] * cotangent[:, None, :].astype(jnp.float32)).astype(
        jnp.bfloat16
    )
    padded_cot = jnp.concatenate(
        [route_cot.reshape(n_routes, model_width), jnp.zeros((1, model_width), jnp.bfloat16)], 0
    )
    cot_out = padded_cot[slot_source].reshape(groups, exp_dev, capacity, model_width)
    arrived_cot = lax.all_to_all(cot_out, "expert", split_axis=0, concat_axis=0, tiled=True)
    swish, d_swish = swish_parts(gate_pre)
    hidden = (swish * up_pre).astype(jnp.bfloat16)
    d_hidden = jnp.einsum(
        "secd,ehd->sech", arrived_cot, down_proj, preferred_element_type=jnp.float32
    )
    d_gate = (d_hidden * up_pre * d_swish).astype(jnp.bfloat16)
    d_up = (d_hidden * swish).astype(jnp.bfloat16)
    route_dx = (
        jnp.einsum("sech,edh->secd", d_gate, gate_proj, preferred_element_type=jnp.float32)
        + jnp.einsum("sech,edh->secd", d_up, up_proj, preferred_element_type=jnp.float32)
    ).astype(jnp.bfloat16)
    dx_back = lax.all_to_all(route_dx, "expert", split_axis=0, concat_axis=0, tiled=True)
    token_dx = dx_back.reshape(experts * capacity, model_width)[slot_index].reshape(
        tok_dev, top_count, model_width
    )
    input_grad = jnp.sum(token_dx.astype(jnp.float32), axis=1).astype(jnp.bfloat16)
    full_terms = three_terms(arrived, arrived_cot, d_gate, d_up, hidden)
    shares = lax.psum_scatter(
        full_terms.astype(jnp.bfloat16), "dp", scatter_dimension=0, tiled=True
    ).astype(jnp.float32)
    return (layer_output, input_grad, route_weight_grad, shares[:, 0], shares[:, 1], shares[:, 2])


def solution(mesh):
    placed = (
        P(("dp", "expert"), None),
        P(("dp", "expert"), None),
        P(("dp", "expert"), None),
        P(("dp", "expert"), None),
        P("expert", None, None),
        P("expert", None, None),
        P("expert", None, None),
    )
    return jax.shard_map(
        on_device,
        mesh=mesh,
        in_specs=placed,
        out_specs=(
            P(("dp", "expert"), None),
            P(("dp", "expert"), None),
            P(("dp", "expert"), None),
            P("dp", "expert", None),
            P("dp", "expert", None),
            P("dp", "expert", None),
        ),
        check_vma=False,
    )
```

profile of v0, /device:TPU:0, one launch (start us, length us, event | category | flops | bytes accessed | tf_op | source)
XLA Modules:
  0.0 521.4 jit_solution(13140044641961346660)
XLA Ops:
  7.2 0.7 broadcast_multiply_fusion
  7.9 0.8 copy.34
  8.6 0.1 eq.29
  8.8 0.1 copy.33
  8.9 0.1 mul.70
  9.0 4.5 reduce-window.6
  13.6 0.1 copy.36
  14.0 4.3 scatter_custom_fusion
  18.4 1.1 concatenate.6
  19.5 7.1 %gather_fusion = bf16[1536,2048]{1,0:T(8,128)(2,1)} fusion(bf16[129,2048]{1,0:T(8,128)(2,1)S(1)} %concatenate.6, s32[2048]{0:T(1024)S(1)} %get-tuple-element.33), kind=kCustom, calls=%fused_computation | custom fusion | bytes 12589056 | tf_op jit(solution)/shard_map/gather | solution.py:59
  26.6 5.3 %all-to-all-start = ((bf16[8,2,96,2048]{3,2,1,0:T(8,128)(2,1)}), bf16[8,2,96,2048]{3,2,1,0:T(8,128)(2,1)}, u32[]{:S(2)}, u32[]{:S(2)}) async-start(bf16[8,2,96,2048]{3,2,1,0:T(8,128)(2,1)} %bitcast.145), calls=%async_computation | async-start | bytes 12582912 | tf_op jit(solution)/shard_map/all_to_all | solution.py:60
  31.9 0.1 copy.41
  32.1 0.1 convert_element_type.56
  32.2 0.9 fusion
  33.2 2.3 concatenate.7
  35.5 15.5 %gather_fusion.2 = bf16[1536,2048]{1,0:T(8,128)(2,1)} fusion(bf16[1025,2048]{1,0:T(8,128)(2,1)} %concatenate.7, s32[2048]{0:T(1024)S(1)} %get-tuple-element.32), kind=kCustom, calls=%fused_computation.2 | custom fusion | bytes 12589056 | tf_op jit(solution)/shard_map/gather | solution.py:84
  51.0 52.8 %all-to-all-done = bf16[8,2,96,2048]{3,2,1,0:T(8,128)(2,1)} async-done(((bf16[8,2,96,2048]{3,2,1,0:T(8,128)(2,1)}), bf16[8,2,96,2048]{3,2,1,0:T(8,128)(2,1)}, u32[]{:S(2)}, u32[]{:S(2)}) %all-to-all-start) | async-done | bytes 6291488 | tf_op jit(solution)/shard_map/all_to_all | solution.py:60
  103.8 4.7 all-to-all-start.2
  108.5 0.3 reduce-scatter.2.cloned.1.call-start
  108.8 10.0 %fusion.11 = f32[2,8,96,640]{3,2,1,0:T(8,128)} fusion(bf16[2,2048,640]{2,1,0:T(8,128)(2,1)} %param.12, bf16[8,2,96,2048]{3,2,1,0:T(8,128)(2,1)} %all-to-all-done), kind=kOutput, calls=%fused_computation.24 | convolution fusion | flops 4026531840 | bytes 15466496 | tf_op jit(solution)/shard_map/secd,edh->sech/dot_general | solution.py:14
  118.7 9.9 %fusion.15 = f32[2,8,96,640]{3,2,1,0:T(8,128)} fusion(bf16[2,2048,640]{2,1,0:T(8,128)(2,1)} %param.11, bf16[8,2,96,2048]{3,2,1,0:T(8,128)(2,1)} %all-to-all-done), kind=kOutput, calls=%fused_computation.28 | convolution fusion | flops 4026531840 | bytes 15466496 | tf_op jit(solution)/shard_map/secd,edh->sech/dot_general | solution.py:13
  128.7 51.4 %all-to-all-done.2 = bf16[8,2,96,2048]{3,2,1,0:T(8,128)(2,1)} async-done(((bf16[8,2,96,2048]{3,2,1,0:T(8,128)(2,1)}), bf16[8,2,96,2048]{3,2,1,0:T(8,128)(2,1)}, u32[]{:S(2)}, u32[]{:S(2)}) %all-to-all-start.2) | async-done | bytes 6291488 | tf_op jit(solution)/shard_map/all_to_all | solution.py:85
  180.1 12.1 %fusion.33 = (bf16[8,2,96,640]{3,2,0,1:T(8,128)(2,1)S(1)}, bf16[8,2,96,640]{3,2,0,1:T(8,128)(2,1)S(1)}, bf16[8,2,96,640]{3,2,0,1:T(8,128)(2,1)}) fusion(f32[2,8,96,640]{3,2,1,0:T(8,128)} %fusion.11, f32[2,8,96,640]{3,2,1,0:T(8,128)} %fusion.15, bf16[2,640,2048]{2,1,0:T(8,128)(2,1)} %param.13, bf16[8,2,96,2048]{3,2,1,0:T(8,128)(2,1)} %all-to-all-done.2), kind=kOutput, calls=%fused_computation.43 | convolution fusion | flops 4041277440 | bytes 25296896 | tf_op jit(solution)/shard_map/secd,ehd->sech/dot_general | solution.py:88
  192.2 7.9 %fusion.8 = bf16[2048,1,2,640]{0,3,2,1:T(8,128)(2,1)S(1)} fusion(bf16[8,2,96,640]{3,2,0,1:T(8,128)(2,1)S(1)} %get-tuple-element.28, bf16[8,2,96,2048]{3,2,1,0:T(8,128)(2,1)} %all-to-all-done.2), kind=kOutput, calls=%fused_computation.21 | convolution fusion | flops 4029153280 | bytes 13500416 | tf_op jit(solution)/shard_map/secd,sech->deh/dot_general | solution.py:31
  200.0 7.1 %fusion.6 = bf16[2048,1,2,640]{0,3,2,1:T(8,128)(2,1)S(1)} fusion(bf16[8,2,96,640]{3,2,0,1:T(8,128)(2,1)S(1)} %get-tuple-element.27, bf16[8,2,96,2048]{3,2,1,0:T(8,128)(2,1)} %all-to-all-done), kind=kOutput, calls=%fused_computation.19 | convolution fusion | flops 4029153280 | bytes 13500416 | tf_op jit(solution)/shard_map/secd,sech->deh/dot_general | solution.py:29
  207.1 17.3 %fusion.7 = bf16[2048,1,2,640]{0,3,2,1:T(8,128)(2,1)S(1)} fusion(bf16[8,2,96,640]{3,2,0,1:T(8,128)(2,1)} %get-tuple-element.29, bf16[8,2,96,2048]{3,2,1,0:T(8,128)(2,1)} %all-to-all-done), kind=kOutput, calls=%fused_computation.20 | convolution fusion | flops 4029153280 | bytes 13500416 | tf_op jit(solution)/shard_map/secd,sech->deh/dot_general | solution.py:30
  224.4 6.8 %pad_maximum_fusion = bf16[2048,3,2,640]{0,3,2,1:T(8,128)(2,1)} fusion(bf16[2048,1,2,640]{0,3,2,1:T(8,128)(2,1)S(1)} %fusion.8, bf16[2048,1,2,640]{0,3,2,1:T(8,128)(2,1)S(1)} %fusion.7, bf16[2048,1,2,640]{0,3,2,1:T(8,128)(2,1)S(1)} %fusion.6), kind=kLoop, calls=%fused_computation.5 | loop fusion | flops 15728640 | bytes 31457280 | tf_op jit(solution)/shard_map/stack | solution.py:27
  231.2 8.1 %convert_bitcast_fusion = bf16[8,2,96,2048]{3,2,0,1:T(8,128)(2,1)S(1)} fusion(bf16[8,2,96,640]{3,2,0,1:T(8,128)(2,1)} %copy-done.7, bf16[2,640,2048]{2,1,0:T(8,128)(2,1)} %param.13), kind=kOutput, calls=%fused_computation.14 | convolution fusion | flops 4029677568 | bytes 13500416 | tf_op jit(solution)/shard_map/sech,ehd->secd/dot_general | solution.py:21
  239.3 3.2 copy.40
  242.5 4.7 all-to-all-start.1
  247.2 10.8 %fusion.9 = f32[2,8,96,2048]{3,2,1,0:T(8,128)} fusion(bf16[8,2,96,640]{3,2,0,1:T(8,128)(2,1)} %get-tuple-element.29, bf16[2,2048,640]{2,1,0:T(8,128)(2,1)} %param.12), kind=kOutput, calls=%fused_computation.22 | convolution fusion | flops 4026531840 | bytes 19791872 | tf_op jit(solution)/shard_map/sech,edh->secd/dot_general | solution.py:95
  258.0 9.7 %fusion.1 = bf16[8,2,96,2048]{3,2,0,1:T(8,128)(2,1)S(1)} fusion(f32[2,8,96,2048]{3,2,1,0:T(8,128)} %fusion.9, bf16[8,2,96,640]{3,2,0,1:T(8,128)(2,1)S(1)} %get-tuple-element.27, bf16[2,2048,640]{2,1,0:T(8,128)(2,1)} %param.11), kind=kOutput, calls=%fused_computation.13 | convolution fusion | flops 4032823296 | bytes 26083328 | tf_op jit(solution)/shard_map/sech,edh->secd/dot_general | solution.py:94
  267.7 3.8 copy.44
  271.6 47.2 %all-to-all-done.1 = bf16[8,2,96,2048]{3,2,1,0:T(8,128)(2,1)} async-done(((bf16[8,2,96,2048]{3,2,1,0:T(8,128)(2,1)}), bf16[8,2,96,2048]{3,2,1,0:T(8,128)(2,1)}, u32[]{:S(2)}, u32[]{:S(2)}) %all-to-all-start.1) | async-done | bytes 6291488 | tf_op jit(solution)/shard_map/all_to_all | solution.py:68
  318.8 4.8 all-to-all-start.3
  323.6 12.4 %gather_fusion.1 = bf16[1024,2048]{1,0:T(8,128)(2,1)} fusion(bf16[1536,2048]{1,0:T(8,128)(2,1)} %bitcast.14, s32[1024]{0:T(1024)S(1)} %broadcast_clamp_fusion), kind=kCustom, calls=%fused_computation.1 | custom fusion | bytes 8392704 | tf_op jit(solution)/shard_map/gather | solution.py:69
  336.0 5.0 fusion.24
  341.1 0.7 copy.55
  341.7 53.4 %all-to-all-done.3 = bf16[8,2,96,2048]{3,2,1,0:T(8,128)(2,1)} async-done(((bf16[8,2,96,2048]{3,2,1,0:T(8,128)(2,1)}), bf16[8,2,96,2048]{3,2,1,0:T(8,128)(2,1)}, u32[]{:S(2)}, u32[]{:S(2)}) %all-to-all-start.3) | async-done | bytes 6291488 | tf_op jit(solution)/shard_map/all_to_all | solution.py:97
  395.2 12.7 %gather_fusion.3 = bf16[1024,2048]{1,0:T(8,128)(2,1)} fusion(bf16[1536,2048]{1,0:T(8,128)(2,1)} %bitcast.23, s32[1024]{0:T(1024)S(1)} %broadcast_clamp_fusion), kind=kCustom, calls=%fused_computation.3 | custom fusion | bytes 8392704 | tf_op jit(solution)/shard_map/gather | solution.py:98
  407.9 6.0 %bitcast_reduce_fusion = bf16[128,2048]{1,0:T(8,128)(2,1)} fusion(bf16[1024,2048]{1,0:T(8,128)(2,1)} %gather_fusion.3), kind=kLoop, calls=%fused_computation.33 | loop fusion | flops 1835008 | bytes 4718592 | tf_op jit(solution)/shard_map/reduce_sum | solution.py:101
  413.9 5.2 multiply_reduce_fusion
  419.1 75.1 %reduce-scatter.2.cloned.1.call-done = bf16[512,3,2,640]{0,3,2,1:T(8,128)(2,1)} async-done(((bf16[2048,3,2,640]{0,3,2,1:T(8,128)(2,1)}), bf16[512,3,2,640]{0,3,2,1:T(8,128)(2,1)}) %reduce-scatter.2.cloned.1.call-update) | async-done | bytes 3932176 | tf_op jit(solution)/shard_map/reduce_scatter | solution.py:103
  494.2 3.2 convert_element_type.62
  497.4 3.6 slice_bitcast_fusion
  501.0 5.1 copy.50
  506.1 5.1 copy.49
  511.2 3.1 copy.48
  (31 shorter events, 0.6 us)
Async XLA Ops:
  14.0 4.4 copy-start.4
  26.6 5.3 %copy-start.6 = (f32[128,8]{0,1:T(8,128)S(1)}, f32[128,8]{0,1:T(8,128)}, u32[]{:S(2)}) copy-start(f32[128,8]{0,1:T(8,128)} %param.9) | copy-start | bytes 12292
  26.6 5.5 %copy-start.3 = (bf16[128,2048]{1,0:T(8,128)(2,1)S(1)}, bf16[128,2048]{1,0:T(8,128)(2,1)}, u32[]{:S(2)}) copy-start(bf16[128,2048]{1,0:T(8,128)(2,1)} %param.10) | copy-start | bytes 1572868
  26.6 77.1 %all-to-all-start = ((bf16[8,2,96,2048]{3,2,1,0:T(8,128)(2,1)}), bf16[8,2,96,2048]{3,2,1,0:T(8,128)(2,1)}, u32[]{:S(2)}, u32[]{:S(2)}) async-start(bf16[8,2,96,2048]{3,2,1,0:T(8,128)(2,1)} %bitcast.145), calls=%async_computation | async-start | bytes 12582912 | tf_op jit(solution)/shard_map/all_to_all | solution.py:60
  32.0 3.5 copy-start.1
  103.8 76.3 %all-to-all-start.2 = ((bf16[8,2,96,2048]{3,2,1,0:T(8,128)(2,1)}), bf16[8,2,96,2048]{3,2,1,0:T(8,128)(2,1)}, u32[]{:S(2)}, u32[]{:S(2)}) async-start(bf16[8,2,96,2048]{3,2,1,0:T(8,128)(2,1)} %bitcast.146), calls=%async_computation.2 | async-start | bytes 12582912 | tf_op jit(solution)/shard_map/all_to_all | solution.py:85
  108.5 385.7 %reduce-scatter.2.cloned.1.call-start = ((), (), s32[]{:S(2)}) async-start(), calls=%async_computation.5 | async-start | bytes 19660800 | tf_op jit(solution)/shard_map/reduce_scatter | solution.py:103
  192.2 7.9 %copy-start.7 = (bf16[8,2,96,640]{3,2,0,1:T(8,128)(2,1)}, bf16[8,2,96,640]{3,2,0,1:T(8,128)(2,1)S(1)}, u32[]{:S(2)}) copy-start(bf16[8,2,96,640]{3,2,0,1:T(8,128)(2,1)S(1)} %get-tuple-element.28) | copy-start | bytes 5898244
  242.5 76.3 %all-to-all-start.1 = ((bf16[8,2,96,2048]{3,2,1,0:T(8,128)(2,1)}), bf16[8,2,96,2048]{3,2,1,0:T(8,128)(2,1)}, u32[]{:S(2)}, u32[]{:S(2)}) async-start(bf16[8,2,96,2048]{3,2,1,0:T(8,128)(2,1)} %copy.40), calls=%async_computation.1 | async-start | bytes 12582912 | tf_op jit(solution)/shard_map/all_to_all | solution.py:68
  271.6 52.0 %copy-start.5 = (s32[1024,1]{0,1:T(1,128)S(1)}, s32[1024,1]{0,1:T(1,128)}, u32[]{:S(2)}) copy-start(s32[1024,1]{0,1:T(1,128)} %copy-done.4) | copy-start | bytes 12292
  318.8 76.4 %all-to-all-start.3 = ((bf16[8,2,96,2048]{3,2,1,0:T(8,128)(2,1)}), bf16[8,2,96,2048]{3,2,1,0:T(8,128)(2,1)}, u32[]{:S(2)}, u32[]{:S(2)}) async-start(bf16[8,2,96,2048]{3,2,1,0:T(8,128)(2,1)} %copy.44), calls=%async_computation.3 | async-start | bytes 12582912 | tf_op jit(solution)/shard_map/all_to_all | solution.py:97
  395.2 18.7 %copy-start.2 = (f32[128,8]{1,0:T(8,128)S(1)}, f32[128,8]{1,0:T(8,128)}, u32[]{:S(2)}) copy-start(f32[128,8]{1,0:T(8,128)} %copy-done.1) | copy-start | bytes 12292
  407.9 6.0 %copy-start = (bf16[1024,2048]{1,0:T(8,128)(2,1)S(1)}, bf16[1024,2048]{1,0:T(8,128)(2,1)}, u32[]{:S(2)}) copy-start(bf16[1024,2048]{1,0:T(8,128)(2,1)} %gather_fusion.1) | copy-start | bytes 12582916
Sparse Core Ops, SparseCore 0:
  231.3 262.8 reduce-scatter.1
where the time goes:
time: 523 us; the launch traced here: 521 us
  waiting for transfers between devices  280 us (54%)
  matrix products  97.8 us (19%)
  local copies, waits for them, and re-layouts  81.7 us (16%)
  other arithmetic  27.6 us (5%)
  starting transfers between devices  19.8 us (4%)
  between operations  14.5 us (3%)
    reduce_scatter x1, waiting for transfers between devices, on_device(): lax.psum_scatter(full_terms.astype(jnp.bfloat16), 'dp', scatter_dimension...  75.1 us
    all_to_all x1, waiting for transfers between devices, on_device(): lax.all_to_all(route_dx, 'expert', split_axis=0, concat_axis=0, tiled=True)  53.4 us
    all_to_all x1, waiting for transfers between devices, on_device(): lax.all_to_all(outgoing, 'expert', split_axis=0, concat_axis=0, tiled=True)  52.8 us
    all_to_all x1, waiting for transfers between devices, on_device(): lax.all_to_all(cot_out, 'expert', split_axis=0, concat_axis=0, tiled=True)  51.4 us
    all_to_all x1, waiting for transfers between devices, on_device(): lax.all_to_all(expert_out, 'expert', split_axis=0, concat_axis=0, tiled=T...  47.2 us
    dot_general x1, matrix products, three_terms(): jnp.einsum('secd,sech->deh', feat_rows, d_up, preferred_element_type=jnp....  17.3 us
    gather x1, local copies, waits for them, and re-layouts, on_device(): padded_cot[slot_source].reshape(groups, exp_dev, capacity, model_width)  15.5 us
    unnamed x21, local copies, waits for them, and re-layouts  14.2 us
  transfers between devices with their start and end apart: 5, of which 5 were waited for; matrix products, arithmetic and copies ran while one was open for 22% of the time, Pallas kernels for 0%

commit v1 on v0

v1 whole, which is shorter than its diff:
```python
import functools

import jax
import jax.numpy as jnp
from jax import lax
from jax.experimental import pallas as pl
from jax.experimental.pallas import tpu as pltpu
from jax.sharding import PartitionSpec as P

VMEM_BYTES = 56 * 1024 * 1024


def swap(value, axis, mask):
    return lax.ppermute(value, axis, [(i, i ^ mask) for i in range(lax.axis_size(axis))])


def way_bits(axis):
    bits = [1 << b for b in range(1, lax.axis_size(axis).bit_length() - 1)]
    return list(zip(bits, bits[::-1]))


def gather_rows(own, axis):
    half = own.shape[0] // 2
    first, second = own[:half], own[half:]
    for bit_first, bit_second in way_bits(axis):
        first, second = (
            jnp.concatenate([first, swap(first, axis, bit_first)], 0),
            jnp.concatenate([second, swap(second, axis, bit_second)], 0),
        )
    both = jnp.concatenate([first, second], 0)
    return jnp.concatenate([both, swap(both, axis, 1)], 0)


def add_to(kept, received):
    return (kept.astype(jnp.float32) + received.astype(jnp.float32)).astype(kept.dtype)


def scatter_rows(parts, axis):
    half = parts.shape[0] // 2
    both = add_to(parts[:half], swap(parts[half:], axis, 1))
    half = half // 2
    first, second = both[:half], both[half:]
    for bit_first, bit_second in way_bits(axis)[::-1]:
        half = half // 2
        first, second = (
            add_to(first[:half], swap(first[half:], axis, bit_first)),
            add_to(second[:half], swap(second[half:], axis, bit_second)),
        )
    return jnp.concatenate([first, second], 0)


def routes_kernel(hid, x_ref, c_ref, w_ref, wgu_ref, wd_ref, hw_ref, dgu_ref, rwg_ref):
    cols = wd_ref.shape[0]
    x, c = x_ref[...], c_ref[...]
    weight = w_ref[...]
    step = 256 if cols % 256 == 0 else 128
    sums = [jnp.zeros((x.shape[0], 1), jnp.float32) for _ in range(cols // hid)]
    for start in range(0, cols, step):
        gate = jnp.dot(x, wgu_ref[:, start : start + step], preferred_element_type=jnp.float32)
        up = jnp.dot(
            x, wgu_ref[:, cols + start : cols + start + step], preferred_element_type=jnp.float32
        )
        d_plain = lax.dot_general(
            c,
            wd_ref[start : start + step, :],
            (((1,), (1,)), ((), ())),
            preferred_element_type=jnp.float32,
        )
        sig = jax.nn.sigmoid(gate)
        swish = gate * sig
        d_swish = sig * (1.0 + gate * (1.0 - sig))
        hidden = swish * up
        product = hidden * d_plain
        for lane in range(0, step, 128):
            here = slice(lane, lane + 128)
            e = (start + lane) // hid
            w = weight[:, e : e + 1]
            d_hidden = d_plain[:, here] * w
            at = start + lane
            hw_ref[:, at : at + 128] = (hidden[:, here] * w).astype(jnp.bfloat16)
            dgu_ref[:, at : at + 128] = (d_hidden * up[:, here] * d_swish[:, here]).astype(
                jnp.bfloat16
            )
            dgu_ref[:, cols + at : cols + at + 128] = (d_hidden * swish[:, here]).astype(
                jnp.bfloat16
            )
            sums[e] = sums[e] + jnp.sum(product[:, here], axis=1, keepdims=True)
    rwg_ref[...] = jnp.concatenate(sums, axis=1)


def routes_pass(x, c, weight, wgu, wd, hid):
    rows, width = x.shape
    cols = wd.shape[0]
    tile = min(256, rows)
    return pl.pallas_call(
        functools.partial(routes_kernel, hid),
        grid=(rows // tile,),
        in_specs=[
            pl.BlockSpec((tile, width), lambda i: (i, 0)),
            pl.BlockSpec((tile, width), lambda i: (i, 0)),
            pl.BlockSpec((tile, weight.shape[1]), lambda i: (i, 0)),
            pl.BlockSpec(wgu.shape, lambda i: (0, 0), pipeline_mode=pl.Buffered(1)),
            pl.BlockSpec(wd.shape, lambda i: (0, 0), pipeline_mode=pl.Buffered(1)),
        ],
        out_specs=[
            pl.BlockSpec((tile, cols), lambda i: (i, 0)),
            pl.BlockSpec((tile, 2 * cols), lambda i: (i, 0)),
            pl.BlockSpec((tile, weight.shape[1]), lambda i: (i, 0)),
        ],
        out_shape=[
            jax.ShapeDtypeStruct((rows, cols), jnp.bfloat16),
            jax.ShapeDtypeStruct((rows, 2 * cols), jnp.bfloat16),
            jax.ShapeDtypeStruct((rows, weight.shape[1]), jnp.float32),
        ],
        compiler_params=pltpu.CompilerParams(vmem_limit_bytes=VMEM_BYTES),
        cost_estimate=pl.CostEstimate(
            flops=6 * rows * width * cols,
            bytes_accessed=2 * (2 * rows * width + 3 * width * cols + 3 * rows * cols),
            transcendentals=rows * cols,
        ),
        name="routes_pass",
    )(x, c, weight, wgu, wd)


def halving_plan(masks):
    keep = [0]
    for mask in masks[1:]:
        keep = keep + [mask ^ k for k in keep]
    return keep, [masks[0] ^ k for k in keep]


def slots_of(order, wanted):
    slots, writes, last = [], [], wanted.index(next(r for r in order if r in wanted))
    for rel in order:
        if rel in wanted:
            last = wanted.index(rel)
        slots.append(last)
        writes.append(int(rel in wanted))
    return slots, writes


def grad_kernel(block_ref, slot_ref, write_ref, src_ref, rhs_ref, *outs):
    j = pl.program_id(0)
    hid = outs[0].shape[-1]
    value = lax.dot_general(
        src_ref[...], rhs_ref[...], (((0,), (0,)), ((), ())), preferred_element_type=jnp.float32
    ).astype(jnp.bfloat16)
    for n, out in enumerate(outs):

        @pl.when(write_ref[n, j] == 1)
        def _(out=out, e=n // 2):
            out[...] = value[None, :, e * hid : (e + 1) * hid]


def grad_pass(src, rhs, part, experts, n_dp, masks, relative):
    rows, width = src.shape
    own = width // n_dp
    cols = rhs.shape[1] // part[1]
    hid = cols // experts
    plans = [halving_plan(masks if e % 2 == 0 else masks[::-1]) for e in range(experts)]
    order = [r for r in range(1, n_dp)] + [0]
    slots, writes = [], []
    for keep, send in plans:
        for wanted in (keep, send):
            s, w = slots_of(order, wanted)
            slots.append(s)
            writes.append(w)
    blocks = relative[jnp.array(order, jnp.int32)]
    specs = [
        pl.BlockSpec((1, own, hid), functools.partial(lambda n, j, b, s, w: (s[n, j], 0, 0), n))
        for n in range(2 * experts)
    ]
    outs = pl.pallas_call(
        grad_kernel,
        grid_spec=pltpu.PrefetchScalarGridSpec(
            num_scalar_prefetch=3,
            grid=(n_dp,),
            in_specs=[
                pl.BlockSpec((rows, own), lambda j, b, s, w: (0, b[j])),
                pl.BlockSpec(
                    (rows, cols), lambda j, b, s, w: (0, part[0]), pipeline_mode=pl.Buffered(1)
                ),
            ],
            out_specs=specs,
        ),
        out_shape=[jax.ShapeDtypeStruct((n_dp // 2, own, hid), jnp.bfloat16)] * (2 * experts),
        compiler_params=pltpu.CompilerParams(vmem_limit_bytes=VMEM_BYTES),
        cost_estimate=pl.CostEstimate(
            flops=2 * rows * width * cols,
            bytes_accessed=2 * (rows * width + rows * cols + width * cols),
            transcendentals=0,
        ),
        name="grad_pass",
    )(blocks, jnp.array(slots, jnp.int32), jnp.array(writes, jnp.int32), src, rhs)
    return [(outs[2 * e], outs[2 * e + 1]) for e in range(experts)]


def reduce_blocks(keep, send, masks, axis):
    for n, mask in enumerate(masks):
        got = swap(send, axis, mask)
        if n == len(masks) - 1:
            return keep[0].astype(jnp.float32) + got[0].astype(jnp.float32)
        total = add_to(keep, got)
        half = total.shape[0] // 2
        keep, send = total[:half], total[half:]


def on_device(tokens, routes, route_weights, cotangent, gate_proj, up_proj, down_proj):
    width = tokens.shape[1]
    exp_dev, hid = down_proj.shape[:2]
    groups = lax.axis_size("expert")
    n_dp = lax.axis_size("dp")
    experts = exp_dev * groups
    mine = lax.axis_index("expert") * exp_dev
    masks = [(2 << b) - 1 for b in range(n_dp.bit_length() - 1)]
    relative = lax.axis_index("dp") ^ jnp.arange(n_dp, dtype=jnp.int32)

    named = routes[:, :, None] == jnp.arange(experts, dtype=jnp.int32)[None, None, :]
    dense = jnp.sum(jnp.where(named, route_weights[:, :, None], 0.0), axis=1)
    x = gather_rows(tokens, "expert")
    c = gather_rows(cotangent, "expert")
    weight = lax.dynamic_slice_in_dim(gather_rows(dense, "expert"), mine, exp_dev, 1)

    wgu = jnp.concatenate([gate_proj[e] for e in range(exp_dev)] + [up_proj[e] for e in range(exp_dev)], 1)
    wd = down_proj.reshape(exp_dev * hid, width)
    hw, dgu, rwg = routes_pass(x, c, weight, wgu, wd, hid)

    gate_parts = grad_pass(x, dgu, (0, 2), exp_dev, n_dp, masks, relative)
    up_parts = grad_pass(x, dgu, (1, 2), exp_dev, n_dp, masks, relative)
    down_parts = grad_pass(c, hw, (0, 1), exp_dev, n_dp, masks, relative)
    grads = [
        jnp.stack(
            [
                reduce_blocks(keep, send, masks if e % 2 == 0 else masks[::-1], "dp")
                for e, (keep, send) in enumerate(parts)
            ],
            axis=1,
        )
        for parts in (gate_parts, up_parts, down_parts)
    ]

    out = jnp.dot(hw, wd, preferred_element_type=jnp.float32).astype(jnp.bfloat16)
    dx = lax.dot_general(
        dgu, wgu, (((1,), (1,)), ((), ())), preferred_element_type=jnp.float32
    ).astype(jnp.bfloat16)
    layer_output = scatter_rows(out, "expert")
    input_grad = scatter_rows(dx, "expert")
    spread = lax.dynamic_update_slice_in_dim(
        jnp.zeros((rwg.shape[0], experts), jnp.float32), rwg, mine, 1
    )
    rwg_dense = scatter_rows(spread, "expert")
    route_weight_grad = jnp.sum(jnp.where(named, rwg_dense[:, None, :], 0.0), axis=2)
    return (layer_output, input_grad, route_weight_grad, *grads)


def solution(mesh):
    rows = P(("dp", "expert"), None)
    held = P("expert", None, None)
    owned = P("dp", "expert", None)
    return jax.shard_map(
        on_device,
        mesh=mesh,
        in_specs=(rows, rows, rows, rows, held, held, held),
        out_specs=(rows, rows, rows, owned, owned, owned),
        check_vma=False,
    )
```

time: 523 us -> 462 us (0.88)
  starting transfers between devices: 19.8 us -> 128 us
  waiting for transfers between devices: 280 us -> 190 us
  matrix products: 97.8 us -> 25 us
  Pallas kernels: 0 us -> 60.7 us
  local copies, waits for them, and re-layouts: 81.7 us -> 40 us
  between operations: 14.5 us -> 1.28 us
  other arithmetic: 27.6 us -> 16.3 us
    all_to_all x4 -> x0, waiting for transfers between devices: 205 us -> none  [the longest x1 53.4 us: on_device(): lax.all_to_all(route_dx, 'expert', split_axis=0, concat_axis=0, tiled=True)]
    ppermute x0 -> x42, waiting for transfers between devices: none -> 190 us  [swap(): lax.ppermute(value, axis, [(i, i ^ mask) for i in range(lax.axis_size(axi...]
    ppermute x0 -> x42, starting transfers between devices: none -> 128 us  [swap(): lax.ppermute(value, axis, [(i, i ^ mask) for i in range(lax.axis_size(axi...]
    reduce_scatter x1 -> x0, waiting for transfers between devices: 75.1 us -> none  [on_device(): lax.psum_scatter(full_terms.astype(jnp.bfloat16), 'dp', scatter_dimension...]
    dot_general x10 -> x2, matrix products: 97.8 us -> 25 us  [the longest x1 16.3 us: on_device(): lax.dot_general(dgu, wgu, (((1,), (1,)), ((), ())), preferred_element_typ...]
    pallas_call x0 -> x4, Pallas kernels: none -> 60.7 us  [the longest x3 34.7 us: grad_pass(): pl.pallas_call(grad_kernel, grid_spec=pltpu.PrefetchScalarGridSpec(num_sc...]
    gather x4 -> x1, local copies, waits for them, and re-layouts: 47.7 us -> 1.14 us  [grad_pass(): blocks = relative[jnp.array(order, jnp.int32)]]
    all_to_all x4 -> x0, starting transfers between devices: 19.5 us -> none  [the longest x1 5.3 us: on_device(): lax.all_to_all(outgoing, 'expert', split_axis=0, concat_axis=0, tiled=True)]
  transfers between devices with their start and end apart: 5 -> 42, of which waited for: 5 -> 26; matrix products, arithmetic and copies ran while one was open for 22% -> 15% of each run, Pallas kernels for 0% -> 8%
where the time goes in v1:
time: 462 us; the launch traced here: 461 us
  waiting for transfers between devices  190 us (41%)
  starting transfers between devices  128 us (28%)
  Pallas kernels  60.7 us (13%)
  local copies, waits for them, and re-layouts  40 us (9%)
  matrix products  25 us (5%)
  other arithmetic  16.3 us (4%)
    ppermute x42, waiting for transfers between devices, swap(): lax.ppermute(value, axis, [(i, i ^ mask) for i in range(lax.axis_size(axi...  190 us
    ppermute x42, starting transfers between devices, swap(): lax.ppermute(value, axis, [(i, i ^ mask) for i in range(lax.axis_size(axi...  128 us
    pallas_call x3, Pallas kernels, grad_pass(): pl.pallas_call(grad_kernel, grid_spec=pltpu.PrefetchScalarGridSpec(num_sc...  34.7 us
    unnamed x70, local copies, waits for them, and re-layouts  26.4 us
    pallas_call x1, Pallas kernels, routes_pass(): pl.pallas_call(functools.partial(routes_kernel, hid), grid=(rows // tile,...  26 us
    dot_general x1, matrix products, on_device(): lax.dot_general(dgu, wgu, (((1,), (1,)), ((), ())), preferred_element_typ...  16.3 us
  transfers between devices with their start and end apart: 42, of which 26 were waited for; matrix products, arithmetic and copies ran while one was open for 15% of the time, Pallas kernels for 8%

profile of v1, /device:TPU:0, one launch (start us, length us, event | category | flops | bytes accessed | tf_op | source)
XLA Modules:
  0.0 461.1 jit_solution(16294510614196566280)
XLA Ops:
  0.6 1.7 constant_dynamic-update-slice_fusion.18
  2.3 2.9 collective-permute-start.5
  5.3 1.7 constant_dynamic-update-slice_fusion.5
  7.8 2.0 collective-permute-start.10
  12.5 2.2 collective-permute-start.6
  14.6 2.7 collective-permute-done
  17.3 1.8 collective-permute-start.1
  20.6 6.8 %collective-permute-done.6 = bf16[128,2048]{1,0:T(8,128)(2,1)S(1)} collective-permute-done((bf16[128,2048]{1,0:T(8,128)(2,1)S(1)}, bf16[128,2048]{1,0:T(8,128)(2,1)S(1)}, u32[]{:S(2)}, u32[]{:S(2)}) %collective-permute-start.6) | collective-permute-done | bytes 524320 | tf_op jit(solution)/shard_map/ppermute | solution.py:14
  29.1 2.0 collective-permute-start.7
  31.2 7.5 %collective-permute-done.1 = bf16[128,2048]{1,0:T(8,128)(2,1)S(1)} collective-permute-done((bf16[128,2048]{1,0:T(8,128)(2,1)S(1)}, bf16[128,2048]{1,0:T(8,128)(2,1)S(1)}, u32[]{:S(2)}, u32[]{:S(2)}) %collective-permute-start.1) | collective-permute-done | bytes 524320 | tf_op jit(solution)/shard_map/ppermute | solution.py:14
  40.3 2.0 collective-permute-start.2
  42.4 1.9 collective-permute-done.7
  50.3 8.4 %collective-permute-done.8 = bf16[128,2048]{1,0:T(8,128)(2,1)S(1)} collective-permute-done((bf16[128,2048]{1,0:T(8,128)(2,1)S(1)}, bf16[128,2048]{1,0:T(8,128)(2,1)S(1)}, u32[]{:S(2)}, u32[]{:S(2)}) %collective-permute-start.8) | collective-permute-done | bytes 524320 | tf_op jit(solution)/shard_map/ppermute | solution.py:14
  59.7 4.7 %collective-permute-done.3 = bf16[128,2048]{1,0:T(8,128)(2,1)S(1)} collective-permute-done((bf16[128,2048]{1,0:T(8,128)(2,1)S(1)}, bf16[128,2048]{1,0:T(8,128)(2,1)S(1)}, u32[]{:S(2)}, u32[]{:S(2)}) %collective-permute-start.3) | collective-permute-done | bytes 524320 | tf_op jit(solution)/shard_map/ppermute | solution.py:14
  65.2 2.0 copy-done.13
  68.4 6.6 %pad_maximum_fusion.wgu_ref = bf16[2048,2560]{1,0:T(8,128)(2,1)} fusion(bf16[2048,640]{1,0:T(8,128)(2,1)S(1)} %get-tuple-element.63, bf16[2048,640]{1,0:T(8,128)(2,1)S(1)} %get-tuple-element.62, bf16[2048,640]{1,0:T(8,128)(2,1)S(1)} %get-tuple-element.94, bf16[2048,640]{1,0:T(8,128)(2,1)S(1)} %get-tuple-element.95), kind=kLoop, calls=%fused_computation.1 | loop fusion | flops 41943040 | bytes 20971520 | tf_op jit(solution)/shard_map/concatenate | solution.py:224
  82.1 3.3 constant_dynamic-update-slice_fusion.19.c_ref.src_ref
  85.5 1.8 constant_dynamic-update-slice_fusion.6.x_ref.src_ref
  87.3 1.9 copy-done.15
  89.2 26.0 %routes_pass.1 = (bf16[1024,1280]{1,0:T(8,128)(2,1)}, bf16[1024,2560]{1,0:T(8,128)(2,1)}, f32[1024,2]{1,0:T(8,128)}) custom-call(bf16[1024,2048]{1,0:T(8,128)(2,1)} %copy-done.15, bf16[1024,2048]{1,0:T(8,128)(2,1)} %constant_dynamic-update-slice_fusion.19.c_ref.src_ref, f32[1024,2]{1,0:T(8,128)} %copy.45.w_ref, bf16[2048,2560]{1,0:T(8,128)(2,1)} %pad_maximum_fusion.wgu_ref, ...), custom_call_target="tpu_custom_call" | custom-call | flops 16106127360 | bytes 31981568 | tf_op jit(solution)/shard_map/routes_pass/pallas_call | solution.py:95
  117.0 16.3 %convolution_convert_fusion = bf16[1024,2048]{1,0:T(8,128)(2,1)} fusion(bf16[1024,2560]{1,0:T(8,128)(2,1)} %get-tuple-element.22.rhs_ref, bf16[2048,640]{1,0:T(8,128)(2,1)} %copy-done, bf16[2048,640]{1,0:T(8,128)(2,1)S(1)} %get-tuple-element.62, bf16[2048,640]{1,0:T(8,128)(2,1)} %copy-done.1, bf16[2048,640]{1,0:T(8,128)(2,1)} %copy-done.2), kind=kOutput, calls=%fused_computation.4 | convolution fusion | flops 10781458432 | bytes 19922944 | tf_op jit(solution)/shard_map/dot_general | solution.py:243
  133.3 8.7 %convolution_convert_fusion.1 = bf16[1024,2048]{1,0:T(8,128)(2,1)S(1)} fusion(bf16[1024,1280]{1,0:T(8,128)(2,1)} %get-tuple-element.21.rhs_ref, bf16[1280,2048]{1,0:T(8,128)(2,1)} %bitcast.29), kind=kOutput, calls=%fused_computation.5 | convolution fusion | flops 5370806272 | bytes 12058624 | tf_op jit(solution)/shard_map/dot_general | solution.py:242
  142.0 11.7 %grad_pass.5 = (bf16[2,512,640]{2,1,0:T(8,128)(2,1)}, bf16[2,512,640]{2,1,0:T(8,128)(2,1)}, bf16[2,512,640]{2,1,0:T(8,128)(2,1)}, bf16[2,512,640]{2,1,0:T(8,128)(2,1)}) custom-call(s32[4]{0:T(128)} %gather_fusion, s32[4,4]{1,0:T(4,128)} %constant.27.clone.slot_ref, s32[4,4]{1,0:T(4,128)} %constant.28.clone.write_ref, ...), custom_call_target="tpu_custom_call" | custom-call | flops 5368709120 | bytes 12058624 | tf_op jit(solution)/shard_map/grad_pass/pallas_call | solution.py:173
  154.9 11.5 %grad_pass.4 = (bf16[2,512,640]{2,1,0:T(8,128)(2,1)}, bf16[2,512,640]{2,1,0:T(8,128)(2,1)}, bf16[2,512,640]{2,1,0:T(8,128)(2,1)}, bf16[2,512,640]{2,1,0:T(8,128)(2,1)}) custom-call(s32[4]{0:T(128)} %gather_fusion, s32[4,4]{1,0:T(4,128)} %constant.27.clone.slot_ref, s32[4,4]{1,0:T(4,128)} %constant.28.clone.write_ref, bf16[1024,2048]{1,0:T(8,128)(2,1)} %copy-done.15, ...), custom_call_target="tpu_custom_call" | custom-call | flops 5368709120 | bytes 12058624 | tf_op jit(solution)/shard_map/grad_pass/pallas_call | solution.py:173
  167.4 2.5 collective-permute-start.40
  171.4 11.5 %grad_pass.3 = (bf16[2,512,640]{2,1,0:T(8,128)(2,1)}, bf16[2,512,640]{2,1,0:T(8,128)(2,1)}, bf16[2,512,640]{2,1,0:T(8,128)(2,1)}, bf16[2,512,640]{2,1,0:T(8,128)(2,1)}) custom-call(s32[4]{0:T(128)} %gather_fusion, s32[4,4]{1,0:T(4,128)} %constant.27.clone.slot_ref, s32[4,4]{1,0:T(4,128)} %constant.28.clone.write_ref, bf16[1024,2048]{1,0:T(8,128)(2,1)} %copy-done.15, ...), custom_call_target="tpu_custom_call" | custom-call | flops 5368709120 | bytes 12058624 | tf_op jit(solution)/shard_map/grad_pass/pallas_call | solution.py:173
  184.5 1.8 slice.241
  187.3 3.0 collective-permute-done.27
  191.9 2.1 collective-permute-done.29
  195.6 3.7 collective-permute-done.38
  199.3 30.0 %collective-permute-start.32 = (bf16[2,512,640]{2,1,0:T(8,128)(2,1)S(1)}, bf16[2,512,640]{2,1,0:T(8,128)(2,1)S(1)}, u32[]{:S(2)}, u32[]{:S(2)}) collective-permute-start(bf16[2,512,640]{2,1,0:T(8,128)(2,1)S(1)} %copy-done.19), channel_id=1, source_target_pairs={{0,24},{8,16},{16,8},{24,0},{1,25},{9,17},{17,9},{25,1},{2,26},{10... | collective-permute-start | bytes 3932168 | tf_op jit(solution)/shard_map/ppermute | solution.py:14
  231.0 24.4 %collective-permute-done.34 = bf16[2,512,640]{2,1,0:T(8,128)(2,1)S(1)} collective-permute-done((bf16[2,512,640]{2,1,0:T(8,128)(2,1)}, bf16[2,512,640]{2,1,0:T(8,128)(2,1)S(1)}, u32[]{:S(2)}, u32[]{:S(2)}) %collective-permute-start.34) | collective-permute-done | bytes 1310752 | tf_op jit(solution)/shard_map/ppermute | solution.py:14
  255.8 28.2 %collective-permute-done.36 = bf16[2,512,640]{2,1,0:T(8,128)(2,1)S(1)} collective-permute-done((bf16[2,512,640]{2,1,0:T(8,128)(2,1)S(1)}, bf16[2,512,640]{2,1,0:T(8,128)(2,1)S(1)}, u32[]{:S(2)}, u32[]{:S(2)}) %collective-permute-start.36) | collective-permute-done | bytes 1310752 | tf_op jit(solution)/shard_map/ppermute | solution.py:14
  284.0 1.9 collective-permute-start.39
  286.4 23.1 %collective-permute-done.30 = bf16[2,512,640]{2,1,0:T(8,128)(2,1)S(1)} collective-permute-done((bf16[2,512,640]{2,1,0:T(8,128)(2,1)S(1)}, bf16[2,512,640]{2,1,0:T(8,128)(2,1)S(1)}, u32[]{:S(2)}, u32[]{:S(2)}) %collective-permute-start.30) | collective-permute-done | bytes 1310752 | tf_op jit(solution)/shard_map/ppermute | solution.py:14
  309.5 2.2 collective-permute-start.41
  312.1 28.3 %collective-permute-done.32 = bf16[2,512,640]{2,1,0:T(8,128)(2,1)S(1)} collective-permute-done((bf16[2,512,640]{2,1,0:T(8,128)(2,1)S(1)}, bf16[2,512,640]{2,1,0:T(8,128)(2,1)S(1)}, u32[]{:S(2)}, u32[]{:S(2)}) %collective-permute-start.32) | collective-permute-done | bytes 1310752 | tf_op jit(solution)/shard_map/ppermute | solution.py:14
  342.3 12.0 %collective-permute-done.39 = bf16[1,512,640]{2,1,0:T(8,128)(2,1)S(1)} collective-permute-done((bf16[1,512,640]{2,1,0:T(8,128)(2,1)S(1)}, bf16[1,512,640]{2,1,0:T(8,128)(2,1)S(1)}, u32[]{:S(2)}, u32[]{:S(2)}) %collective-permute-start.39) | collective-permute-done | bytes 655392 | tf_op jit(solution)/shard_map/ppermute | solution.py:14
  354.3 28.6 %collective-permute-start.37 = (bf16[1,512,640]{2,1,0:T(8,128)(2,1)S(1)}, bf16[1,512,640]{2,1,0:T(8,128)(2,1)S(1)}, u32[]{:S(2)}, u32[]{:S(2)}) collective-permute-start(bf16[1,512,640]{2,1,0:T(8,128)(2,1)S(1)} %slice.267), channel_id=1, source_target_pairs={{0,8},{8,0},{16,24},{24,16},{1,9},{9,1},{17,25},{25,17},{2,10},{10... | collective-permute-start | bytes 1966088 | tf_op jit(solution)/shard_map/ppermute | solution.py:14
  383.1 3.1 collective-permute-start.31
  386.3 20.8 %collective-permute-start.33 = (bf16[1,512,640]{2,1,0:T(8,128)(2,1)S(1)}, bf16[1,512,640]{2,1,0:T(8,128)(2,1)S(1)}, u32[]{:S(2)}, u32[]{:S(2)}) collective-permute-start(bf16[1,512,640]{2,1,0:T(8,128)(2,1)S(1)} %slice.263), channel_id=1, source_target_pairs={{0,8},{8,0},{16,24},{24,16},{1,9},{9,1},{17,25},{25,17},{2,10},{10... | collective-permute-start | bytes 1966088 | tf_op jit(solution)/shard_map/ppermute | solution.py:14
  407.8 7.8 %collective-permute-done.31 = bf16[1,512,640]{2,1,0:T(8,128)(2,1)S(1)} collective-permute-done((bf16[1,512,640]{2,1,0:T(8,128)(2,1)S(1)}, bf16[1,512,640]{2,1,0:T(8,128)(2,1)S(1)}, u32[]{:S(2)}, u32[]{:S(2)}) %collective-permute-start.31) | collective-permute-done | bytes 655392 | tf_op jit(solution)/shard_map/ppermute | solution.py:14
  415.8 7.1 %collective-permute-done.33 = bf16[1,512,640]{2,1,0:T(8,128)(2,1)S(1)} collective-permute-done((bf16[1,512,640]{2,1,0:T(8,128)(2,1)S(1)}, bf16[1,512,640]{2,1,0:T(8,128)(2,1)S(1)}, u32[]{:S(2)}, u32[]{:S(2)}) %collective-permute-start.33) | collective-permute-done | bytes 655392 | tf_op jit(solution)/shard_map/ppermute | solution.py:14
  429.4 3.5 copy.44
  432.9 3.5 copy.43
  436.4 3.7 copy.42
  443.7 6.6 %collective-permute-done.16 = bf16[128,2048]{1,0:T(8,128)(2,1)S(1)} collective-permute-done((bf16[128,2048]{1,0:T(8,128)(2,1)S(1)}, bf16[128,2048]{1,0:T(8,128)(2,1)S(1)}, u32[]{:S(2)}, u32[]{:S(2)}) %collective-permute-start.16) | collective-permute-done | bytes 524320 | tf_op jit(solution)/shard_map/ppermute | solution.py:14
  455.8 2.9 collective-permute-done.17
  (187 shorter events, 59.4 us)
Async XLA Ops:
  2.3 26.0 %copy-start.4 = (bf16[128,2048]{1,0:T(8,128)(2,1)S(1)}, bf16[128,2048]{1,0:T(8,128)(2,1)}, u32[]{:S(2)}) copy-start(bf16[128,2048]{1,0:T(8,128)(2,1)} %param.19) | copy-start | bytes 1572868
  2.3 10.1 %collective-permute-start.5 = (bf16[64,2048]{1,0:T(8,128)(2,1)S(1)}, bf16[64,2048]{1,0:T(8,128)(2,1)S(1)}, u32[]{:S(2)}, u32[]{:S(2)}) collective-permute-start(bf16[64,2048]{1,0:T(8,128)(2,1)S(1)} %get-tuple-element.78), channel_id=1, source_target_pairs={{0,2},{1,3},{2,0},{3,1},{4,6},{5,7},{6,4},{7,5},{8,10},{9,11},{10,... | collective-permute-start | bytes 786440 | tf_op jit(solution)/shard_map/ppermute | solution.py:14
  7.0 10.3 %collective-permute-start = (bf16[64,2048]{1,0:T(8,128)(2,1)S(1)}, bf16[64,2048]{1,0:T(8,128)(2,1)S(1)}, u32[]{:S(2)}, u32[]{:S(2)}) collective-permute-start(bf16[64,2048]{1,0:T(8,128)(2,1)S(1)} %get-tuple-element.85), channel_id=1, source_target_pairs={{0,2},{1,3},{2,0},{3,1},{4,6},{5,7},{6,4},{7,5},{8,10},{9,11},{10,... | collective-permute-start | bytes 786440 | tf_op jit(solution)/shard_map/ppermute | solution.py:14
  7.8 67.1 %collective-permute-start.10 = (f32[64,16]{0,1:T(8,128)S(1)}, f32[64,16]{0,1:T(8,128)S(1)}, u32[]{:S(2)}, u32[]{:S(2)}) collective-permute-start(f32[64,16]{0,1:T(8,128)S(1)} %get-tuple-element.93), channel_id=1, source_target_pairs={{0,2},{1,3},{2,0},{3,1},{4,6},{5,7},{6,4},{7,5},{8,10},{9,11},{10,... | collective-permute-start | bytes 12296 | tf_op jit(solution)/shard_map/ppermute | solution.py:14
  9.8 66.1 %collective-permute-start.12 = (f32[64,16]{0,1:T(8,128)S(1)}, f32[64,16]{0,1:T(8,128)S(1)}, u32[]{:S(2)}, u32[]{:S(2)}) collective-permute-start(f32[64,16]{0,1:T(8,128)S(1)} %get-tuple-element.92), channel_id=1, source_target_pairs={{0,4},{1,5},{2,6},{3,7},{4,0},{5,1},{6,2},{7,3},{8,12},{9,13},{10,... | collective-permute-start | bytes 12296 | tf_op jit(solution)/shard_map/ppermute | solution.py:14
  12.5 15.0 %collective-permute-start.6 = (bf16[128,2048]{1,0:T(8,128)(2,1)S(1)}, bf16[128,2048]{1,0:T(8,128)(2,1)S(1)}, u32[]{:S(2)}, u32[]{:S(2)}) collective-permute-start(bf16[128,2048]{1,0:T(8,128)(2,1)S(1)} %pad_maximum_fusion.6), channel_id=1, source_target_pairs={{0,4},{1,5},{2,6},{3,7},{4,0},{5,1},{6,2},{7,3},{8,12},{9,13},{10,... | collective-permute-start | bytes 1572872 | tf_op jit(solution)/shard_map/ppermute | solution.py:14
  17.3 50.0 %slice-start.2 = ((s8[5242880]{0:T(1024)(128)(4,1)}), s8[4194304]{0:T(1024)(128)(4,1)S(1)}, s32[]{:S(2)}) async-start(s8[5242880]{0:T(1024)(128)(4,1)} %bitcast.26), calls=%async_computation.2 | async-start | bytes 8388608
  17.3 21.3 %collective-permute-start.1 = (bf16[128,2048]{1,0:T(8,128)(2,1)S(1)}, bf16[128,2048]{1,0:T(8,128)(2,1)S(1)}, u32[]{:S(2)}, u32[]{:S(2)}) collective-permute-start(bf16[128,2048]{1,0:T(8,128)(2,1)S(1)} %pad_maximum_fusion.4), channel_id=1, source_target_pairs={{0,4},{1,5},{2,6},{3,7},{4,0},{5,1},{6,2},{7,3},{8,12},{9,13},{10,... | collective-permute-start | bytes 1572872 | tf_op jit(solution)/shard_map/ppermute | solution.py:14
  27.5 39.8 %slice-start = ((s8[5242880]{0:T(1024)(128)(4,1)}), s8[4194304]{0:T(1024)(128)(4,1)S(1)}, s32[]{:S(2)}) async-start(s8[5242880]{0:T(1024)(128)(4,1)} %bitcast.24), calls=%async_computation | async-start | bytes 8388608
  29.1 15.2 %collective-permute-start.7 = (bf16[64,2048]{1,0:T(8,128)(2,1)S(1)}, bf16[64,2048]{1,0:T(8,128)(2,1)S(1)}, u32[]{:S(2)}, u32[]{:S(2)}) collective-permute-start(bf16[64,2048]{1,0:T(8,128)(2,1)S(1)} %get-tuple-element.76), channel_id=1, source_target_pairs={{0,4},{1,5},{2,6},{3,7},{4,0},{5,1},{6,2},{7,3},{8,12},{9,13},{10,... | collective-permute-start | bytes 786440 | tf_op jit(solution)/shard_map/ppermute | solution.py:14
  40.3 7.0 %collective-permute-start.2 = (bf16[64,2048]{1,0:T(8,128)(2,1)S(1)}, bf16[64,2048]{1,0:T(8,128)(2,1)S(1)}, u32[]{:S(2)}, u32[]{:S(2)}) collective-permute-start(bf16[64,2048]{1,0:T(8,128)(2,1)S(1)} %get-tuple-element.83), channel_id=1, source_target_pairs={{0,4},{1,5},{2,6},{3,7},{4,0},{5,1},{6,2},{7,3},{8,12},{9,13},{10,... | collective-permute-start | bytes 786440 | tf_op jit(solution)/shard_map/ppermute | solution.py:14
  44.4 14.3 %collective-permute-start.8 = (bf16[128,2048]{1,0:T(8,128)(2,1)S(1)}, bf16[128,2048]{1,0:T(8,128)(2,1)S(1)}, u32[]{:S(2)}, u32[]{:S(2)}) collective-permute-start(bf16[128,2048]{1,0:T(8,128)(2,1)S(1)} %pad_maximum_fusion.7), channel_id=1, source_target_pairs={{0,2},{1,3},{2,0},{3,1},{4,6},{5,7},{6,4},{7,5},{8,10},{9,11},{10,... | collective-permute-start | bytes 1572872 | tf_op jit(solution)/shard_map/ppermute | solution.py:14
  47.3 17.0 %collective-permute-start.3 = (bf16[128,2048]{1,0:T(8,128)(2,1)S(1)}, bf16[128,2048]{1,0:T(8,128)(2,1)S(1)}, u32[]{:S(2)}, u32[]{:S(2)}) collective-permute-start(bf16[128,2048]{1,0:T(8,128)(2,1)S(1)} %pad_maximum_fusion.5), channel_id=1, source_target_pairs={{0,2},{1,3},{2,0},{3,1},{4,6},{5,7},{6,4},{7,5},{8,10},{9,11},{10,... | collective-permute-start | bytes 1572872 | tf_op jit(solution)/shard_map/ppermute | solution.py:14
  59.7 22.5 %collective-permute-start.9 = (bf16[512,2048]{1,0:T(8,128)(2,1)}, bf16[512,2048]{1,0:T(8,128)(2,1)}, u32[]{:S(2)}, u32[]{:S(2)}) collective-permute-start(bf16[512,2048]{1,0:T(8,128)(2,1)} %get-tuple-element.72), channel_id=1, source_target_pairs={{0,1},{1,0},{2,3},{3,2},{4,5},{5,4},{6,7},{7,6},{8,9},{9,8},{10,11... | collective-permute-start | bytes 6291464 | tf_op jit(solution)/shard_map/ppermute | solution.py:14
  67.3 18.2 %collective-permute-start.4 = (bf16[512,2048]{1,0:T(8,128)(2,1)}, bf16[512,2048]{1,0:T(8,128)(2,1)}, u32[]{:S(2)}, u32[]{:S(2)}) collective-permute-start(bf16[512,2048]{1,0:T(8,128)(2,1)} %get-tuple-element.79), channel_id=1, source_target_pairs={{0,1},{1,0},{2,3},{3,2},{4,5},{5,4},{6,7},{7,6},{8,9},{9,8},{10,11... | collective-permute-start | bytes 6291464 | tf_op jit(solution)/shard_map/ppermute | solution.py:14
  75.1 3.7 collective-permute-start.11
  76.0 3.7 collective-permute-start.13
  79.8 1.2 collective-permute-start.14
  116.5 37.2 %collective-permute-start.25 = (f32[512,16]{0,1:T(8,128)S(1)}, f32[512,16]{0,1:T(8,128)S(1)}, u32[]{:S(2)}, u32[]{:S(2)}) collective-permute-start(f32[512,16]{0,1:T(8,128)S(1)} %slice.251), channel_id=1, source_target_pairs={{0,1},{1,0},{2,3},{3,2},{4,5},{5,4},{6,7},{7,6},{8,9},{9,8},{10,11... | collective-permute-start | bytes 98312 | tf_op jit(solution)/shard_map/ppermute | solution.py:14
  153.7 16.1 %collective-permute-start.26 = (f32[128,16]{0,1:T(8,128)S(1)}, f32[128,16]{0,1:T(8,128)S(1)}, u32[]{:S(2)}, u32[]{:S(2)}) collective-permute-start(f32[128,16]{0,1:T(8,128)S(1)} %slice.253), channel_id=1, source_target_pairs={{0,4},{1,5},{2,6},{3,7},{4,0},{5,1},{6,2},{7,3},{8,12},{9,13},{10,... | collective-permute-start | bytes 24584 | tf_op jit(solution)/shard_map/ppermute | solution.py:14
  166.4 32.9 %collective-permute-start.38 = (bf16[2,512,640]{2,1,0:T(8,128)(2,1)}, bf16[2,512,640]{2,1,0:T(8,128)(2,1)S(1)}, u32[]{:S(2)}, u32[]{:S(2)}) collective-permute-start(bf16[2,512,640]{2,1,0:T(8,128)(2,1)} %get-tuple-element.33), channel_id=1, source_target_pairs={{0,8},{8,0},{16,24},{24,16},{1,9},{9,1},{17,25},{25,17},{2,10},{10... | collective-permute-start | bytes 3932168 | tf_op jit(solution)/shard_map/ppermute | solution.py:14
  167.4 62.4 %collective-permute-start.40 = (bf16[2,512,640]{2,1,0:T(8,128)(2,1)}, bf16[2,512,640]{2,1,0:T(8,128)(2,1)S(1)}, u32[]{:S(2)}, u32[]{:S(2)}) collective-permute-start(bf16[2,512,640]{2,1,0:T(8,128)(2,1)} %get-tuple-element.35), channel_id=1, source_target_pairs={{0,24},{8,16},{16,8},{24,0},{1,25},{9,17},{17,9},{25,1},{2,26},{10... | collective-permute-start | bytes 3932168 | tf_op jit(solution)/shard_map/ppermute | solution.py:14
  169.8 16.8 %collective-permute-start.28 = (f32[128,16]{0,1:T(8,128)S(1)}, f32[128,16]{0,1:T(8,128)S(1)}, u32[]{:S(2)}, u32[]{:S(2)}) collective-permute-start(f32[128,16]{0,1:T(8,128)S(1)} %get-tuple-element.91), channel_id=1, source_target_pairs={{0,2},{1,3},{2,0},{3,1},{4,6},{5,7},{6,4},{7,5},{8,10},{9,11},{10,... | collective-permute-start | bytes 24584 | tf_op jit(solution)/shard_map/ppermute | solution.py:14
  182.9 72.6 %collective-permute-start.34 = (bf16[2,512,640]{2,1,0:T(8,128)(2,1)}, bf16[2,512,640]{2,1,0:T(8,128)(2,1)S(1)}, u32[]{:S(2)}, u32[]{:S(2)}) collective-permute-start(bf16[2,512,640]{2,1,0:T(8,128)(2,1)} %get-tuple-element.29), channel_id=1, source_target_pairs={{0,8},{8,0},{16,24},{24,16},{1,9},{9,1},{17,25},{25,17},{2,10},{10... | collective-permute-start | bytes 3932168 | tf_op jit(solution)/shard_map/ppermute | solution.py:14
  183.6 100.5 %collective-permute-start.36 = (bf16[2,512,640]{2,1,0:T(8,128)(2,1)S(1)}, bf16[2,512,640]{2,1,0:T(8,128)(2,1)S(1)}, u32[]{:S(2)}, u32[]{:S(2)}) collective-permute-start(bf16[2,512,640]{2,1,0:T(8,128)(2,1)S(1)} %copy-done.18), channel_id=1, source_target_pairs={{0,24},{8,16},{16,8},{24,0},{1,25},{9,17},{17,9},{25,1},{2,26},{10... | collective-permute-start | bytes 3932168 | tf_op jit(solution)/shard_map/ppermute | solution.py:14
  186.3 43.0 %copy-start.11 = (bf16[2,512,640]{2,1,0:T(8,128)(2,1)S(1)}, bf16[2,512,640]{2,1,0:T(8,128)(2,1)}, u32[]{:S(2)}) copy-start(bf16[2,512,640]{2,1,0:T(8,128)(2,1)} %get-tuple-element.32) | copy-start | bytes 3932164
  186.7 3.7 collective-permute-start.27
  190.3 3.7 collective-permute-start.29
  194.0 115.5 %collective-permute-start.30 = (bf16[2,512,640]{2,1,0:T(8,128)(2,1)S(1)}, bf16[2,512,640]{2,1,0:T(8,128)(2,1)S(1)}, u32[]{:S(2)}, u32[]{:S(2)}) collective-permute-start(bf16[2,512,640]{2,1,0:T(8,128)(2,1)S(1)} %copy-done.20), channel_id=1, source_target_pairs={{0,8},{8,0},{16,24},{24,16},{1,9},{9,1},{17,25},{25,17},{2,10},{10... | collective-permute-start | bytes 3932168 | tf_op jit(solution)/shard_map/ppermute | solution.py:14
  199.3 141.0 %collective-permute-start.32 = (bf16[2,512,640]{2,1,0:T(8,128)(2,1)S(1)}, bf16[2,512,640]{2,1,0:T(8,128)(2,1)S(1)}, u32[]{:S(2)}, u32[]{:S(2)}) collective-permute-start(bf16[2,512,640]{2,1,0:T(8,128)(2,1)S(1)} %copy-done.19), channel_id=1, source_target_pairs={{0,24},{8,16},{16,8},{24,0},{1,25},{9,17},{17,9},{25,1},{2,26},{10... | collective-permute-start | bytes 3932168 | tf_op jit(solution)/shard_map/ppermute | solution.py:14
  229.8 193.3 %collective-permute-start.20 = (bf16[512,2048]{1,0:T(8,128)(2,1)S(1)}, bf16[512,2048]{1,0:T(8,128)(2,1)S(1)}, u32[]{:S(2)}, u32[]{:S(2)}) collective-permute-start(bf16[512,2048]{1,0:T(8,128)(2,1)S(1)} %slice.241), channel_id=1, source_target_pairs={{0,1},{1,0},{2,3},{3,2},{4,5},{5,4},{6,7},{7,6},{8,9},{9,8},{10,11... | collective-permute-start | bytes 6291464 | tf_op jit(solution)/shard_map/ppermute | solution.py:14
  231.0 54.9 %copy-start.6 = (bf16[2,512,640]{2,1,0:T(8,128)(2,1)S(1)}, bf16[2,512,640]{2,1,0:T(8,128)(2,1)}, u32[]{:S(2)}) copy-start(bf16[2,512,640]{2,1,0:T(8,128)(2,1)} %get-tuple-element.30) | copy-start | bytes 3932164
  255.5 171.7 %collective-permute-start.15 = (bf16[512,2048]{1,0:T(8,128)(2,1)S(1)}, bf16[512,2048]{1,0:T(8,128)(2,1)S(1)}, u32[]{:S(2)}, u32[]{:S(2)}) collective-permute-start(bf16[512,2048]{1,0:T(8,128)(2,1)S(1)} %slice.231), channel_id=1, source_target_pairs={{0,1},{1,0},{2,3},{3,2},{4,5},{5,4},{6,7},{7,6},{8,9},{9,8},{10,11... | collective-permute-start | bytes 6291464 | tf_op jit(solution)/shard_map/ppermute | solution.py:14
  284.0 70.3 %collective-permute-start.39 = (bf16[1,512,640]{2,1,0:T(8,128)(2,1)S(1)}, bf16[1,512,640]{2,1,0:T(8,128)(2,1)S(1)}, u32[]{:S(2)}, u32[]{:S(2)}) collective-permute-start(bf16[1,512,640]{2,1,0:T(8,128)(2,1)S(1)} %slice.269), channel_id=1, source_target_pairs={{0,24},{8,16},{16,8},{24,0},{1,25},{9,17},{17,9},{25,1},{2,26},{10... | collective-permute-start | bytes 1966088 | tf_op jit(solution)/shard_map/ppermute | solution.py:14
  309.5 73.6 %collective-permute-start.41 = (bf16[1,512,640]{2,1,0:T(8,128)(2,1)S(1)}, bf16[1,512,640]{2,1,0:T(8,128)(2,1)S(1)}, u32[]{:S(2)}, u32[]{:S(2)}) collective-permute-start(bf16[1,512,640]{2,1,0:T(8,128)(2,1)S(1)} %slice.271), channel_id=1, source_target_pairs={{0,8},{8,0},{16,24},{24,16},{1,9},{9,1},{17,25},{25,17},{2,10},{10... | collective-permute-start | bytes 1966088 | tf_op jit(solution)/shard_map/ppermute | solution.py:14
  311.7 30.0 %copy-start.7 = (bf16[2,512,640]{2,1,0:T(8,128)(2,1)S(1)}, bf16[2,512,640]{2,1,0:T(8,128)(2,1)}, u32[]{:S(2)}) copy-start(bf16[2,512,640]{2,1,0:T(8,128)(2,1)} %get-tuple-element.26) | copy-start | bytes 3932164
  340.4 46.0 %collective-permute-start.35 = (bf16[1,512,640]{2,1,0:T(8,128)(2,1)S(1)}, bf16[1,512,640]{2,1,0:T(8,128)(2,1)S(1)}, u32[]{:S(2)}, u32[]{:S(2)}) collective-permute-start(bf16[1,512,640]{2,1,0:T(8,128)(2,1)S(1)} %slice.265), channel_id=1, source_target_pairs={{0,24},{8,16},{16,8},{24,0},{1,25},{9,17},{17,9},{25,1},{2,26},{10... | collective-permute-start | bytes 1966088 | tf_op jit(solution)/shard_map/ppermute | solution.py:14
  354.3 53.0 %collective-permute-start.37 = (bf16[1,512,640]{2,1,0:T(8,128)(2,1)S(1)}, bf16[1,512,640]{2,1,0:T(8,128)(2,1)S(1)}, u32[]{:S(2)}, u32[]{:S(2)}) collective-permute-start(bf16[1,512,640]{2,1,0:T(8,128)(2,1)S(1)} %slice.267), channel_id=1, source_target_pairs={{0,8},{8,0},{16,24},{24,16},{1,9},{9,1},{17,25},{25,17},{2,10},{10... | collective-permute-start | bytes 1966088 | tf_op jit(solution)/shard_map/ppermute | solution.py:14
  383.1 32.6 %collective-permute-start.31 = (bf16[1,512,640]{2,1,0:T(8,128)(2,1)S(1)}, bf16[1,512,640]{2,1,0:T(8,128)(2,1)S(1)}, u32[]{:S(2)}, u32[]{:S(2)}) collective-permute-start(bf16[1,512,640]{2,1,0:T(8,128)(2,1)S(1)} %slice.261), channel_id=1, source_target_pairs={{0,24},{8,16},{16,8},{24,0},{1,25},{9,17},{17,9},{25,1},{2,26},{10... | collective-permute-start | bytes 1966088 | tf_op jit(solution)/shard_map/ppermute | solution.py:14
  386.3 36.5 %collective-permute-start.33 = (bf16[1,512,640]{2,1,0:T(8,128)(2,1)S(1)}, bf16[1,512,640]{2,1,0:T(8,128)(2,1)S(1)}, u32[]{:S(2)}, u32[]{:S(2)}) collective-permute-start(bf16[1,512,640]{2,1,0:T(8,128)(2,1)S(1)} %slice.263), channel_id=1, source_target_pairs={{0,8},{8,0},{16,24},{24,16},{1,9},{9,1},{17,25},{25,17},{2,10},{10... | collective-permute-start | bytes 1966088 | tf_op jit(solution)/shard_map/ppermute | solution.py:14
  424.1 16.0 %collective-permute-start.21 = (bf16[128,2048]{1,0:T(8,128)(2,1)S(1)}, bf16[128,2048]{1,0:T(8,128)(2,1)S(1)}, u32[]{:S(2)}, u32[]{:S(2)}) collective-permute-start(bf16[128,2048]{1,0:T(8,128)(2,1)S(1)} %get-tuple-element.66), channel_id=1, source_target_pairs={{0,4},{1,5},{2,6},{3,7},{4,0},{5,1},{6,2},{7,3},{8,12},{9,13},{10,... | collective-permute-start | bytes 1572872 | tf_op jit(solution)/shard_map/ppermute | solution.py:14
  425.7 14.9 %collective-permute-start.23 = (bf16[128,2048]{1,0:T(8,128)(2,1)S(1)}, bf16[128,2048]{1,0:T(8,128)(2,1)S(1)}, u32[]{:S(2)}, u32[]{:S(2)}) collective-permute-start(bf16[128,2048]{1,0:T(8,128)(2,1)S(1)} %get-tuple-element.67), channel_id=1, source_target_pairs={{0,2},{1,3},{2,0},{3,1},{4,6},{5,7},{6,4},{7,5},{8,10},{9,11},{10,... | collective-permute-start | bytes 1572872 | tf_op jit(solution)/shard_map/ppermute | solution.py:14
  428.1 22.2 %collective-permute-start.16 = (bf16[128,2048]{1,0:T(8,128)(2,1)S(1)}, bf16[128,2048]{1,0:T(8,128)(2,1)S(1)}, u32[]{:S(2)}, u32[]{:S(2)}) collective-permute-start(bf16[128,2048]{1,0:T(8,128)(2,1)S(1)} %get-tuple-element.70), channel_id=1, source_target_pairs={{0,4},{1,5},{2,6},{3,7},{4,0},{5,1},{6,2},{7,3},{8,12},{9,13},{10,... | collective-permute-start | bytes 1572872 | tf_op jit(solution)/shard_map/ppermute | solution.py:14
  428.6 23.1 %collective-permute-start.18 = (bf16[128,2048]{1,0:T(8,128)(2,1)S(1)}, bf16[128,2048]{1,0:T(8,128)(2,1)S(1)}, u32[]{:S(2)}, u32[]{:S(2)}) collective-permute-start(bf16[128,2048]{1,0:T(8,128)(2,1)S(1)} %get-tuple-element.71), channel_id=1, source_target_pairs={{0,2},{1,3},{2,0},{3,1},{4,6},{5,7},{6,4},{7,5},{8,10},{9,11},{10,... | collective-permute-start | bytes 1572872 | tf_op jit(solution)/shard_map/ppermute | solution.py:14
  441.0 14.7 %collective-permute-start.22 = (bf16[64,2048]{1,0:T(8,128)(2,1)S(1)}, bf16[64,2048]{1,0:T(8,128)(2,1)S(1)}, u32[]{:S(2)}, u32[]{:S(2)}) collective-permute-start(bf16[64,2048]{1,0:T(8,128)(2,1)S(1)} %slice.245), channel_id=1, source_target_pairs={{0,2},{1,3},{2,0},{3,1},{4,6},{5,7},{6,4},{7,5},{8,10},{9,11},{10,... | collective-permute-start | bytes 786440 | tf_op jit(solution)/shard_map/ppermute | solution.py:14
  442.5 13.2 %collective-permute-start.24 = (bf16[64,2048]{1,0:T(8,128)(2,1)S(1)}, bf16[64,2048]{1,0:T(8,128)(2,1)S(1)}, u32[]{:S(2)}, u32[]{:S(2)}) collective-permute-start(bf16[64,2048]{1,0:T(8,128)(2,1)S(1)} %slice.249), channel_id=1, source_target_pairs={{0,4},{1,5},{2,6},{3,7},{4,0},{5,1},{6,2},{7,3},{8,12},{9,13},{10,... | collective-permute-start | bytes 786440 | tf_op jit(solution)/shard_map/ppermute | solution.py:14
  452.2 6.4 %collective-permute-start.17 = (bf16[64,2048]{1,0:T(8,128)(2,1)S(1)}, bf16[64,2048]{1,0:T(8,128)(2,1)S(1)}, u32[]{:S(2)}, u32[]{:S(2)}) collective-permute-start(bf16[64,2048]{1,0:T(8,128)(2,1)S(1)} %slice.235), channel_id=1, source_target_pairs={{0,2},{1,3},{2,0},{3,1},{4,6},{5,7},{6,4},{7,5},{8,10},{9,11},{10,... | collective-permute-start | bytes 786440 | tf_op jit(solution)/shard_map/ppermute | solution.py:14
  453.8 6.4 %collective-permute-start.19 = (bf16[64,2048]{1,0:T(8,128)(2,1)S(1)}, bf16[64,2048]{1,0:T(8,128)(2,1)S(1)}, u32[]{:S(2)}, u32[]{:S(2)}) collective-permute-start(bf16[64,2048]{1,0:T(8,128)(2,1)S(1)} %slice.239), channel_id=1, source_target_pairs={{0,4},{1,5},{2,6},{3,7},{4,0},{5,1},{6,2},{7,3},{8,12},{9,13},{10,... | collective-permute-start | bytes 786440 | tf_op jit(solution)/shard_map/ppermute | solution.py:14
  (19 other events, 221.8 us)

commit v2 on v0

--- a/solution.py
+++ b/solution.py
@@ -1,7 +1,404 @@
+import functools
+
 import jax
 import jax.numpy as jnp
 from jax import lax
+from jax.experimental import pallas as pl
+from jax.experimental.pallas import tpu as pltpu
 from jax.sharding import PartitionSpec as P
+
+MIB = 1024 * 1024
+DECLARED = 1 << 20
+ROUTES_BYTES, OUT_BYTES, GRAD_BYTES, SUM_BYTES = 56 * MIB, 56 * MIB, 56 * MIB, 8 * MIB
+
+
+def swap(value, axis, mask):
+    return lax.ppermute(value, axis, [(i, i ^ mask) for i in range(lax.axis_size(axis))])
+
+
+def together(values):
+    return list(lax.optimization_barrier(tuple(values)))
+
+
+def way_bits(axis):
+    bits = [1 << b for b in range(1, lax.axis_size(axis).bit_length() - 1)]
+    return list(zip(bits, bits[::-1]))
+
+
+def join(parts):
+    return parts[0] if len(parts) == 1 else jnp.concatenate(parts, 0)
+
+
+def gather_planes(own, masks, work):
+    pieces, halves, made, tied = [], own, [], 0
+    ways = way_bits("expert")
+    for n in range(len(masks)):
+        first, second = halves
+        for s, (bit_first, bit_second) in enumerate(ways):
+            sent = [swap(first, "expert", bit_first), swap(second, "expert", bit_second)]
+            if s == len(ways) - 1 and n + 1 < len(masks):
+                sent += [swap(half, "dp", masks[n + 1]) for half in own]
+            beside = []
+            if pieces:
+                pieces[-1].append(swap(pieces[-1][0], "expert", 1))
+                made.append(work(pieces[-1], len(pieces) <= len(ways)))
+            ended = range(tied, len(made) if len(sent) > 2 else len(made) - 1)
+            for p in ended:
+                beside += made[p]
+            got = together(sent + beside)
+            rest = got[len(sent) :]
+            for p in ended:
+                made[p], rest = rest[: len(made[p])], rest[len(made[p]) :]
+                tied = p + 1
+            halves = got[2 : len(sent)]
+            whole = [join([first, got[0]]), join([second, got[1]])]
+            pieces.append([join(whole if s == 0 else got[:2])])
+            first, second = whole
+    pieces[-1].append(swap(pieces[-1][0], "expert", 1))
+    made.append(work(pieces[-1], len(pieces) <= len(ways)))
+    return pieces, made
+
+
+def add_to(kept, received):
+    return (kept.astype(jnp.float32) + received.astype(jnp.float32)).astype(kept.dtype)
+
+
+def scatter_round(sides, s, bits, beside):
+    if s == 0:
+        sides = [[p[0][: p[0].shape[0] // 2], p[0][p[0].shape[0] // 2 :]] for p in sides]
+    *beside, first, second = together(
+        beside + [swap(side[-1], "expert", bit) for side, bit in zip(sides, bits)]
+    )
+    summed = []
+    for side, value in zip(sides, (first, second)):
+        at, kept = 0, []
+        for part in side[:-1]:
+            kept.append(add_to(part, value[at : at + part.shape[0]]))
+            at += part.shape[0]
+        summed.append(kept)
+    return summed, beside
+
+
+def tile_of(cols):
+    return 256 if cols % 256 == 0 else 128
+
+
+def split_in_two(value):
+    high = value.astype(jnp.bfloat16)
+    return high, (value - high.astype(jnp.float32)).astype(jnp.bfloat16)
+
+
+def by_expert(values, lane, hid):
+    spread = values[-1]
+    for e in range(len(values) - 2, -1, -1):
+        spread = jnp.where(lane < (e + 1) * hid, values[e], spread)
+    return spread
+
+
+def routes_kernel(blocks, hid, experts, with_rwg, mine_ref, *refs):
+    xcs, (wg, wu, wd, hw, dg, du, *more) = refs[:blocks], refs[blocks:]
+    extra_ref, sums = more[0] if with_rwg else None, more[-1]
+    j, (tile, width) = pl.program_id(0), wd.shape
+    held = sums.shape[1]
+
+    @pl.when(j == 0)
+    def _():
+        sums[...] = jnp.zeros(sums.shape, jnp.float32)
+
+    mine = mine_ref[0]
+    end = 0
+    for xc in xcs:
+        rows = slice(end, end + xc.shape[0])
+        end = rows.stop
+        lane = lax.broadcasted_iota(jnp.int32, (xc.shape[0], tile), 1) + j * tile
+        tail = xc[:, 2 * width :].astype(jnp.float32)
+        spot = lax.broadcasted_iota(jnp.int32, tail.shape, 1)
+        spots = [(spot == mine + e, spot == experts + mine + e) for e in range(held)]
+        weights = [
+            jnp.sum(jnp.where(high | low, tail, 0.0), axis=1, keepdims=True) for high, low in spots
+        ]
+        gate = jnp.dot(xc[:, :width], wg[...], preferred_element_type=jnp.float32)
+        up = jnp.dot(xc[:, :width], wu[...], preferred_element_type=jnp.float32)
+        d_plain = lax.dot_general(
+            xc[:, width : 2 * width],
+            wd[...],
+            (((1,), (1,)), ((), ())),
+            preferred_element_type=jnp.float32,
+        )
+        weight = by_expert(weights, lane, hid)
+        sig = jax.nn.sigmoid(gate)
+        swish = gate * sig
+        hidden = swish * up
+        d_hidden = d_plain * weight
+        hw[rows, :] = (hidden * weight).astype(jnp.bfloat16)
+        dg[rows, :] = (d_hidden * up * (sig * (1.0 + gate * (1.0 - sig)))).astype(jnp.bfloat16)
+        du[rows, :] = (d_hidden * swish).astype(jnp.bfloat16)
+        if not with_rwg:
+            continue
+        product = hidden * d_plain
+        for e in range(held):
+            inside = (lane >= e * hid) & (lane < (e + 1) * hid)
+            sums[rows, e : e + 1] += jnp.sum(
+                jnp.where(inside, product, 0.0), axis=1, keepdims=True
+            )
+
+    if with_rwg:
+
+        @pl.when(j == pl.num_programs(0) - 1)
+        def _():
+            spot = lax.broadcasted_iota(jnp.int32, extra_ref.shape, 1)
+            placed = jnp.zeros(extra_ref.shape, jnp.float32)
+            for e in range(held):
+                top, rest = split_in_two(sums[:, e : e + 1])
+                placed = jnp.where(spot == mine + e, top.astype(jnp.float32), placed)
+                placed = jnp.where(spot == experts + mine + e, rest.astype(jnp.float32), placed)
+            extra_ref[...] = placed.astype(jnp.bfloat16)
+
+
+def routes_pass(blocks, mine, wgu, wd, hid, experts, with_rwg):
+    rows, wide = sum(block.shape[0] for block in blocks), blocks[0].shape[1]
+    cols, width = wd.shape
+    tile, once = tile_of(cols), pl.Buffered(1)
+    steps = cols // tile
+    extra = wide - 2 * width
+    return pl.pallas_call(
+        functools.partial(routes_kernel, len(blocks), hid, experts, with_rwg),
+        grid=(steps,),
+        in_specs=[pl.BlockSpec(memory_space=pltpu.SMEM)]
+        + [pl.BlockSpec(b.shape, lambda j: (0, 0), pipeline_mode=once) for b in blocks]
+        + [
+            pl.BlockSpec((width, tile), lambda j: (0, j)),
+            pl.BlockSpec((width, tile), lambda j: (0, steps + j)),
+            pl.BlockSpec((tile, width), lambda j: (j, 0)),
+        ],
+        out_specs=[pl.BlockSpec((rows, tile), lambda j: (0, j))] * 3
+        + [pl.BlockSpec((rows, extra), lambda j: (0, 0))] * with_rwg,
+        out_shape=[jax.ShapeDtypeStruct((rows, cols), jnp.bfloat16)] * 3
+        + [jax.ShapeDtypeStruct((rows, extra), jnp.bfloat16)] * with_rwg,
+        scratch_shapes=[pltpu.VMEM((rows, cols // hid), jnp.float32)],
+        compiler_params=pltpu.CompilerParams(vmem_limit_bytes=ROUTES_BYTES),
+        cost_estimate=pl.CostEstimate(
+            flops=6 * rows * width * cols // DECLARED,
+            bytes_accessed=2 * (2 * rows * width + 3 * width * cols) // DECLARED,
+            transcendentals=0,
+        ),
+        name="routes_pass",
+    )(mine, *blocks, wgu, wgu, wd)
+
+
+def out_kernel(pieces, token_ref, *refs):
+    made, (wd, wgu), outs = refs[: 4 * pieces], refs[4 * pieces : 4 * pieces + 2], refs[4 * pieces + 2 :]
+    j, steps = pl.program_id(0), (pl.num_programs(0) - 1) // 2
+    tile = wd.shape[1]
+    cols = wd.shape[0]
+
+    def put(p, value):
+        half = value.shape[0] // 2
+        outs[2 * p][:, : value.shape[1]] = value[:half].astype(jnp.bfloat16)
+        outs[2 * p + 1][:, : value.shape[1]] = value[half:].astype(jnp.bfloat16)
+
+    for p in range(pieces):
+        hw, dg, du, extra = made[4 * p : 4 * p + 4]
+
+        @pl.when(j < steps)
+        def _():
+            put(p, jnp.dot(hw[...], wd[...], preferred_element_type=jnp.float32))
+
+        @pl.when((j >= steps) & (j < 2 * steps))
+        def _():
+            put(
+                p,
+                sum(
+                    lax.dot_general(
+                        d[...],
+                        wgu[:, at : at + cols],
+                        (((1,), (1,)), ((), ())),
+                        preferred_element_type=jnp.float32,
+                    )
+                    for d, at in ((dg, 0), (du, cols))
+                ),
+            )
+
+        @pl.when(j == 2 * steps)
+        def _():
+            put(p, extra[...])
+
+
+def out_pass(made, wgu, wd, token):
+    cols, width = wd.shape
+    tile = 512 if width % 512 == 0 else 128
+    steps, wide = width // tile, 2 * width + made[0][3].shape[1]
+    flat = [value for each in made for value in each]
+    outs = []
+    for each in made:
+        outs += [jax.ShapeDtypeStruct((each[0].shape[0] // 2, wide), jnp.bfloat16)] * 2
+    rows = sum(each[0].shape[0] for each in made)
+    got = pl.pallas_call(
+        functools.partial(out_kernel, len(made)),
+        grid=(2 * steps + 1,),
+        in_specs=[pl.BlockSpec(memory_space=pltpu.SMEM)]
+        + [pl.BlockSpec(v.shape, lambda j: (0, 0), pipeline_mode=pl.Buffered(1)) for v in flat]
+        + [
+            pl.BlockSpec((cols, tile), lambda j: (0, jnp.minimum(j, steps - 1))),
+            pl.BlockSpec((tile, 2 * cols), lambda j: (jnp.clip(j - steps, 0, steps - 1), 0)),
+        ],
+        out_specs=[pl.BlockSpec((o.shape[0], tile), lambda j: (0, j)) for o in outs],
+        out_shape=outs,
+        compiler_params=pltpu.CompilerParams(vmem_limit_bytes=OUT_BYTES),
+        cost_estimate=pl.CostEstimate(
+            flops=(6 * rows * width * cols) // DECLARED,
+            bytes_accessed=2 * (2 * rows * width + 3 * width * cols) // DECLARED,
+            transcendentals=0,
+        ),
+        name="out_pass",
+    )(token, *flat, wd, wgu)
+    return list(got)
+
+
+def grad_kernel(sources, parts, block_ref, *refs):
+    srcs, rhss, refs = refs[:sources], refs[sources : sources + parts], refs[sources + parts :]
+    j, out_ref, turned = pl.program_id(0), refs[-2], refs[-1]
+
+    @pl.when(j == 0)
+    def _():
+        at = 0
+        for src in srcs:
+            turned[:, at : at + src.shape[0]] = src[...].T
+            at += src.shape[0]
+
+    rhs = jnp.concatenate([ref[...] for ref in rhss], 0)
+    total = jnp.dot(turned[...], rhs, preferred_element_type=jnp.float32)
+    if len(refs) == 2:
+        out_ref[...] = total.astype(out_ref.dtype)
+    else:
+        total = total + refs[0][...].astype(jnp.float32)
+        for e in range(out_ref.shape[1]):
+
+            @pl.when(j == e)
+            def _():
+                out_ref[:, e, :] = total
+
+
+def grad_pass(srcs, rhss, block, own, hid, name, first=0, exp_dev=None, got=None):
+    rows, cols = sum(src.shape[0] for src in srcs), exp_dev * hid
+    in_specs = [pl.BlockSpec((src.shape[0], own), lambda j, b: (0, b[0])) for src in srcs]
+    in_specs += [pl.BlockSpec((rhs.shape[0], hid), lambda j, b: (0, first + j)) for rhs in rhss]
+    out_spec = pl.BlockSpec((own, hid), lambda j, b: (0, j))
+    out_shape = jax.ShapeDtypeStruct((own, cols), jnp.bfloat16)
+    operands = [*srcs, *rhss]
+    if got is not None:
+        in_specs.append(out_spec)
+        operands.append(got)
+        out_spec = pl.BlockSpec((own, exp_dev, hid), lambda j, b: (0, 0, 0))
+        out_shape = jax.ShapeDtypeStruct((own, exp_dev, hid), jnp.float32)
+    return pl.pallas_call(
+        functools.partial(grad_kernel, len(srcs), len(rhss)),
+        grid_spec=pltpu.PrefetchScalarGridSpec(
+            num_scalar_prefetch=1,
+            grid=(exp_dev,),
+            in_specs=in_specs,
+            out_specs=out_spec,
+            scratch_shapes=[pltpu.VMEM((own, rows), jnp.bfloat16)],
+        ),
+        out_shape=out_shape,
+        compiler_params=pltpu.CompilerParams(vmem_limit_bytes=GRAD_BYTES),
+        cost_estimate=pl.CostEstimate(
+            flops=2 * rows * own * cols // DECLARED,
+            bytes_accessed=2 * (rows * (own + cols) + own * cols) // DECLARED,
+            transcendentals=0,
+        ),
+        name=name,
+    )(block, *operands)
+
+
+def sum_kernel(keep_ref, got_ref, out_ref):
+    total = keep_ref[...].astype(jnp.float32) + got_ref[...].astype(jnp.float32)
+    hid = out_ref.shape[2]
+    for e in range(out_ref.shape[1]):
+        out_ref[:, e, :] = total[:, e * hid : (e + 1) * hid]
+
+
+def sum_pass(keep, got, exp_dev):
+    rows, cols = keep.shape
+    tile = min(128, rows)
+    block = pl.BlockSpec((tile, cols), lambda i: (i, 0))
+    return pl.pallas_call(
+        sum_kernel,
+        grid=(rows // tile,),
+        in_specs=[block, block],
+        out_specs=pl.BlockSpec((tile, exp_dev, cols // exp_dev), lambda i: (i, 0, 0)),
+        out_shape=jax.ShapeDtypeStruct((rows, exp_dev, cols // exp_dev), jnp.float32),
+        compiler_params=pltpu.CompilerParams(vmem_limit_bytes=SUM_BYTES),
+        name="sum_pass",
+    )(keep, got)
+
+
+def dense_form(tokens, routes, route_weights, cotangent, gate_proj, up_proj, down_proj):
+    tok_dev, width = tokens.shape
+    exp_dev, hid = down_proj.shape[:2]
+    cols = exp_dev * hid
+    n_dp = lax.axis_size("dp")
+    own = width // n_dp
+    experts = exp_dev * lax.axis_size("expert")
+    mine = (lax.axis_index("expert") * exp_dev).reshape(1).astype(jnp.int32)
+    here = lax.axis_index("dp")
+
+    named = routes[:, :, None] == jnp.arange(experts, dtype=jnp.int32)[None, None, :]
+    dense = jnp.sum(jnp.where(named, route_weights[:, :, None], 0.0), axis=1)
+    high = lax.reduce_precision(dense, 8, 7)
+    space = -(2 * experts) % 128
+    xc = jnp.concatenate(
+        [tokens, cotangent, high.astype(jnp.bfloat16), (dense - high).astype(jnp.bfloat16)]
+        + [jnp.zeros((tok_dev, space), jnp.bfloat16)],
+        1,
+    )
+    wgu = jnp.concatenate(
+        [gate_proj[e] for e in range(exp_dev)] + [up_proj[e] for e in range(exp_dev)], 1
+    )
+    wd = down_proj.reshape(cols, width)
+
+    def work(blocks, with_rwg):
+        return list(routes_pass(blocks, mine, wgu, wd, hid, experts, with_rwg))
+
+    halves = [xc[: tok_dev // 2], xc[tok_dev // 2 :]]
+    pieces, made = gather_planes(halves, list(range(0, n_dp, 2)), work)
+    arrived = [block for piece in pieces for block in piece]
+    hws, dgs, dus = [[values[n] for values in made] for n in range(3)]
+    own_made = made[: len(way_bits("expert"))]
+    mates, token = (here ^ 1).reshape(1).astype(jnp.int32), here.reshape(1).astype(jnp.int32)
+
+    def grad(rhss, block, of_cot, name, first=0, count=exp_dev, got=None):
+        block = block + (n_dp if of_cot else 0)
+        return grad_pass(arrived, rhss, block, own, hid, name, first, count, got)
+
+    gate_send, mates = together([grad(dgs, mates, False, "gate_send"), mates])
+    up_send, after = together([grad(dus, mates, False, "up_send"), mates])
+    gate_got, up_send, mates, token, *shares = together(
+        [swap(gate_send, "dp", 1), up_send, after, token] + out_pass(own_made, wgu, wd, after)
+    )
+    chip = [add_to(k, swap(v, "expert", 1)) for k, v in zip(shares[::2], shares[1::2])]
+    down_send = grad(hws, mates, True, "down_send")
+    *chip[-1:], token, down_send = together([chip[-1], token, down_send])
+    sides = [[p[: p.shape[0] // 2] for p in chip], [p[p.shape[0] // 2 :] for p in chip]]
+    gate_grad = grad(dgs, token, False, "gate_grad", got=gate_got)
+    beside = [swap(up_send, "dp", 1), down_send, gate_grad, token]
+    rounds = list(enumerate(way_bits("expert")))[::-1]
+    for s, bits in rounds[:-1]:
+        sides, beside = scatter_round(sides, s, bits, beside)
+    up_got, down_send, gate_grad, token = beside
+    down_got = swap(down_send, "dp", 1)
+    up_grad = grad(dus, token, False, "up_grad", got=up_got)
+    down_keep = grad(hws, token, True, "down_keep")
+    sides, (down_got, up_grad, down_keep) = scatter_round(
+        sides, *rounds[-1], [down_got, up_grad, down_keep]
+    )
+    summed = join([sides[0][0], sides[1][0]])
+    grads = [gate_grad, up_grad, sum_pass(down_keep, down_got, exp_dev)]
+
+    tail = summed[:, 2 * width :].astype(jnp.float32)
+    rwg_dense = tail[:, :experts] + tail[:, experts : 2 * experts]
+    route_weight_grad = jnp.sum(jnp.where(named, rwg_dense[:, None, :], 0.0), axis=2)
+    return (summed[:, :width], summed[:, width : 2 * width], route_weight_grad, *grads)
 
 
 def swish_parts(gate_pre):
@@ -34,7 +431,7 @@
     )
 
 
-def on_device(tokens, routes, route_weights, cotangent, gate_proj, up_proj, down_proj):
+def slots_form(tokens, routes, route_weights, cotangent, gate_proj, up_proj, down_proj):
     tok_dev, model_width = tokens.shape
     top_count = routes.shape[1]
     exp_dev = gate_proj.shape[0]
@@ -106,27 +503,20 @@
     return (layer_output, input_grad, route_weight_grad, shares[:, 0], shares[:, 1], shares[:, 2])
 
 
+def on_device(tokens, routes, route_weights, cotangent, gate_proj, up_proj, down_proj):
+    experts = gate_proj.shape[0] * lax.axis_size("expert")
+    form = dense_form if experts <= 2 * routes.shape[1] else slots_form
+    return form(tokens, routes, route_weights, cotangent, gate_proj, up_proj, down_proj)
+
+
 def solution(mesh):
-    placed = (
-        P(("dp", "expert"), None),
-        P(("dp", "expert"), None),
-        P(("dp", "expert"), None),
-        P(("dp", "expert"), None),
-        P("expert", None, None),
-        P("expert", None, None),
-        P("expert", None, None),
-    )
+    rows = P(("dp", "expert"), None)
+    held = P("expert", None, None)
+    owned = P("dp", "expert", None)
     return jax.shard_map(
         on_device,
         mesh=mesh,
-        in_specs=placed,
-        out_specs=(
-            P(("dp", "expert"), None),
-            P(("dp", "expert"), None),
-            P(("dp", "expert"), None),
-            P("dp", "expert", None),
-            P("dp", "expert", None),
-            P("dp", "expert", None),
-        ),
+        in_specs=(rows, rows, rows, rows, held, held, held),
+        out_specs=(rows, rows, rows, owned, owned, owned),
         check_vma=False,
     )

time: 523 us -> 245 us (0.47)
  waiting for transfers between devices: 280 us -> 44.4 us
  Pallas kernels: 0 us -> 137 us
  matrix products: 97.8 us -> 0 us
  local copies, waits for them, and re-layouts: 81.7 us -> 20.7 us
  between operations: 14.5 us -> 0.95 us
  other arithmetic: 27.6 us -> 17 us
    all_to_all x4 -> x0, waiting for transfers between devices: 205 us -> none  [the longest x1 53.4 us: on_device(): lax.all_to_all(route_dx, 'expert', split_axis=0, concat_axis=0, tiled=True)]
    pallas_call x0 -> x12, Pallas kernels: none -> 137 us  [the longest x4 60.2 us: routes_pass(): pl.pallas_call(functools.partial(routes_kernel, len(blocks), hid, experts...]
    dot_general x10 -> x0, matrix products: 97.8 us -> none  [the longest x1 17.3 us: three_terms(): jnp.einsum('secd,sech->deh', feat_rows, d_up, preferred_element_type=jnp....]
    reduce_scatter x1 -> x0, waiting for transfers between devices: 75.1 us -> none  [on_device(): lax.psum_scatter(full_terms.astype(jnp.bfloat16), 'dp', scatter_dimension...]
    gather x4 -> x0, local copies, waits for them, and re-layouts: 47.7 us -> none  [the longest x1 15.5 us: on_device(): padded_cot[slot_source].reshape(groups, exp_dev, capacity, model_width)]
    ppermute x0 -> x23, waiting for transfers between devices: none -> 44.4 us  [swap(): lax.ppermute(value, axis, [(i, i ^ mask) for i in range(lax.axis_size(axi...]
    ppermute x0 -> x23, starting transfers between devices: none -> 24.7 us  [swap(): lax.ppermute(value, axis, [(i, i ^ mask) for i in range(lax.axis_size(axi...]
    all_to_all x4 -> x0, starting transfers between devices: 19.5 us -> none  [the longest x1 5.3 us: on_device(): lax.all_to_all(outgoing, 'expert', split_axis=0, concat_axis=0, tiled=True)]
  transfers between devices with their start and end apart: 5 -> 23, of which waited for: 5 -> 10; matrix products, arithmetic and copies ran while one was open for 22% -> 12% of each run, Pallas kernels for 0% -> 46%
where the time goes in v2:
time: 245 us; the launch traced here: 244 us
  Pallas kernels  137 us (56%)
  waiting for transfers between devices  44.4 us (18%)
  starting transfers between devices  24.7 us (10%)
  local copies, waits for them, and re-layouts  20.7 us (8%)
  other arithmetic  17 us (7%)
    pallas_call x4, Pallas kernels, routes_pass(): pl.pallas_call(functools.partial(routes_kernel, len(blocks), hid, experts...  60.2 us
    pallas_call x6, Pallas kernels, grad_pass(): pl.pallas_call(functools.partial(grad_kernel, len(srcs), len(rhss)), grid...  48.5 us
    ppermute x23, waiting for transfers between devices, swap(): lax.ppermute(value, axis, [(i, i ^ mask) for i in range(lax.axis_size(axi...  44.4 us
    pallas_call x1, Pallas kernels, out_pass(): pl.pallas_call(functools.partial(out_kernel, len(made)), grid=(2 * steps...  25.5 us
    ppermute x23, starting transfers between devices, swap(): lax.ppermute(value, axis, [(i, i ^ mask) for i in range(lax.axis_size(axi...  24.7 us
    unnamed x27, local copies, waits for them, and re-layouts  9.51 us
    concatenate x6, other arithmetic, join(): return parts[0] if len(parts) == 1 else jnp.concatenate(parts, 0)  6.72 us
    concatenate x1, other arithmetic, dense_form(): jnp.concatenate([gate_proj[e] for e in range(exp_dev)] + [up_proj[e] for...  5.57 us
  transfers between devices with their start and end apart: 23, of which 10 were waited for; matrix products, arithmetic and copies ran while one was open for 12% of the time, Pallas kernels for 46%

profile of v2, /device:TPU:0, one launch (start us, length us, event | category | flops | bytes accessed | tf_op | source)
XLA Modules:
  0.0 244.4 jit_solution(18268917755188225748)
XLA Ops:
  1.7 2.3 concatenate.35
  4.1 4.1 %collective-permute-start.6 = (bf16[64,4224]{1,0:T(8,128)(2,1)S(1)}, bf16[64,4224]{1,0:T(8,128)(2,1)}, u32[]{:S(2)}, u32[]{:S(2)}) collective-permute-start(bf16[64,4224]{1,0:T(8,128)(2,1)S(1)} %get-tuple-element.140), channel_id=1, source_target_pairs={{0,16},{8,24},{16,0},{24,8},{1,17},{9,25},{17,1},{25,9},{2,18},{10... | collective-permute-start | bytes 1622024 | tf_op jit(solution)/shard_map/ppermute | solution.py:16
  8.2 1.5 collective-permute-start.1
  10.1 1.5 collective-permute-start
  11.6 4.5 %slice_bitcast_fusion.1 = (bf16[2048,640]{1,0:T(8,128)(2,1)S(1)}, bf16[2048,640]{1,0:T(8,128)(2,1)S(1)}, bf16[2048,640]{1,0:T(8,128)(2,1)S(1)}, bf16[2048,640]{1,0:T(8,128)(2,1)S(1)}) fusion(bf16[2,2048,640]{2,1,0:T(8,128)(2,1)} %param.12, bf16[2,2048,640]{2,1,0:T(8,128)(2,1)} %param.11), kind=kLoop, calls=%fused_computation.4 | loop fusion | bytes 20971520 | tf_op jit(solution)/shard_map/squeeze | solution.py:356
  16.1 5.9 %collective-permute-done.1 = bf16[64,4224]{1,0:T(8,128)(2,1)S(1)} collective-permute-done((bf16[64,4224]{1,0:T(8,128)(2,1)S(1)}, bf16[64,4224]{1,0:T(8,128)(2,1)S(1)}, u32[]{:S(2)}, u32[]{:S(2)}) %collective-permute-start.1) | collective-permute-done | bytes 540704 | tf_op jit(solution)/shard_map/ppermute | solution.py:16
  22.0 1.3 collective-permute-done
  23.5 1.2 pad_maximum_fusion.3
  24.7 1.5 collective-permute-start.4
  27.8 5.6 %pad_maximum_fusion.refs_2_.refs_3_.refs_9_ = bf16[2048,2560]{1,0:T(8,128)(2,1)} fusion(bf16[2048,640]{1,0:T(8,128)(2,1)S(1)} %get-tuple-element.133, bf16[2048,640]{1,0:T(8,128)(2,1)S(1)} %get-tuple-element.132, bf16[2048,640]{1,0:T(8,128)(2,1)S(1)} %get-tuple-element.144, bf16[2048,640]{1,0:T(8,128)(2,1)S(1)} %get-tuple-element.145), kind=kLoop, calls=%fused_computation | loop fusion | flops 41943040 | bytes 20971520 | tf_op jit(solution)/shard_map/concatenate | solution.py:355
  33.4 15.3 %routes_pass.4 = (bf16[512,1280]{1,0:T(8,128)(2,1)}, bf16[512,1280]{1,0:T(8,128)(2,1)}, bf16[512,1280]{1,0:T(8,128)(2,1)}, bf16[512,128]{1,0:T(8,128)(2,1)}) custom-call(s32[1]{0:T(128)} %bitcast.1.mine_ref, bf16[256,4224]{1,0:T(8,128)(2,1)} %copy-done.1, bf16[256,4224]{1,0:T(8,128)(2,1)} %collective-permute-done.2.refs_1_, ...), custom_call_target="tpu_custom_call" | custom-call | flops 7680 | bytes 19 | tf_op jit(solution)/shard_map/routes_pass/pallas_call | solution.py:164
  48.7 6.7 %collective-permute-done.5 = bf16[64,4224]{1,0:T(8,128)(2,1)} collective-permute-done((bf16[64,4224]{1,0:T(8,128)(2,1)S(1)}, bf16[64,4224]{1,0:T(8,128)(2,1)}, u32[]{:S(2)}, u32[]{:S(2)}) %collective-permute-start.5) | collective-permute-done | bytes 540704 | tf_op jit(solution)/shard_map/ppermute | solution.py:16
  55.4 1.5 collective-permute-start.8
  56.9 1.5 collective-permute-start.9
  58.5 1.3 constant_dynamic-update-slice_fusion.1
  59.8 1.4 constant_dynamic-update-slice_fusion.refs_0_.refs_2_
  61.2 2.3 constant_dynamic-update-slice_fusion.5
  63.5 5.5 %collective-permute-done.8 = bf16[64,4224]{1,0:T(8,128)(2,1)S(1)} collective-permute-done((bf16[64,4224]{1,0:T(8,128)(2,1)}, bf16[64,4224]{1,0:T(8,128)(2,1)S(1)}, u32[]{:S(2)}, u32[]{:S(2)}) %collective-permute-start.8) | collective-permute-done | bytes 540704 | tf_op jit(solution)/shard_map/ppermute | solution.py:16
  70.0 1.1 pad_maximum_fusion.5
  72.0 2.1 pad_maximum_fusion.4
  74.1 1.3 collective-permute-start.11
  76.2 1.9 constant_dynamic-update-slice_fusion.3
  79.0 1.3 copy-done.4
  80.3 15.3 %routes_pass.5 = (bf16[512,1280]{1,0:T(8,128)(2,1)}, bf16[512,1280]{1,0:T(8,128)(2,1)}, bf16[512,1280]{1,0:T(8,128)(2,1)}, bf16[512,128]{1,0:T(8,128)(2,1)}) custom-call(s32[1]{0:T(128)} %bitcast.1.mine_ref, bf16[256,4224]{1,0:T(8,128)(2,1)} %copy-done.2, bf16[256,4224]{1,0:T(8,128)(2,1)} %copy-done.4, ...), custom_call_target="tpu_custom_call" | custom-call | flops 7680 | bytes 19 | tf_op jit(solution)/shard_map/routes_pass/pallas_call | solution.py:164
  95.6 2.4 collective-permute-done.11
  98.0 1.3 constant_dynamic-update-slice_fusion.7
  99.5 15.1 %routes_pass.6 = (bf16[512,1280]{1,0:T(8,128)(2,1)}, bf16[512,1280]{1,0:T(8,128)(2,1)}, bf16[512,1280]{1,0:T(8,128)(2,1)}) custom-call(s32[1]{0:T(128)} %bitcast.1.mine_ref, bf16[256,4224]{1,0:T(8,128)(2,1)} %constant_dynamic-update-slice_fusion.2.refs_0_.refs_4_, bf16[256,4224]{1,0:T(8,128)(2,1)} %collective-permute-done.10.refs_1_.refs_5_, ...), custom_call_target="tpu_custom_call" | custom-call | flops 7680 | bytes 19 | tf_op jit(solution)/shard_map/routes_pass/pallas_call | solution.py:164
  114.7 14.5 %routes_pass.7 = (bf16[512,1280]{1,0:T(8,128)(2,1)}, bf16[512,1280]{1,0:T(8,128)(2,1)}, bf16[512,1280]{1,0:T(8,128)(2,1)}) custom-call(s32[1]{0:T(128)} %bitcast.1.mine_ref, bf16[256,4224]{1,0:T(8,128)(2,1)} %copy-done.3, bf16[256,4224]{1,0:T(8,128)(2,1)} %collective-permute-done.13.refs_1_.refs_7_, ...), custom_call_target="tpu_custom_call" | custom-call | flops 7680 | bytes 19 | tf_op jit(solution)/shard_map/routes_pass/pallas_call | solution.py:164
  129.1 7.8 %gate_send.1 = bf16[512,1280]{1,0:T(8,128)(2,1)} custom-call(s32[1]{0:T(128)} %bitcast.block_ref.token_ref, bf16[256,4224]{1,0:T(8,128)(2,1)} %copy-done.1, bf16[256,4224]{1,0:T(8,128)(2,1)} %collective-permute-done.2.refs_1_, bf16[256,4224]{1,0:T(8,128)(2,1)} %copy-done.2, bf16[256,4224]{1,0:T(8,128)(2,1)} %copy-done.4, ...), custom_call_target="tpu_custom_call" | custom-call | flops 2560 | bytes 8 | tf_op jit(solution)/shard_map/gate_send/pallas_call | solution.py:294
  136.9 2.2 collective-permute-start.14
  139.1 7.6 %up_send.1 = bf16[512,1280]{1,0:T(8,128)(2,1)} custom-call(s32[1]{0:T(128)} %bitcast.block_ref.token_ref, bf16[256,4224]{1,0:T(8,128)(2,1)} %copy-done.1, bf16[256,4224]{1,0:T(8,128)(2,1)} %collective-permute-done.2.refs_1_, bf16[256,4224]{1,0:T(8,128)(2,1)} %copy-done.2, bf16[256,4224]{1,0:T(8,128)(2,1)} %copy-done.4, ...), custom_call_target="tpu_custom_call" | custom-call | flops 2560 | bytes 8 | tf_op jit(solution)/shard_map/up_send/pallas_call | solution.py:294
  146.6 25.5 %out_pass.1 = (bf16[256,4224]{1,0:T(8,128)(2,1)}, bf16[256,4224]{1,0:T(8,128)(2,1)}, bf16[256,4224]{1,0:T(8,128)(2,1)}, bf16[256,4224]{1,0:T(8,128)(2,1)}) custom-call(s32[1]{0:T(128)} %bitcast.block_ref.token_ref, bf16[512,1280]{1,0:T(8,128)(2,1)} %get-tuple-element.98.refs_0_.refs_8_, bf16[512,1280]{1,0:T(8,128)(2,1)} %get-tuple-element.86.refs_8_.refs_1_, ...), custom_call_target="tpu_custom_call" | custom-call | flops 15360 | bytes 23 | tf_op jit(solution)/shard_map/out_pass/pallas_call | solution.py:236
  173.2 7.7 %down_send.1 = bf16[512,1280]{1,0:T(8,128)(2,1)} custom-call(s32[1]{0:T(128)S(6)} %add.29.block_ref, bf16[256,4224]{1,0:T(8,128)(2,1)} %copy-done.1, bf16[256,4224]{1,0:T(8,128)(2,1)} %collective-permute-done.2.refs_1_, bf16[256,4224]{1,0:T(8,128)(2,1)} %copy-done.2, bf16[256,4224]{1,0:T(8,128)(2,1)} %copy-done.4, ...), custom_call_target="tpu_custom_call" | custom-call | flops 2560 | bytes 8 | tf_op jit(solution)/shard_map/down_send/pallas_call | solution.py:294
  181.4 1.5 fusion.3
  182.9 1.4 collective-permute-start.19
  184.3 1.5 collective-permute-start.18
  185.9 9.0 %gate_grad.1 = f32[512,2,640]{2,1,0:T(2,128)} custom-call(s32[1]{0:T(128)} %bitcast.7.block_ref, bf16[256,4224]{1,0:T(8,128)(2,1)} %copy-done.1, bf16[256,4224]{1,0:T(8,128)(2,1)} %collective-permute-done.2.refs_1_, bf16[256,4224]{1,0:T(8,128)(2,1)} %copy-done.2, bf16[256,4224]{1,0:T(8,128)(2,1)} %copy-done.4, ...), custom_call_target="tpu_custom_call" | custom-call | flops 2560 | bytes 8 | tf_op jit(solution)/shard_map/gate_grad/pallas_call | solution.py:294
  195.4 8.2 %collective-permute-done.16.refs_12_ = bf16[512,1280]{1,0:T(8,128)(2,1)S(1)} collective-permute-done((bf16[512,1280]{1,0:T(8,128)(2,1)}, bf16[512,1280]{1,0:T(8,128)(2,1)S(1)}, u32[]{:S(2)}, u32[]{:S(2)}) %collective-permute-start.16) | collective-permute-done | bytes 1310752 | tf_op jit(solution)/shard_map/ppermute | solution.py:16
  203.6 5.1 %collective-permute-done.19 = bf16[128,4224]{1,0:T(8,128)(2,1)} collective-permute-done((bf16[128,4224]{1,0:T(8,128)(2,1)}, bf16[128,4224]{1,0:T(8,128)(2,1)}, u32[]{:S(2)}, u32[]{:S(2)}) %collective-permute-start.19) | collective-permute-done | bytes 1081376 | tf_op jit(solution)/shard_map/ppermute | solution.py:16
  208.7 1.1 collective-permute-done.18
  209.8 1.9 collective-permute-start.20
  211.8 2.1 add_convert_fusion.2
  214.6 1.5 collective-permute-start.22
  216.1 7.5 %down_keep.1.keep_ref = bf16[512,1280]{1,0:T(8,128)(2,1)} custom-call(s32[1]{0:T(128)S(6)} %add.31.block_ref, bf16[256,4224]{1,0:T(8,128)(2,1)} %copy-done.1, bf16[256,4224]{1,0:T(8,128)(2,1)} %collective-permute-done.2.refs_1_, bf16[256,4224]{1,0:T(8,128)(2,1)} %copy-done.2, bf16[256,4224]{1,0:T(8,128)(2,1)} %copy-done.4, ...), custom_call_target="tpu_custom_call" | custom-call | flops 2560 | bytes 8 | tf_op jit(solution)/shard_map/down_keep/pallas_call | solution.py:294
  223.6 9.0 %up_grad.1 = f32[512,2,640]{2,1,0:T(2,128)} custom-call(s32[1]{0:T(128)} %bitcast.7.block_ref, bf16[256,4224]{1,0:T(8,128)(2,1)} %copy-done.1, bf16[256,4224]{1,0:T(8,128)(2,1)} %collective-permute-done.2.refs_1_, bf16[256,4224]{1,0:T(8,128)(2,1)} %copy-done.2, bf16[256,4224]{1,0:T(8,128)(2,1)} %copy-done.4, ...), custom_call_target="tpu_custom_call" | custom-call | flops 2560 | bytes 8 | tf_op jit(solution)/shard_map/up_grad/pallas_call | solution.py:294
  232.7 7.3 %collective-permute-done.20.got_ref = bf16[512,1280]{1,0:T(8,128)(2,1)S(1)} collective-permute-done((bf16[512,1280]{1,0:T(8,128)(2,1)S(1)}, bf16[512,1280]{1,0:T(8,128)(2,1)S(1)}, u32[]{:S(2)}, u32[]{:S(2)}) %collective-permute-start.20) | collective-permute-done | bytes 1310752 | tf_op jit(solution)/shard_map/ppermute | solution.py:16
  240.2 1.1 fusion
  242.1 2.3 sum_pass.1
  (69 shorter events, 11.0 us)
Async XLA Ops:
  4.1 44.6 %collective-permute-start.6 = (bf16[64,4224]{1,0:T(8,128)(2,1)S(1)}, bf16[64,4224]{1,0:T(8,128)(2,1)}, u32[]{:S(2)}, u32[]{:S(2)}) collective-permute-start(bf16[64,4224]{1,0:T(8,128)(2,1)S(1)} %get-tuple-element.140), channel_id=1, source_target_pairs={{0,16},{8,24},{16,0},{24,8},{1,17},{9,25},{17,1},{25,9},{2,18},{10... | collective-permute-start | bytes 1622024 | tf_op jit(solution)/shard_map/ppermute | solution.py:16
  8.2 13.7 %collective-permute-start.1 = (bf16[64,4224]{1,0:T(8,128)(2,1)S(1)}, bf16[64,4224]{1,0:T(8,128)(2,1)S(1)}, u32[]{:S(2)}, u32[]{:S(2)}) collective-permute-start(bf16[64,4224]{1,0:T(8,128)(2,1)S(1)} %get-tuple-element.140), channel_id=1, source_target_pairs={{0,4},{1,5},{2,6},{3,7},{4,0},{5,1},{6,2},{7,3},{8,12},{9,13},{10,... | collective-permute-start | bytes 1622024 | tf_op jit(solution)/shard_map/ppermute | solution.py:16
  9.8 45.6 %collective-permute-start.5 = (bf16[64,4224]{1,0:T(8,128)(2,1)S(1)}, bf16[64,4224]{1,0:T(8,128)(2,1)}, u32[]{:S(2)}, u32[]{:S(2)}) collective-permute-start(bf16[64,4224]{1,0:T(8,128)(2,1)S(1)} %get-tuple-element.141), channel_id=1, source_target_pairs={{0,16},{8,24},{16,0},{24,8},{1,17},{9,25},{17,1},{25,9},{2,18},{10... | collective-permute-start | bytes 1622024 | tf_op jit(solution)/shard_map/ppermute | solution.py:16
  10.1 13.2 %collective-permute-start = (bf16[64,4224]{1,0:T(8,128)(2,1)S(1)}, bf16[64,4224]{1,0:T(8,128)(2,1)S(1)}, u32[]{:S(2)}, u32[]{:S(2)}) collective-permute-start(bf16[64,4224]{1,0:T(8,128)(2,1)S(1)} %get-tuple-element.141), channel_id=1, source_target_pairs={{0,2},{1,3},{2,0},{3,1},{4,6},{5,7},{6,4},{7,5},{8,10},{9,11},{10,... | collective-permute-start | bytes 1622024 | tf_op jit(solution)/shard_map/ppermute | solution.py:16
  23.5 3.8 %copy-start.1 = (bf16[256,4224]{1,0:T(8,128)(2,1)}, bf16[256,4224]{1,0:T(8,128)(2,1)S(1)}, u32[]{:S(2)}) copy-start(bf16[256,4224]{1,0:T(8,128)(2,1)S(1)} %pad_maximum_fusion.1.refs_0_) | copy-start | bytes 6488068
  23.5 9.9 %collective-permute-start.2 = (bf16[256,4224]{1,0:T(8,128)(2,1)S(1)}, bf16[256,4224]{1,0:T(8,128)(2,1)}, u32[]{:S(2)}, u32[]{:S(2)}) collective-permute-start(bf16[256,4224]{1,0:T(8,128)(2,1)S(1)} %pad_maximum_fusion.1.refs_0_), channel_id=1, source_target_pairs={{0,1},{1,0},{2,3},{3,2},{4,5},{5,4},{6,7},{7,6},{8,9},{9,8},{10,11... | collective-permute-start | bytes 6488072 | tf_op jit(solution)/shard_map/ppermute | solution.py:16
  24.7 30.7 %collective-permute-start.4 = (bf16[128,4224]{1,0:T(8,128)(2,1)}, bf16[128,4224]{1,0:T(8,128)(2,1)}, u32[]{:S(2)}, u32[]{:S(2)}) collective-permute-start(bf16[128,4224]{1,0:T(8,128)(2,1)} %pad_maximum_fusion.3), channel_id=1, source_target_pairs={{0,2},{1,3},{2,0},{3,1},{4,6},{5,7},{6,4},{7,5},{8,10},{9,11},{10,... | collective-permute-start | bytes 3244040 | tf_op jit(solution)/shard_map/ppermute | solution.py:16
  27.3 28.1 %collective-permute-start.3 = (bf16[128,4224]{1,0:T(8,128)(2,1)}, bf16[128,4224]{1,0:T(8,128)(2,1)}, u32[]{:S(2)}, u32[]{:S(2)}) collective-permute-start(bf16[128,4224]{1,0:T(8,128)(2,1)} %pad_maximum_fusion.2), channel_id=1, source_target_pairs={{0,4},{1,5},{2,6},{3,7},{4,0},{5,1},{6,2},{7,3},{8,12},{9,13},{10,... | collective-permute-start | bytes 3244040 | tf_op jit(solution)/shard_map/ppermute | solution.py:16
  55.4 13.7 %collective-permute-start.8 = (bf16[64,4224]{1,0:T(8,128)(2,1)}, bf16[64,4224]{1,0:T(8,128)(2,1)S(1)}, u32[]{:S(2)}, u32[]{:S(2)}) collective-permute-start(bf16[64,4224]{1,0:T(8,128)(2,1)} %collective-permute-done.5), channel_id=1, source_target_pairs={{0,2},{1,3},{2,0},{3,1},{4,6},{5,7},{6,4},{7,5},{8,10},{9,11},{10,... | collective-permute-start | bytes 1622024 | tf_op jit(solution)/shard_map/ppermute | solution.py:16
  56.9 13.1 %collective-permute-start.9 = (bf16[64,4224]{1,0:T(8,128)(2,1)}, bf16[64,4224]{1,0:T(8,128)(2,1)S(1)}, u32[]{:S(2)}, u32[]{:S(2)}) collective-permute-start(bf16[64,4224]{1,0:T(8,128)(2,1)} %collective-permute-done.6), channel_id=1, source_target_pairs={{0,4},{1,5},{2,6},{3,7},{4,0},{5,1},{6,2},{7,3},{8,12},{9,13},{10,... | collective-permute-start | bytes 1622024 | tf_op jit(solution)/shard_map/ppermute | solution.py:16
  61.1 13.0 %copy-start.2 = (bf16[256,4224]{1,0:T(8,128)(2,1)}, bf16[256,4224]{1,0:T(8,128)(2,1)S(1)}, u32[]{:S(2)}) copy-start(bf16[256,4224]{1,0:T(8,128)(2,1)S(1)} %constant_dynamic-update-slice_fusion.refs_0_.refs_2_) | copy-start | bytes 6488068
  61.1 17.8 %collective-permute-start.7 = (bf16[256,4224]{1,0:T(8,128)(2,1)S(1)}, bf16[256,4224]{1,0:T(8,128)(2,1)S(1)}, u32[]{:S(2)}, u32[]{:S(2)}) collective-permute-start(bf16[256,4224]{1,0:T(8,128)(2,1)S(1)} %constant_dynamic-update-slice_fusion.refs_0_.refs_2_), channel_id=1, source_target_pairs={{0,1},{1,0},{2,3},{3,2},{4,5},{5,4},{6,7},{7,6},{8,9},{9,8},{10,11... | collective-permute-start | bytes 6488072 | tf_op jit(solution)/shard_map/ppermute | solution.py:16
  71.2 24.5 %collective-permute-start.12 = (bf16[128,4224]{1,0:T(8,128)(2,1)S(1)}, bf16[128,4224]{1,0:T(8,128)(2,1)S(1)}, u32[]{:S(2)}, u32[]{:S(2)}) collective-permute-start(bf16[128,4224]{1,0:T(8,128)(2,1)S(1)} %pad_maximum_fusion.5), channel_id=1, source_target_pairs={{0,2},{1,3},{2,0},{3,1},{4,6},{5,7},{6,4},{7,5},{8,10},{9,11},{10,... | collective-permute-start | bytes 3244040 | tf_op jit(solution)/shard_map/ppermute | solution.py:16
  74.1 23.9 %collective-permute-start.11 = (bf16[128,4224]{1,0:T(8,128)(2,1)}, bf16[128,4224]{1,0:T(8,128)(2,1)}, u32[]{:S(2)}, u32[]{:S(2)}) collective-permute-start(bf16[128,4224]{1,0:T(8,128)(2,1)} %pad_maximum_fusion.4), channel_id=1, source_target_pairs={{0,4},{1,5},{2,6},{3,7},{4,0},{5,1},{6,2},{7,3},{8,12},{9,13},{10,... | collective-permute-start | bytes 3244040 | tf_op jit(solution)/shard_map/ppermute | solution.py:16
  79.0 20.6 %collective-permute-start.10 = (bf16[256,4224]{1,0:T(8,128)(2,1)}, bf16[256,4224]{1,0:T(8,128)(2,1)}, u32[]{:S(2)}, u32[]{:S(2)}) collective-permute-start(bf16[256,4224]{1,0:T(8,128)(2,1)} %constant_dynamic-update-slice_fusion.2.refs_0_.refs_4_), channel_id=1, source_target_pairs={{0,1},{1,0},{2,3},{3,2},{4,5},{5,4},{6,7},{7,6},{8,9},{9,8},{10,11... | collective-permute-start | bytes 6488072 | tf_op jit(solution)/shard_map/ppermute | solution.py:16
  79.0 1.3 copy-start.4
  99.4 15.2 %copy-start.3 = (bf16[256,4224]{1,0:T(8,128)(2,1)}, bf16[256,4224]{1,0:T(8,128)(2,1)S(1)}, u32[]{:S(2)}) copy-start(bf16[256,4224]{1,0:T(8,128)(2,1)S(1)} %constant_dynamic-update-slice_fusion.6.refs_0_.refs_6_) | copy-start | bytes 6488068
  99.4 15.2 %collective-permute-start.13 = (bf16[256,4224]{1,0:T(8,128)(2,1)S(1)}, bf16[256,4224]{1,0:T(8,128)(2,1)}, u32[]{:S(2)}, u32[]{:S(2)}) collective-permute-start(bf16[256,4224]{1,0:T(8,128)(2,1)S(1)} %constant_dynamic-update-slice_fusion.6.refs_0_.refs_6_), channel_id=1, source_target_pairs={{0,1},{1,0},{2,3},{3,2},{4,5},{5,4},{6,7},{7,6},{8,9},{9,8},{10,11... | collective-permute-start | bytes 6488072 | tf_op jit(solution)/shard_map/ppermute | solution.py:16
  136.9 35.2 %collective-permute-start.14 = (bf16[512,1280]{1,0:T(8,128)(2,1)}, bf16[512,1280]{1,0:T(8,128)(2,1)S(1)}, u32[]{:S(2)}, u32[]{:S(2)}) collective-permute-start(bf16[512,1280]{1,0:T(8,128)(2,1)} %gate_send.1), channel_id=1, source_target_pairs={{0,8},{8,0},{16,24},{24,16},{1,9},{9,1},{17,25},{25,17},{2,10},{10... | collective-permute-start | bytes 3932168 | tf_op jit(solution)/shard_map/ppermute | solution.py:16
  172.1 1.1 copy-start.9
  172.1 8.8 %collective-permute-start.17 = (bf16[256,4224]{1,0:T(8,128)(2,1)}, bf16[256,4224]{1,0:T(8,128)(2,1)S(1)}, u32[]{:S(2)}, u32[]{:S(2)}) collective-permute-start(bf16[256,4224]{1,0:T(8,128)(2,1)} %get-tuple-element.110), channel_id=1, source_target_pairs={{0,1},{1,0},{2,3},{3,2},{4,5},{5,4},{6,7},{7,6},{8,9},{9,8},{10,11... | collective-permute-start | bytes 6488072 | tf_op jit(solution)/shard_map/ppermute | solution.py:16
  172.2 31.4 %collective-permute-start.16 = (bf16[512,1280]{1,0:T(8,128)(2,1)}, bf16[512,1280]{1,0:T(8,128)(2,1)S(1)}, u32[]{:S(2)}, u32[]{:S(2)}) collective-permute-start(bf16[512,1280]{1,0:T(8,128)(2,1)} %up_send.1), channel_id=1, source_target_pairs={{0,8},{8,0},{16,24},{24,16},{1,9},{9,1},{17,25},{25,17},{2,10},{10... | collective-permute-start | bytes 3932168 | tf_op jit(solution)/shard_map/ppermute | solution.py:16
  172.3 22.5 %collective-permute-start.15 = (bf16[256,4224]{1,0:T(8,128)(2,1)}, bf16[256,4224]{1,0:T(8,128)(2,1)S(1)}, u32[]{:S(2)}, u32[]{:S(2)}) collective-permute-start(bf16[256,4224]{1,0:T(8,128)(2,1)} %get-tuple-element.107), channel_id=1, source_target_pairs={{0,1},{1,0},{2,3},{3,2},{4,5},{5,4},{6,7},{7,6},{8,9},{9,8},{10,11... | collective-permute-start | bytes 6488072 | tf_op jit(solution)/shard_map/ppermute | solution.py:16
  173.2 7.7 %copy-start.6 = (bf16[256,4224]{1,0:T(8,128)(2,1)S(1)}, bf16[256,4224]{1,0:T(8,128)(2,1)}, u32[]{:S(2)}) copy-start(bf16[256,4224]{1,0:T(8,128)(2,1)} %get-tuple-element.109) | copy-start | bytes 6488068
  182.9 25.8 %collective-permute-start.19 = (bf16[128,4224]{1,0:T(8,128)(2,1)}, bf16[128,4224]{1,0:T(8,128)(2,1)}, u32[]{:S(2)}, u32[]{:S(2)}) collective-permute-start(bf16[128,4224]{1,0:T(8,128)(2,1)} %get-tuple-element.136), channel_id=1, source_target_pairs={{0,2},{1,3},{2,0},{3,1},{4,6},{5,7},{6,4},{7,5},{8,10},{9,11},{10,... | collective-permute-start | bytes 3244040 | tf_op jit(solution)/shard_map/ppermute | solution.py:16
  184.3 10.5 %copy-start.5 = (bf16[256,4224]{1,0:T(8,128)(2,1)S(1)}, bf16[256,4224]{1,0:T(8,128)(2,1)}, u32[]{:S(2)}) copy-start(bf16[256,4224]{1,0:T(8,128)(2,1)} %get-tuple-element.106) | copy-start | bytes 6488068
  184.3 25.5 %collective-permute-start.18 = (bf16[128,4224]{1,0:T(8,128)(2,1)}, bf16[128,4224]{1,0:T(8,128)(2,1)}, u32[]{:S(2)}, u32[]{:S(2)}) collective-permute-start(bf16[128,4224]{1,0:T(8,128)(2,1)} %get-tuple-element.137), channel_id=1, source_target_pairs={{0,4},{1,5},{2,6},{3,7},{4,0},{5,1},{6,2},{7,3},{8,12},{9,13},{10,... | collective-permute-start | bytes 3244040 | tf_op jit(solution)/shard_map/ppermute | solution.py:16
  194.8 15.0 %copy-start.8 = (bf16[512,1280]{1,0:T(8,128)(2,1)S(1)}, bf16[512,1280]{1,0:T(8,128)(2,1)}, u32[]{:S(2)}) copy-start(bf16[512,1280]{1,0:T(8,128)(2,1)} %down_send.1) | copy-start | bytes 3932164
  203.6 5.1 %copy-start.7 = (bf16[512,1280]{1,0:T(8,128)(2,1)}, bf16[512,1280]{1,0:T(8,128)(2,1)S(1)}, u32[]{:S(2)}) copy-start(bf16[512,1280]{1,0:T(8,128)(2,1)S(1)} %collective-permute-done.16.refs_12_) | copy-start | bytes 3932164
  209.8 30.1 %collective-permute-start.20 = (bf16[512,1280]{1,0:T(8,128)(2,1)S(1)}, bf16[512,1280]{1,0:T(8,128)(2,1)S(1)}, u32[]{:S(2)}, u32[]{:S(2)}) collective-permute-start(bf16[512,1280]{1,0:T(8,128)(2,1)S(1)} %copy-done.8), channel_id=1, source_target_pairs={{0,8},{8,0},{16,24},{24,16},{1,9},{9,1},{17,25},{25,17},{2,10},{10... | collective-permute-start | bytes 3932168 | tf_op jit(solution)/shard_map/ppermute | solution.py:16
  213.9 18.7 %collective-permute-start.21 = (bf16[64,4224]{1,0:T(8,128)(2,1)S(1)}, bf16[64,4224]{1,0:T(8,128)(2,1)S(1)}, u32[]{:S(2)}, u32[]{:S(2)}) collective-permute-start(bf16[64,4224]{1,0:T(8,128)(2,1)S(1)} %slice.80), channel_id=1, source_target_pairs={{0,2},{1,3},{2,0},{3,1},{4,6},{5,7},{6,4},{7,5},{8,10},{9,11},{10,... | collective-permute-start | bytes 1622024 | tf_op jit(solution)/shard_map/ppermute | solution.py:16
  214.6 18.1 %collective-permute-start.22 = (bf16[64,4224]{1,0:T(8,128)(2,1)S(1)}, bf16[64,4224]{1,0:T(8,128)(2,1)S(1)}, u32[]{:S(2)}, u32[]{:S(2)}) collective-permute-start(bf16[64,4224]{1,0:T(8,128)(2,1)S(1)} %slice.82), channel_id=1, source_target_pairs={{0,4},{1,5},{2,6},{3,7},{4,0},{5,1},{6,2},{7,3},{8,12},{9,13},{10,... | collective-permute-start | bytes 1622024 | tf_op jit(solution)/shard_map/ppermute | solution.py:16
  240.2 1.3 copy-start.10
  240.2 1.9 copy-start

commit v3 on v2

--- a/solution.py
+++ b/solution.py
@@ -20,63 +20,12 @@
     return list(lax.optimization_barrier(tuple(values)))
 
 
-def way_bits(axis):
-    bits = [1 << b for b in range(1, lax.axis_size(axis).bit_length() - 1)]
-    return list(zip(bits, bits[::-1]))
-
-
 def join(parts):
     return parts[0] if len(parts) == 1 else jnp.concatenate(parts, 0)
 
 
-def gather_planes(own, masks, work):
-    pieces, halves, made, tied = [], own, [], 0
-    ways = way_bits("expert")
-    for n in range(len(masks)):
-        first, second = halves
-        for s, (bit_first, bit_second) in enumerate(ways):
-            sent = [swap(first, "expert", bit_first), swap(second, "expert", bit_second)]
-            if s == len(ways) - 1 and n + 1 < len(masks):
-                sent += [swap(half, "dp", masks[n + 1]) for half in own]
-            beside = []
-            if pieces:
-                pieces[-1].append(swap(pieces[-1][0], "expert", 1))
-                made.append(work(pieces[-1], len(pieces) <= len(ways)))
-            ended = range(tied, len(made) if len(sent) > 2 else len(made) - 1)
-            for p in ended:
-                beside += made[p]
-            got = together(sent + beside)
-            rest = got[len(sent) :]
-            for p in ended:
-                made[p], rest = rest[: len(made[p])], rest[len(made[p]) :]
-                tied = p + 1
-            halves = got[2 : len(sent)]
-            whole = [join([first, got[0]]), join([second, got[1]])]
-            pieces.append([join(whole if s == 0 else got[:2])])
-            first, second = whole
-    pieces[-1].append(swap(pieces[-1][0], "expert", 1))
-    made.append(work(pieces[-1], len(pieces) <= len(ways)))
-    return pieces, made
-
-
 def add_to(kept, received):
     return (kept.astype(jnp.float32) + received.astype(jnp.float32)).astype(kept.dtype)
-
-
-def scatter_round(sides, s, bits, beside):
-    if s == 0:
-        sides = [[p[0][: p[0].shape[0] // 2], p[0][p[0].shape[0] // 2 :]] for p in sides]
-    *beside, first, second = together(
-        beside + [swap(side[-1], "expert", bit) for side, bit in zip(sides, bits)]
-    )
-    summed = []
-    for side, value in zip(sides, (first, second)):
-        at, kept = 0, []
-        for part in side[:-1]:
-            kept.append(add_to(part, value[at : at + part.shape[0]]))
-            at += part.shape[0]
-        summed.append(kept)
-    return summed, beside
 
 
 def tile_of(cols):
@@ -95,8 +44,8 @@
     return spread
 
 
-def routes_kernel(blocks, hid, experts, with_rwg, mine_ref, *refs):
-    xcs, (wg, wu, wd, hw, dg, du, *more) = refs[:blocks], refs[blocks:]
+def routes_kernel(counts, hid, experts, with_rwg, mine_ref, *refs):
+    xcs, (wg, wu, wd, hw, dg, du, *more) = refs[: sum(counts)], refs[sum(counts) :]
     extra_ref, sums = more[0] if with_rwg else None, more[-1]
     j, (tile, width) = pl.program_id(0), wd.shape
     held = sums.shape[1]
@@ -107,20 +56,23 @@
 
     mine = mine_ref[0]
     end = 0
-    for xc in xcs:
-        rows = slice(end, end + xc.shape[0])
+    for count in counts:
+        group, xcs = xcs[:count], xcs[count:]
+        x = jnp.concatenate([ref[:, :width] for ref in group], 0)
+        c = jnp.concatenate([ref[:, width : 2 * width] for ref in group], 0)
+        tail = jnp.concatenate([ref[:, 2 * width :] for ref in group], 0).astype(jnp.float32)
+        rows = slice(end, end + x.shape[0])
         end = rows.stop
-        lane = lax.broadcasted_iota(jnp.int32, (xc.shape[0], tile), 1) + j * tile
-        tail = xc[:, 2 * width :].astype(jnp.float32)
+        lane = lax.broadcasted_iota(jnp.int32, (x.shape[0], tile), 1) + j * tile
         spot = lax.broadcasted_iota(jnp.int32, tail.shape, 1)
         spots = [(spot == mine + e, spot == experts + mine + e) for e in range(held)]
         weights = [
             jnp.sum(jnp.where(high | low, tail, 0.0), axis=1, keepdims=True) for high, low in spots
         ]
-        gate = jnp.dot(xc[:, :width], wg[...], preferred_element_type=jnp.float32)
-        up = jnp.dot(xc[:, :width], wu[...], preferred_element_type=jnp.float32)
+        gate = jnp.dot(x, wg[...], preferred_element_type=jnp.float32)
+        up = jnp.dot(x, wu[...], preferred_element_type=jnp.float32)
         d_plain = lax.dot_general(
-            xc[:, width : 2 * width],
+            c,
             wd[...],
             (((1,), (1,)), ((), ())),
             preferred_element_type=jnp.float32,
@@ -155,14 +107,15 @@
             extra_ref[...] = placed.astype(jnp.bfloat16)
 
 
-def routes_pass(blocks, mine, wgu, wd, hid, experts, with_rwg):
+def routes_pass(groups, mine, wgu, wd, hid, experts, with_rwg, declared=DECLARED):
+    counts, blocks = [len(group) for group in groups], [b for group in groups for b in group]
     rows, wide = sum(block.shape[0] for block in blocks), blocks[0].shape[1]
     cols, width = wd.shape
     tile, once = tile_of(cols), pl.Buffered(1)
     steps = cols // tile
     extra = wide - 2 * width
     return pl.pallas_call(
-        functools.partial(routes_kernel, len(blocks), hid, experts, with_rwg),
+        functools.partial(routes_kernel, counts, hid, experts, with_rwg),
         grid=(steps,),
         in_specs=[pl.BlockSpec(memory_space=pltpu.SMEM)]
         + [pl.BlockSpec(b.shape, lambda j: (0, 0), pipeline_mode=once) for b in blocks]
@@ -178,26 +131,25 @@
         scratch_shapes=[pltpu.VMEM((rows, cols // hid), jnp.float32)],
         compiler_params=pltpu.CompilerParams(vmem_limit_bytes=ROUTES_BYTES),
         cost_estimate=pl.CostEstimate(
-            flops=6 * rows * width * cols // DECLARED,
-            bytes_accessed=2 * (2 * rows * width + 3 * width * cols) // DECLARED,
+            flops=6 * rows * width * cols // declared,
+            bytes_accessed=2 * (2 * rows * width + 3 * width * cols) // declared,
             transcendentals=0,
         ),
         name="routes_pass",
     )(mine, *blocks, wgu, wgu, wd)
 
 
-def out_kernel(pieces, token_ref, *refs):
-    made, (wd, wgu), outs = refs[: 4 * pieces], refs[4 * pieces : 4 * pieces + 2], refs[4 * pieces + 2 :]
+def out_kernel(sections, token_ref, *refs):
+    made, (wd, wgu), outs = refs[: 4 * sections], refs[4 * sections : 4 * sections + 2], refs[4 * sections + 2 :]
     j, steps = pl.program_id(0), (pl.num_programs(0) - 1) // 2
-    tile = wd.shape[1]
     cols = wd.shape[0]
 
     def put(p, value):
-        half = value.shape[0] // 2
-        outs[2 * p][:, : value.shape[1]] = value[:half].astype(jnp.bfloat16)
-        outs[2 * p + 1][:, : value.shape[1]] = value[half:].astype(jnp.bfloat16)
-
-    for p in range(pieces):
+        half, tile = value.shape[0] // 2, value.shape[1]
+        outs[2 * p][:, :tile] = value[:half].astype(jnp.bfloat16)
+        outs[2 * p + 1][:, :tile] = value[half:].astype(jnp.bfloat16)
+
+    for p in range(sections):
         hw, dg, du, extra = made[4 * p : 4 * p + 4]
 
         @pl.when(j < steps)
@@ -224,20 +176,24 @@
             put(p, extra[...])
 
 
-def out_pass(made, wgu, wd, token):
+def out_pass(sections, wgu, wd, token):
     cols, width = wd.shape
     tile = 512 if width % 512 == 0 else 128
-    steps, wide = width // tile, 2 * width + made[0][3].shape[1]
-    flat = [value for each in made for value in each]
-    outs = []
-    for each in made:
-        outs += [jax.ShapeDtypeStruct((each[0].shape[0] // 2, wide), jnp.bfloat16)] * 2
-    rows = sum(each[0].shape[0] for each in made)
+    steps, wide = width // tile, 2 * width + sections[0][0][3].shape[1]
+    flat, specs, outs = [], [], []
+    for values, rows in sections:
+        flat += values
+        specs += [
+            pl.BlockSpec((rows, v.shape[1]), lambda j: (0, 0), pipeline_mode=pl.Buffered(1))
+            for v in values
+        ]
+        outs += [jax.ShapeDtypeStruct((rows // 2, wide), jnp.bfloat16)] * 2
+    total = sum(rows for _, rows in sections)
     got = pl.pallas_call(
-        functools.partial(out_kernel, len(made)),
+        functools.partial(out_kernel, len(sections)),
         grid=(2 * steps + 1,),
         in_specs=[pl.BlockSpec(memory_space=pltpu.SMEM)]
-        + [pl.BlockSpec(v.shape, lambda j: (0, 0), pipeline_mode=pl.Buffered(1)) for v in flat]
+        + specs
         + [
             pl.BlockSpec((cols, tile), lambda j: (0, jnp.minimum(j, steps - 1))),
             pl.BlockSpec((tile, 2 * cols), lambda j: (jnp.clip(j - steps, 0, steps - 1), 0)),
@@ -246,8 +202,8 @@
         out_shape=outs,
         compiler_params=pltpu.CompilerParams(vmem_limit_bytes=OUT_BYTES),
         cost_estimate=pl.CostEstimate(
-            flops=(6 * rows * width * cols) // DECLARED,
-            bytes_accessed=2 * (2 * rows * width + 3 * width * cols) // DECLARED,
+            flops=6 * total * width * cols // DECLARED,
+            bytes_accessed=2 * (2 * total * width + 3 * width * cols) // DECLARED,
             transcendentals=0,
         ),
         name="out_pass",
@@ -255,9 +211,10 @@
     return list(got)
 
 
-def grad_kernel(sources, parts, block_ref, *refs):
-    srcs, rhss, refs = refs[:sources], refs[sources : sources + parts], refs[sources + parts :]
-    j, out_ref, turned = pl.program_id(0), refs[-2], refs[-1]
+def grad_kernel(sources, sets, parts, exp_dev, given, block_ref, *refs):
+    srcs, refs = refs[:sources], refs[sources:]
+    rhss, refs = [refs[t * parts : (t + 1) * parts] for t in range(sets)], refs[sets * parts :]
+    j, gots, outs, turned = pl.program_id(0), refs[:given], refs[given:-1], refs[-1]
 
     @pl.when(j == 0)
     def _():
@@ -266,38 +223,62 @@
             turned[:, at : at + src.shape[0]] = src[...].T
             at += src.shape[0]
 
-    rhs = jnp.concatenate([ref[...] for ref in rhss], 0)
-    total = jnp.dot(turned[...], rhs, preferred_element_type=jnp.float32)
-    if len(refs) == 2:
-        out_ref[...] = total.astype(out_ref.dtype)
-    else:
-        total = total + refs[0][...].astype(jnp.float32)
-        for e in range(out_ref.shape[1]):
-
-            @pl.when(j == e)
-            def _():
-                out_ref[:, e, :] = total
-
-
-def grad_pass(srcs, rhss, block, own, hid, name, first=0, exp_dev=None, got=None):
-    rows, cols = sum(src.shape[0] for src in srcs), exp_dev * hid
+    for t in range(sets):
+
+        @pl.when((j >= t * exp_dev) & (j < (t + 1) * exp_dev))
+        def _():
+            rhs = jnp.concatenate([ref[...] for ref in rhss[t]], 0)
+            total = jnp.dot(turned[...], rhs, preferred_element_type=jnp.float32)
+            if not gots:
+                if len(outs) == 1:
+                    outs[0][...] = total.astype(jnp.bfloat16)
+                for n, out in enumerate(outs if len(outs) > 1 else []):
+
+                    @pl.when(j == n)
+                    def _():
+                        out[...] = total.astype(jnp.bfloat16)
+
+                return
+            for e in range(exp_dev):
+
+                @pl.when(j == t * exp_dev + e)
+                def _():
+                    outs[t][:, e, :] = total + gots[e % given][...].astype(jnp.float32)
+
+
+def grad_pass(srcs, sets, block, own, exp_dev, name, got=(), apart=False):
+    rows, hid = sum(src.shape[0] for src in srcs), sets[0][0].shape[1] // exp_dev
+    cols = len(sets) * exp_dev * hid
     in_specs = [pl.BlockSpec((src.shape[0], own), lambda j, b: (0, b[0])) for src in srcs]
-    in_specs += [pl.BlockSpec((rhs.shape[0], hid), lambda j, b: (0, first + j)) for rhs in rhss]
-    out_spec = pl.BlockSpec((own, hid), lambda j, b: (0, j))
-    out_shape = jax.ShapeDtypeStruct((own, cols), jnp.bfloat16)
-    operands = [*srcs, *rhss]
-    if got is not None:
-        in_specs.append(out_spec)
-        operands.append(got)
-        out_spec = pl.BlockSpec((own, exp_dev, hid), lambda j, b: (0, 0, 0))
-        out_shape = jax.ShapeDtypeStruct((own, exp_dev, hid), jnp.float32)
+    for t, rhss in enumerate(sets):
+        in_specs += [
+            pl.BlockSpec(
+                (rhs.shape[0], hid),
+                functools.partial(
+                    lambda first, j, b: (0, jnp.clip(j - first, 0, exp_dev - 1)), t * exp_dev
+                ),
+            )
+            for rhs in rhss
+        ]
+    out_specs = [pl.BlockSpec((own, hid), lambda j, b: (0, j))]
+    out_shape = [jax.ShapeDtypeStruct((own, cols), jnp.bfloat16)]
+    operands = [*srcs, *(rhs for rhss in sets for rhs in rhss)]
+    if apart:
+        out_specs = [pl.BlockSpec((own, hid), lambda j, b: (0, 0))] * (cols // hid)
+        out_shape = [jax.ShapeDtypeStruct((own, hid), jnp.bfloat16)] * (cols // hid)
+    if got:
+        apart_spec = pl.BlockSpec((own, hid), lambda j, b: (0, 0))
+        in_specs += out_specs if len(got) == 1 else [apart_spec] * len(got)
+        operands += got
+        out_specs = [pl.BlockSpec((own, exp_dev, hid), lambda j, b: (0, 0, 0))] * len(sets)
+        out_shape = [jax.ShapeDtypeStruct((own, exp_dev, hid), jnp.float32)] * len(sets)
     return pl.pallas_call(
-        functools.partial(grad_kernel, len(srcs), len(rhss)),
+        functools.partial(grad_kernel, len(srcs), len(sets), len(sets[0]), exp_dev, len(got)),
         grid_spec=pltpu.PrefetchScalarGridSpec(
             num_scalar_prefetch=1,
-            grid=(exp_dev,),
+            grid=(len(sets) * exp_dev,),
             in_specs=in_specs,
-            out_specs=out_spec,
+            out_specs=out_specs,
             scratch_shapes=[pltpu.VMEM((own, rows), jnp.bfloat16)],
         ),
         out_shape=out_shape,
@@ -311,26 +292,27 @@
     )(block, *operands)
 
 
-def sum_kernel(keep_ref, got_ref, out_ref):
-    total = keep_ref[...].astype(jnp.float32) + got_ref[...].astype(jnp.float32)
+def sum_kernel(keep_ref, *refs):
+    gots, out_ref = refs[:-1], refs[-1]
     hid = out_ref.shape[2]
-    for e in range(out_ref.shape[1]):
-        out_ref[:, e, :] = total[:, e * hid : (e + 1) * hid]
-
-
-def sum_pass(keep, got, exp_dev):
+    for e, got_ref in enumerate(gots):
+        keep = keep_ref[:, e * hid : (e + 1) * hid].astype(jnp.float32)
+        out_ref[:, e, :] = keep + got_ref[...].astype(jnp.float32)
+
+
+def sum_pass(keep, gots):
     rows, cols = keep.shape
-    tile = min(128, rows)
-    block = pl.BlockSpec((tile, cols), lambda i: (i, 0))
+    tile, hid = min(128, rows), cols // len(gots)
     return pl.pallas_call(
         sum_kernel,
         grid=(rows // tile,),
-        in_specs=[block, block],
-        out_specs=pl.BlockSpec((tile, exp_dev, cols // exp_dev), lambda i: (i, 0, 0)),
-        out_shape=jax.ShapeDtypeStruct((rows, exp_dev, cols // exp_dev), jnp.float32),
+        in_specs=[pl.BlockSpec((tile, cols), lambda i: (i, 0))]
+        + [pl.BlockSpec((tile, hid), lambda i: (i, 0))] * len(gots),
+        out_specs=pl.BlockSpec((tile, len(gots), hid), lambda i: (i, 0, 0)),
+        out_shape=jax.ShapeDtypeStruct((rows, len(gots), hid), jnp.float32),
         compiler_params=pltpu.CompilerParams(vmem_limit_bytes=SUM_BYTES),
         name="sum_pass",
-    )(keep, got)
+    )(keep, *gots)
 
 
 def dense_form(tokens, routes, route_weights, cotangent, gate_proj, up_proj, down_proj):
@@ -357,48 +339,86 @@
     )
     wd = down_proj.reshape(cols, width)
 
-    def work(blocks, with_rwg):
-        return list(routes_pass(blocks, mine, wgu, wd, hid, experts, with_rwg))
-
-    halves = [xc[: tok_dev // 2], xc[tok_dev // 2 :]]
-    pieces, made = gather_planes(halves, list(range(0, n_dp, 2)), work)
-    arrived = [block for piece in pieces for block in piece]
-    hws, dgs, dus = [[values[n] for values in made] for n in range(3)]
-    own_made = made[: len(way_bits("expert"))]
+    def work(groups, with_rwg, **kwargs):
+        return list(routes_pass(groups, mine, wgu, wd, hid, experts, with_rwg, **kwargs))
+
+    def across(*blocks):
+        return [swap(block, "expert", 1) for block in blocks]
+
+    half = tok_dev // 2
+    by_x, by_y = 2, 4
+    mate = swap(xc, "dp", 2)
+    near_x, near_y = together([swap(xc, "expert", by_x), swap(xc, "expert", by_y)])
+    near = [xc, near_x, near_y]
+    first = near + across(*near)
+    corner = [swap(near_x[:half], "expert", by_y), swap(near_y[half:], "expert", by_x)]
+    made = work([first[:2], first[2:4], first[4:]], True)
+    corner_x, corner_y, mate, *first_made = together([*corner, mate, *made])
+    corner = [corner_x, corner_y]
+    second = corner + across(*corner) + [mate] + across(mate)
+    made = work([second[:4], second[4:]], True)
+    far_x, far_y, *second_made = together(
+        [swap(mate, "expert", by_x), swap(mate, "expert", by_y), *made]
+    )
+    third = [far_x, far_y] + across(far_x, far_y)
+    corner = [swap(far_x[:half], "expert", by_y), swap(far_y[half:], "expert", by_x)]
+    made = work([third[:2], third[2:]], False)
+    corner_x, corner_y, *third_made = together([*corner, *made])
+    fourth = [corner_x, corner_y] + across(corner_x, corner_y)
+    fourth_made = work([fourth], False)
+    arrived = first + second + third + fourth
+    units = [first_made, second_made, third_made, fourth_made]
+    hws, dgs, dus = [[values[n] for values in units] for n in range(3)]
     mates, token = (here ^ 1).reshape(1).astype(jnp.int32), here.reshape(1).astype(jnp.int32)
 
-    def grad(rhss, block, of_cot, name, first=0, count=exp_dev, got=None):
+    def grad(sets, block, of_cot, name, got=(), apart=False):
         block = block + (n_dp if of_cot else 0)
-        return grad_pass(arrived, rhss, block, own, hid, name, first, count, got)
-
-    gate_send, mates = together([grad(dgs, mates, False, "gate_send"), mates])
-    up_send, after = together([grad(dus, mates, False, "up_send"), mates])
-    gate_got, up_send, mates, token, *shares = together(
-        [swap(gate_send, "dp", 1), up_send, after, token] + out_pass(own_made, wgu, wd, after)
-    )
-    chip = [add_to(k, swap(v, "expert", 1)) for k, v in zip(shares[::2], shares[1::2])]
-    down_send = grad(hws, mates, True, "down_send")
-    *chip[-1:], token, down_send = together([chip[-1], token, down_send])
-    sides = [[p[: p.shape[0] // 2] for p in chip], [p[p.shape[0] // 2 :] for p in chip]]
-    gate_grad = grad(dgs, token, False, "gate_grad", got=gate_got)
-    beside = [swap(up_send, "dp", 1), down_send, gate_grad, token]
-    rounds = list(enumerate(way_bits("expert")))[::-1]
-    for s, bits in rounds[:-1]:
-        sides, beside = scatter_round(sides, s, bits, beside)
-    up_got, down_send, gate_grad, token = beside
-    down_got = swap(down_send, "dp", 1)
-    up_grad = grad(dus, token, False, "up_grad", got=up_got)
-    down_keep = grad(hws, token, True, "down_keep")
-    sides, (down_got, up_grad, down_keep) = scatter_round(
-        sides, *rounds[-1], [down_got, up_grad, down_keep]
-    )
-    summed = join([sides[0][0], sides[1][0]])
-    grads = [gate_grad, up_grad, sum_pass(down_keep, down_got, exp_dev)]
-
-    tail = summed[:, 2 * width :].astype(jnp.float32)
+        return grad_pass(arrived, sets, block, own, exp_dev, name, got, apart)
+
+    gate_send, mates = together([*grad([dgs], mates, False, "gate_send"), mates])
+    *up_send, after = together([*grad([dus], mates, False, "up_send", apart=True), mates])
+    shares = out_pass([(first_made, 6 * tok_dev), (second_made, 2 * tok_dev)], wgu, wd, after)
+    *shares, mates = together([*shares, after])
+    down_send = grad([hws], mates, True, "down_send", apart=True)
+    *values, up_last, gate_got, token = together(
+        [*shares, *down_send, *(swap(send, "dp", 1) for send in up_send[:-1])]
+        + [up_send[-1], swap(gate_send, "dp", 1), token]
+    )
+    shares, down_send, up_got = values[:4], values[4 : 4 + exp_dev], values[4 + exp_dev :]
+    corner = add_to(shares[2], *across(shares[3]))
+    chip = add_to(shares[0], *across(shares[1]))
+    corner, token = together([corner, token])
+    (down_keep,) = grad([hws], token, True, "down_keep")
+    to_x, to_y, up_last, chip, down_keep, token, *down_send = together(
+        [
+            swap(corner[:half], "expert", by_y),
+            swap(corner[half:], "expert", by_x),
+            swap(up_last, "dp", 1),
+            chip,
+            down_keep,
+            token,
+            *down_send,
+        ]
+    )
+    *down_got, last_got = [swap(send, "dp", 1) for send in down_send]
+    mine_too, of_x, of_y = chip[:tok_dev], chip[tok_dev : 2 * tok_dev], chip[2 * tok_dev :]
+    of_x = join([add_to(of_x[:half], to_x), of_x[half:]])
+    of_y = join([of_y[:half], add_to(of_y[half:], to_y)])
+    (gate_grad,) = grad([dgs], token, False, "gate_grad", got=[gate_got])
+    (up_grad,) = grad([dus], token, False, "up_grad", got=[*up_got, up_last])
+    from_x, from_y, gate_grad, up_grad, *down_got = together(
+        [swap(of_x, "expert", by_x), swap(of_y, "expert", by_y), gate_grad, up_grad, *down_got]
+    )
+    summed = sum(v.astype(jnp.float32) for v in (mine_too, from_x, from_y))
+    tail = summed[:, 2 * width :]
     rwg_dense = tail[:, :experts] + tail[:, experts : 2 * experts]
     route_weight_grad = jnp.sum(jnp.where(named, rwg_dense[:, None, :], 0.0), axis=2)
-    return (summed[:, :width], summed[:, width : 2 * width], route_weight_grad, *grads)
+    summed = summed[:, : 2 * width].astype(jnp.bfloat16)
+    layer_output, input_grad, route_weight_grad, last_got = together(
+        [summed[:, :width], summed[:, width:], route_weight_grad, last_got]
+    )
+    grads = [gate_grad, up_grad, sum_pass(down_keep, [*down_got, last_got])]
+    return (layer_output, input_grad, route_weight_grad, *grads)
 
 
 def swish_parts(gate_pre):
@@ -504,8 +524,10 @@
 
 
 def on_device(tokens, routes, route_weights, cotangent, gate_proj, up_proj, down_proj):
-    experts = gate_proj.shape[0] * lax.axis_size("expert")
-    form = dense_form if experts <= 2 * routes.shape[1] else slots_form
+    groups = lax.axis_size("expert")
+    few = gate_proj.shape[0] * groups <= 2 * routes.shape[1]
+    square = groups == 2 * 2 * 2 and lax.axis_size("dp") == 2 * 2
+    form = dense_form if few and square else slots_form
     return form(tokens, routes, route_weights, cotangent, gate_proj, up_proj, down_proj)
 
 

time: 245 us -> 234 us (0.955)
  waiting for transfers between devices: 44.4 us -> 35.9 us
  Pallas kernels: 137 us -> 144 us
  local copies, waits for them, and re-layouts: 20.7 us -> 16.2 us
  other arithmetic: 17 us -> 12.6 us
    ppermute x23 -> x30, waiting for transfers between devices: 44.4 us -> 35.9 us  [swap(): lax.ppermute(value, axis, [(i, i ^ mask) for i in range(lax.axis_size(axi...]
    pallas_call x12, Pallas kernels: 137 us -> 144 us  [the longest x4 61.3 us: routes_pass(): pl.pallas_call(functools.partial(routes_kernel, counts, hid, experts, wit...]
    unnamed x27 -> x42, local copies, waits for them, and re-layouts: 9.51 us -> 3.75 us
    concatenate x6 -> x2, other arithmetic: 6.72 us -> 1.13 us  [join(): return parts[0] if len(parts) == 1 else jnp.concatenate(parts, 0)]
    slice x4 -> x7, local copies, waits for them, and re-layouts: 1.67 us -> 5.23 us  [the longest x1 2.28 us: dense_form(): summed[:, width:]]
    ppermute x23 -> x30, starting transfers between devices: 24.7 us -> 24.7 us  [swap(): lax.ppermute(value, axis, [(i, i ^ mask) for i in range(lax.axis_size(axi...]
  transfers between devices with their start and end apart: 23 -> 30, of which waited for: 10 -> 15; matrix products, arithmetic and copies ran while one was open for 12% -> 9% of each run, Pallas kernels for 46% -> 52%
where the time goes in v3:
time: 234 us
  Pallas kernels  144 us (62%)
  waiting for transfers between devices  35.9 us (15%)
  starting transfers between devices  24.7 us (11%)
  local copies, waits for them, and re-layouts  16.2 us (7%)
  other arithmetic  12.6 us (5%)
    pallas_call x4, Pallas kernels, routes_pass(): pl.pallas_call(functools.partial(routes_kernel, counts, hid, experts, wit...  61.3 us
    pallas_call x6, Pallas kernels, grad_pass(): pl.pallas_call(functools.partial(grad_kernel, len(srcs), len(sets), len(s...  54.5 us
    ppermute x30, waiting for transfers between devices, swap(): lax.ppermute(value, axis, [(i, i ^ mask) for i in range(lax.axis_size(axi...  35.9 us
    pallas_call x1, Pallas kernels, out_pass(): pl.pallas_call(functools.partial(out_kernel, len(sections)), grid=(2 * st...  25.6 us
    ppermute x30, starting transfers between devices, swap(): lax.ppermute(value, axis, [(i, i ^ mask) for i in range(lax.axis_size(axi...  24.7 us
    concatenate x1, other arithmetic, dense_form(): jnp.concatenate([gate_proj[e] for e in range(exp_dev)] + [up_proj[e] for...  5.54 us
  transfers between devices with their start and end apart: 30, of which 15 were waited for; matrix products, arithmetic and copies ran while one was open for 9% of the time, Pallas kernels for 52%

profile of v3, /device:TPU:0, one launch (start us, length us, event | category | flops | bytes accessed | tf_op | source)
XLA Modules:
  0.0 234.0 jit_solution(14602708714529611760)
XLA Ops:
  1.7 2.3 concatenate.12.refs_0_
  4.1 3.0 %collective-permute-start.1 = (bf16[128,4224]{1,0:T(8,128)(2,1)S(1)}, bf16[128,4224]{1,0:T(8,128)(2,1)S(1)}, u32[]{:S(2)}, u32[]{:S(2)}) collective-permute-start(bf16[128,4224]{1,0:T(8,128)(2,1)S(1)} %concatenate.12.refs_0_), channel_id=1, source_target_pairs={{0,4},{1,5},{2,6},{3,7},{4,0},{5,1},{6,2},{7,3},{8,12},{9,13},{10,... | collective-permute-start | bytes 3244040 | tf_op jit(solution)/shard_map/ppermute | solution.py:16
  7.1 1.5 collective-permute-start
  8.6 2.6 %collective-permute-start.7 = (bf16[128,4224]{1,0:T(8,128)(2,1)S(1)}, bf16[128,4224]{1,0:T(8,128)(2,1)}, u32[]{:S(2)}, u32[]{:S(2)}) collective-permute-start(bf16[128,4224]{1,0:T(8,128)(2,1)S(1)} %concatenate.12.refs_0_), channel_id=1, source_target_pairs={{0,16},{8,24},{16,0},{24,8},{1,17},{9,25},{17,1},{25,9},{2,18},{10... | collective-permute-start | bytes 3244040 | tf_op jit(solution)/shard_map/ppermute | solution.py:16
  11.2 4.5 %slice_bitcast_fusion.1 = (bf16[2048,640]{1,0:T(8,128)(2,1)S(1)}, bf16[2048,640]{1,0:T(8,128)(2,1)S(1)}, bf16[2048,640]{1,0:T(8,128)(2,1)S(1)}, bf16[2048,640]{1,0:T(8,128)(2,1)S(1)}) fusion(bf16[2,2048,640]{2,1,0:T(8,128)(2,1)} %param.12, bf16[2,2048,640]{2,1,0:T(8,128)(2,1)} %param.11), kind=kLoop, calls=%fused_computation.3 | loop fusion | bytes 20971520 | tf_op jit(solution)/shard_map/squeeze | solution.py:338
  15.7 15.3 %collective-permute-done.1.refs_2_ = bf16[128,4224]{1,0:T(8,128)(2,1)S(1)} collective-permute-done((bf16[128,4224]{1,0:T(8,128)(2,1)S(1)}, bf16[128,4224]{1,0:T(8,128)(2,1)S(1)}, u32[]{:S(2)}, u32[]{:S(2)}) %collective-permute-start.1) | collective-permute-done | bytes 1081376 | tf_op jit(solution)/shard_map/ppermute | solution.py:16
  31.0 1.5 collective-permute-done.refs_1_
  32.4 0.9 slice.70
  33.3 0.8 slice.71
  34.7 1.5 collective-permute-start.6
  36.8 5.5 %pad_maximum_fusion.refs_6_.refs_7_.refs_4_.refs_5_.refs_9_ = bf16[2048,2560]{1,0:T(8,128)(2,1)} fusion(bf16[2048,640]{1,0:T(8,128)(2,1)S(1)} %get-tuple-element.173, bf16[2048,640]{1,0:T(8,128)(2,1)S(1)} %get-tuple-element.172, bf16[2048,640]{1,0:T(8,128)(2,1)S(1)} %get-tuple-element.184, bf16[2048,640]{1,0:T(8,128)(2,1)S(1)} %get-tuple-element.185), kind=kLoop, calls=%fused_computation | loop fusion | flops 41943040 | bytes 20971520 | tf_op jit(solution)/shard_map/concatenate | solution.py:337
  42.4 20.6 %routes_pass.4 = (bf16[768,1280]{1,0:T(8,128)(2,1)}, bf16[768,1280]{1,0:T(8,128)(2,1)}, bf16[768,1280]{1,0:T(8,128)(2,1)}, bf16[768,128]{1,0:T(8,128)(2,1)}) custom-call(s32[1]{0:T(128)} %bitcast.1.mine_ref, bf16[128,4224]{1,0:T(8,128)(2,1)} %copy-done.1, bf16[128,4224]{1,0:T(8,128)(2,1)} %copy-done.3, bf16[128,4224]{1,0:T(8,128)(2,1)} %copy-done.2, ...), custom_call_target="tpu_custom_call" | custom-call | flops 11520 | bytes 21 | tf_op jit(solution)/shard_map/routes_pass/pallas_call | solution.py:117
  63.2 1.4 collective-permute-start.12
  65.6 1.6 collective-permute-done.8.refs_2_.refs_8_
  68.1 0.8 copy-done.11
  68.9 1.0 copy-done.7
  69.8 15.3 %routes_pass.5 = (bf16[512,1280]{1,0:T(8,128)(2,1)}, bf16[512,1280]{1,0:T(8,128)(2,1)}, bf16[512,1280]{1,0:T(8,128)(2,1)}, bf16[512,128]{1,0:T(8,128)(2,1)}) custom-call(s32[1]{0:T(128)} %bitcast.1.mine_ref, bf16[64,4224]{1,0:T(8,128)(2,1)} %collective-permute-done.5.refs_0_.refs_6_, bf16[64,4224]{1,0:T(8,128)(2,1)} %collective-permute-done.6.refs_1_.refs_7_, ...), custom_call_target="tpu_custom_call" | custom-call | flops 7680 | bytes 19 | tf_op jit(solution)/shard_map/routes_pass/pallas_call | solution.py:117
  85.1 4.6 %collective-permute-done.12.refs_1_.refs_13_ = bf16[128,4224]{1,0:T(8,128)(2,1)S(1)} collective-permute-done((bf16[128,4224]{1,0:T(8,128)(2,1)}, bf16[128,4224]{1,0:T(8,128)(2,1)S(1)}, u32[]{:S(2)}, u32[]{:S(2)}) %collective-permute-start.12) | collective-permute-done | bytes 1081376 | tf_op jit(solution)/shard_map/ppermute | solution.py:16
  89.7 1.1 collective-permute-done.11.refs_0_.refs_12_
  92.4 1.0 collective-permute-done.13.refs_2_.refs_14_
  93.4 1.5 collective-permute-done.14.refs_3_.refs_15_
  95.0 1.0 copy-done.9
  96.0 14.4 %routes_pass.6 = (bf16[512,1280]{1,0:T(8,128)(2,1)}, bf16[512,1280]{1,0:T(8,128)(2,1)}, bf16[512,1280]{1,0:T(8,128)(2,1)}) custom-call(s32[1]{0:T(128)} %bitcast.1.mine_ref, bf16[128,4224]{1,0:T(8,128)(2,1)} %copy-done.5, bf16[128,4224]{1,0:T(8,128)(2,1)} %copy-done.4, bf16[128,4224]{1,0:T(8,128)(2,1)} %copy-done.8, bf16[128,4224]{1,0:T(8,128)(2,1)} %copy-done.9, ...), custom_call_target="tpu_custom_call" | custom-call | flops 7680 | bytes 19 | tf_op jit(solution)/shard_map/routes_pass/pallas_call | solution.py:117
  111.1 1.6 collective-permute-done.17.refs_2_.refs_18_
  113.5 0.8 copy-done.13
  114.3 11.0 %routes_pass.7 = (bf16[256,1280]{1,0:T(8,128)(2,1)}, bf16[256,1280]{1,0:T(8,128)(2,1)}, bf16[256,1280]{1,0:T(8,128)(2,1)}) custom-call(s32[1]{0:T(128)} %bitcast.1.mine_ref, bf16[64,4224]{1,0:T(8,128)(2,1)} %collective-permute-done.15.refs_0_.refs_16_, bf16[64,4224]{1,0:T(8,128)(2,1)} %collective-permute-done.16.refs_1_.refs_17_, ...), custom_call_target="tpu_custom_call" | custom-call | flops 3840 | bytes 17 | tf_op jit(solution)/shard_map/routes_pass/pallas_call | solution.py:117
  125.3 8.5 %gate_send.1 = bf16[512,1280]{1,0:T(8,128)(2,1)} custom-call(s32[1]{0:T(128)} %bitcast.block_ref.token_ref, bf16[128,4224]{1,0:T(8,128)(2,1)} %copy-done.1, bf16[128,4224]{1,0:T(8,128)(2,1)} %copy-done.3, bf16[128,4224]{1,0:T(8,128)(2,1)} %copy-done.2, bf16[128,4224]{1,0:T(8,128)(2,1)} %copy-done.6, bf16[128,4224]{1,0:T(8,128)(2,1)} %collective-permute-done.3.refs_4_, ...), custom_call_target="tpu_custom_call" | custom-call | flops 2560 | bytes 8 | tf_op jit(solution)/shard_map/gate_send/pallas_call | solution.py:275
  133.8 1.7 collective-permute-start.20
  135.5 8.6 %up_send.1 = (bf16[512,640]{1,0:T(8,128)(2,1)}, bf16[512,640]{1,0:T(8,128)(2,1)}) custom-call(s32[1]{0:T(128)} %bitcast.block_ref.token_ref, bf16[128,4224]{1,0:T(8,128)(2,1)} %copy-done.1, bf16[128,4224]{1,0:T(8,128)(2,1)} %copy-done.3, bf16[128,4224]{1,0:T(8,128)(2,1)} %copy-done.2, bf16[128,4224]{1,0:T(8,128)(2,1)} %copy-done.6, ...), custom_call_target="tpu_custom_call" | custom-call | flops 2560 | bytes 8 | tf_op jit(solution)/shard_map/up_send/pallas_call | solution.py:275
  144.7 25.6 %out_pass.1 = (bf16[384,4224]{1,0:T(8,128)(2,1)}, bf16[384,4224]{1,0:T(8,128)(2,1)}, bf16[128,4224]{1,0:T(8,128)(2,1)}, bf16[128,4224]{1,0:T(8,128)(2,1)}) custom-call(s32[1]{0:T(128)} %bitcast.block_ref.token_ref, bf16[768,1280]{1,0:T(8,128)(2,1)} %get-tuple-element.119.refs_0_.refs_20_, bf16[768,1280]{1,0:T(8,128)(2,1)} %get-tuple-element.107.refs_20_.refs_1_, ...), custom_call_target="tpu_custom_call" | custom-call | flops 15360 | bytes 23 | tf_op jit(solution)/shard_map/out_pass/pallas_call | solution.py:192
  170.3 8.7 %down_send.1 = (bf16[512,640]{1,0:T(8,128)(2,1)}, bf16[512,640]{1,0:T(8,128)(2,1)}) custom-call(s32[1]{0:T(128)S(6)} %add.27.block_ref, bf16[128,4224]{1,0:T(8,128)(2,1)} %copy-done.1, bf16[128,4224]{1,0:T(8,128)(2,1)} %copy-done.3, bf16[128,4224]{1,0:T(8,128)(2,1)} %copy-done.2, bf16[128,4224]{1,0:T(8,128)(2,1)} %copy-done.6, ...), custom_call_target="tpu_custom_call" | custom-call | flops 2560 | bytes 8 | tf_op jit(solution)/shard_map/down_send/pallas_call | solution.py:275
  179.6 1.6 collective-permute-start.24
  181.2 1.4 collective-permute-done.21
  182.8 1.1 fusion.3
  184.4 0.9 collective-permute-start.22
  185.3 8.7 %down_keep.1.keep_ref = bf16[512,1280]{1,0:T(8,128)(2,1)} custom-call(s32[1]{0:T(128)S(6)} %add.30.block_ref, bf16[128,4224]{1,0:T(8,128)(2,1)} %copy-done.1, bf16[128,4224]{1,0:T(8,128)(2,1)} %copy-done.3, bf16[128,4224]{1,0:T(8,128)(2,1)} %copy-done.2, bf16[128,4224]{1,0:T(8,128)(2,1)} %copy-done.6, bf16[128,4224]{1,0:T(8,128)(2,1)} %collective-permute-done.3.refs_4_, ...), custom_call_target="tpu_custom_call" | custom-call | flops 2560 | bytes 8 | tf_op jit(solution)/shard_map/down_keep/pallas_call | solution.py:275
  194.0 2.7 %add_convert_fusion = bf16[384,4224]{1,0:T(8,128)(2,1)S(1)} fusion(bf16[384,4224]{1,0:T(8,128)(2,1)} %collective-permute-done.25, bf16[384,4224]{1,0:T(8,128)(2,1)S(1)} %copy-done.14), kind=kLoop, calls=%fused_computation.1 | loop fusion | flops 6488064 | bytes 9732096 | tf_op jit(solution)/shard_map/convert_element_type | solution.py:28
  196.7 1.7 collective-permute-done.23
  199.1 1.6 collective-permute-start.26
  200.7 1.1 pad_maximum_fusion.2
  202.4 1.6 collective-permute-start.28
  204.4 9.9 %gate_grad.1 = f32[512,2,640]{2,1,0:T(2,128)} custom-call(s32[1]{0:T(128)} %bitcast.7.block_ref, bf16[128,4224]{1,0:T(8,128)(2,1)} %copy-done.1, bf16[128,4224]{1,0:T(8,128)(2,1)} %copy-done.3, bf16[128,4224]{1,0:T(8,128)(2,1)} %copy-done.2, bf16[128,4224]{1,0:T(8,128)(2,1)} %copy-done.6, bf16[128,4224]{1,0:T(8,128)(2,1)} %collective-permute-done.3.refs_4_, ...), custom_call_target="tpu_custom_call" | custom-call | flops 2560 | bytes 8 | tf_op jit(solution)/shard_map/gate_grad/pallas_call | solution.py:275
  214.3 10.1 %up_grad.1 = f32[512,2,640]{2,1,0:T(2,128)} custom-call(s32[1]{0:T(128)} %bitcast.7.block_ref, bf16[128,4224]{1,0:T(8,128)(2,1)} %copy-done.1, bf16[128,4224]{1,0:T(8,128)(2,1)} %copy-done.3, bf16[128,4224]{1,0:T(8,128)(2,1)} %copy-done.2, bf16[128,4224]{1,0:T(8,128)(2,1)} %copy-done.6, bf16[128,4224]{1,0:T(8,128)(2,1)} %collective-permute-done.3.refs_4_, ...), custom_call_target="tpu_custom_call" | custom-call | flops 2560 | bytes 8 | tf_op jit(solution)/shard_map/up_grad/pallas_call | solution.py:275
  224.5 1.9 collective-permute-done.27
  226.4 1.4 fusion
  228.5 2.3 fusion.2
  230.8 0.9 collective-permute-done.29.refs_1_
  231.7 2.3 sum_pass.1
  (92 shorter events, 11.9 us)
Async XLA Ops:
  4.1 11.6 %copy-start.1 = (bf16[128,4224]{1,0:T(8,128)(2,1)}, bf16[128,4224]{1,0:T(8,128)(2,1)S(1)}, u32[]{:S(2)}) copy-start(bf16[128,4224]{1,0:T(8,128)(2,1)S(1)} %concatenate.12.refs_0_) | copy-start | bytes 3244036
  4.1 26.9 %collective-permute-start.1 = (bf16[128,4224]{1,0:T(8,128)(2,1)S(1)}, bf16[128,4224]{1,0:T(8,128)(2,1)S(1)}, u32[]{:S(2)}, u32[]{:S(2)}) collective-permute-start(bf16[128,4224]{1,0:T(8,128)(2,1)S(1)} %concatenate.12.refs_0_), channel_id=1, source_target_pairs={{0,4},{1,5},{2,6},{3,7},{4,0},{5,1},{6,2},{7,3},{8,12},{9,13},{10,... | collective-permute-start | bytes 3244040 | tf_op jit(solution)/shard_map/ppermute | solution.py:16
  7.1 25.3 %collective-permute-start = (bf16[128,4224]{1,0:T(8,128)(2,1)S(1)}, bf16[128,4224]{1,0:T(8,128)(2,1)S(1)}, u32[]{:S(2)}, u32[]{:S(2)}) collective-permute-start(bf16[128,4224]{1,0:T(8,128)(2,1)S(1)} %concatenate.12.refs_0_), channel_id=1, source_target_pairs={{0,2},{1,3},{2,0},{3,1},{4,6},{5,7},{6,4},{7,5},{8,10},{9,11},{10,... | collective-permute-start | bytes 3244040 | tf_op jit(solution)/shard_map/ppermute | solution.py:16
  8.6 27.6 %collective-permute-start.2 = (bf16[128,4224]{1,0:T(8,128)(2,1)S(1)}, bf16[128,4224]{1,0:T(8,128)(2,1)S(1)}, u32[]{:S(2)}, u32[]{:S(2)}) collective-permute-start(bf16[128,4224]{1,0:T(8,128)(2,1)S(1)} %concatenate.12.refs_0_), channel_id=1, source_target_pairs={{0,1},{1,0},{2,3},{3,2},{4,5},{5,4},{6,7},{7,6},{8,9},{9,8},{10,11... | collective-permute-start | bytes 3244040 | tf_op jit(solution)/shard_map/ppermute | solution.py:16
  8.6 54.5 %collective-permute-start.7 = (bf16[128,4224]{1,0:T(8,128)(2,1)S(1)}, bf16[128,4224]{1,0:T(8,128)(2,1)}, u32[]{:S(2)}, u32[]{:S(2)}) collective-permute-start(bf16[128,4224]{1,0:T(8,128)(2,1)S(1)} %concatenate.12.refs_0_), channel_id=1, source_target_pairs={{0,16},{8,24},{16,0},{24,8},{1,17},{9,25},{17,1},{25,9},{2,18},{10... | collective-permute-start | bytes 3244040 | tf_op jit(solution)/shard_map/ppermute | solution.py:16
  31.0 11.4 %copy-start.2 = (bf16[128,4224]{1,0:T(8,128)(2,1)}, bf16[128,4224]{1,0:T(8,128)(2,1)S(1)}, u32[]{:S(2)}) copy-start(bf16[128,4224]{1,0:T(8,128)(2,1)S(1)} %collective-permute-done.1.refs_2_) | copy-start | bytes 3244036
  32.4 10.0 %copy-start.3 = (bf16[128,4224]{1,0:T(8,128)(2,1)}, bf16[128,4224]{1,0:T(8,128)(2,1)S(1)}, u32[]{:S(2)}) copy-start(bf16[128,4224]{1,0:T(8,128)(2,1)S(1)} %collective-permute-done.refs_1_) | copy-start | bytes 3244036
  33.3 9.1 %collective-permute-start.3 = (bf16[128,4224]{1,0:T(8,128)(2,1)S(1)}, bf16[128,4224]{1,0:T(8,128)(2,1)}, u32[]{:S(2)}, u32[]{:S(2)}) collective-permute-start(bf16[128,4224]{1,0:T(8,128)(2,1)S(1)} %collective-permute-done.refs_1_), channel_id=1, source_target_pairs={{0,1},{1,0},{2,3},{3,2},{4,5},{5,4},{6,7},{7,6},{8,9},{9,8},{10,11... | collective-permute-start | bytes 3244040 | tf_op jit(solution)/shard_map/ppermute | solution.py:16
  34.1 8.3 %collective-permute-start.4 = (bf16[128,4224]{1,0:T(8,128)(2,1)S(1)}, bf16[128,4224]{1,0:T(8,128)(2,1)}, u32[]{:S(2)}, u32[]{:S(2)}) collective-permute-start(bf16[128,4224]{1,0:T(8,128)(2,1)S(1)} %collective-permute-done.1.refs_2_), channel_id=1, source_target_pairs={{0,1},{1,0},{2,3},{3,2},{4,5},{5,4},{6,7},{7,6},{8,9},{9,8},{10,11... | collective-permute-start | bytes 3244040 | tf_op jit(solution)/shard_map/ppermute | solution.py:16
  34.7 28.4 %collective-permute-start.6 = (bf16[64,4224]{1,0:T(8,128)(2,1)}, bf16[64,4224]{1,0:T(8,128)(2,1)}, u32[]{:S(2)}, u32[]{:S(2)}) collective-permute-start(bf16[64,4224]{1,0:T(8,128)(2,1)} %slice.71), channel_id=1, source_target_pairs={{0,2},{1,3},{2,0},{3,1},{4,6},{5,7},{6,4},{7,5},{8,10},{9,11},{10,... | collective-permute-start | bytes 1622024 | tf_op jit(solution)/shard_map/ppermute | solution.py:16
  36.1 6.2 %copy-start.6 = (bf16[128,4224]{1,0:T(8,128)(2,1)}, bf16[128,4224]{1,0:T(8,128)(2,1)S(1)}, u32[]{:S(2)}) copy-start(bf16[128,4224]{1,0:T(8,128)(2,1)S(1)} %collective-permute-done.2.refs_3_) | copy-start | bytes 3244036
  36.2 26.9 %collective-permute-start.5 = (bf16[64,4224]{1,0:T(8,128)(2,1)}, bf16[64,4224]{1,0:T(8,128)(2,1)}, u32[]{:S(2)}, u32[]{:S(2)}) collective-permute-start(bf16[64,4224]{1,0:T(8,128)(2,1)} %slice.70), channel_id=1, source_target_pairs={{0,4},{1,5},{2,6},{3,7},{4,0},{5,1},{6,2},{7,3},{8,12},{9,13},{10,... | collective-permute-start | bytes 1622024 | tf_op jit(solution)/shard_map/ppermute | solution.py:16
  63.1 5.0 %collective-permute-start.10 = (bf16[128,4224]{1,0:T(8,128)(2,1)}, bf16[128,4224]{1,0:T(8,128)(2,1)S(1)}, u32[]{:S(2)}, u32[]{:S(2)}) collective-permute-start(bf16[128,4224]{1,0:T(8,128)(2,1)} %collective-permute-done.7.refs_4_.refs_10_), channel_id=1, source_target_pairs={{0,1},{1,0},{2,3},{3,2},{4,5},{5,4},{6,7},{7,6},{8,9},{9,8},{10,11... | collective-permute-start | bytes 3244040 | tf_op jit(solution)/shard_map/ppermute | solution.py:16
  63.2 26.5 %collective-permute-start.12 = (bf16[128,4224]{1,0:T(8,128)(2,1)}, bf16[128,4224]{1,0:T(8,128)(2,1)S(1)}, u32[]{:S(2)}, u32[]{:S(2)}) collective-permute-start(bf16[128,4224]{1,0:T(8,128)(2,1)} %collective-permute-done.7.refs_4_.refs_10_), channel_id=1, source_target_pairs={{0,4},{1,5},{2,6},{3,7},{4,0},{5,1},{6,2},{7,3},{8,12},{9,13},{10,... | collective-permute-start | bytes 3244040 | tf_op jit(solution)/shard_map/ppermute | solution.py:16
  64.6 26.1 %collective-permute-start.11 = (bf16[128,4224]{1,0:T(8,128)(2,1)}, bf16[128,4224]{1,0:T(8,128)(2,1)S(1)}, u32[]{:S(2)}, u32[]{:S(2)}) collective-permute-start(bf16[128,4224]{1,0:T(8,128)(2,1)} %collective-permute-done.7.refs_4_.refs_10_), channel_id=1, source_target_pairs={{0,2},{1,3},{2,0},{3,1},{4,6},{5,7},{6,4},{7,5},{8,10},{9,11},{10,... | collective-permute-start | bytes 3244040 | tf_op jit(solution)/shard_map/ppermute | solution.py:16
  65.1 2.1 collective-permute-start.8
  65.1 2.9 %collective-permute-start.9 = (bf16[64,4224]{1,0:T(8,128)(2,1)}, bf16[64,4224]{1,0:T(8,128)(2,1)S(1)}, u32[]{:S(2)}, u32[]{:S(2)}) collective-permute-start(bf16[64,4224]{1,0:T(8,128)(2,1)} %collective-permute-done.6.refs_1_.refs_7_), channel_id=1, source_target_pairs={{0,1},{1,0},{2,3},{3,2},{4,5},{5,4},{6,7},{7,6},{8,9},{9,8},{10,11... | collective-permute-start | bytes 1622024 | tf_op jit(solution)/shard_map/ppermute | solution.py:16
  68.9 1.0 copy-start.7
  89.7 5.3 %copy-start.4 = (bf16[128,4224]{1,0:T(8,128)(2,1)}, bf16[128,4224]{1,0:T(8,128)(2,1)S(1)}, u32[]{:S(2)}) copy-start(bf16[128,4224]{1,0:T(8,128)(2,1)S(1)} %collective-permute-done.12.refs_1_.refs_13_) | copy-start | bytes 3244036
  90.7 4.3 %copy-start.5 = (bf16[128,4224]{1,0:T(8,128)(2,1)}, bf16[128,4224]{1,0:T(8,128)(2,1)S(1)}, u32[]{:S(2)}) copy-start(bf16[128,4224]{1,0:T(8,128)(2,1)S(1)} %collective-permute-done.11.refs_0_.refs_12_) | copy-start | bytes 3244036
  90.7 2.7 %collective-permute-start.13 = (bf16[128,4224]{1,0:T(8,128)(2,1)S(1)}, bf16[128,4224]{1,0:T(8,128)(2,1)S(1)}, u32[]{:S(2)}, u32[]{:S(2)}) collective-permute-start(bf16[128,4224]{1,0:T(8,128)(2,1)S(1)} %collective-permute-done.11.refs_0_.refs_12_), channel_id=1, source_target_pairs={{0,1},{1,0},{2,3},{3,2},{4,5},{5,4},{6,7},{7,6},{8,9},{9,8},{10,11... | collective-permute-start | bytes 3244040 | tf_op jit(solution)/shard_map/ppermute | solution.py:16
  90.7 4.3 %collective-permute-start.14 = (bf16[128,4224]{1,0:T(8,128)(2,1)S(1)}, bf16[128,4224]{1,0:T(8,128)(2,1)S(1)}, u32[]{:S(2)}, u32[]{:S(2)}) collective-permute-start(bf16[128,4224]{1,0:T(8,128)(2,1)S(1)} %collective-permute-done.12.refs_1_.refs_13_), channel_id=1, source_target_pairs={{0,1},{1,0},{2,3},{3,2},{4,5},{5,4},{6,7},{7,6},{8,9},{9,8},{10,11... | collective-permute-start | bytes 3244040 | tf_op jit(solution)/shard_map/ppermute | solution.py:16
  91.3 19.1 %collective-permute-start.16 = (bf16[64,4224]{1,0:T(8,128)(2,1)S(1)}, bf16[64,4224]{1,0:T(8,128)(2,1)}, u32[]{:S(2)}, u32[]{:S(2)}) collective-permute-start(bf16[64,4224]{1,0:T(8,128)(2,1)S(1)} %slice.77), channel_id=1, source_target_pairs={{0,2},{1,3},{2,0},{3,1},{4,6},{5,7},{6,4},{7,5},{8,10},{9,11},{10,... | collective-permute-start | bytes 1622024 | tf_op jit(solution)/shard_map/ppermute | solution.py:16
  91.9 18.6 %collective-permute-start.15 = (bf16[64,4224]{1,0:T(8,128)(2,1)S(1)}, bf16[64,4224]{1,0:T(8,128)(2,1)}, u32[]{:S(2)}, u32[]{:S(2)}) collective-permute-start(bf16[64,4224]{1,0:T(8,128)(2,1)S(1)} %slice.76), channel_id=1, source_target_pairs={{0,4},{1,5},{2,6},{3,7},{4,0},{5,1},{6,2},{7,3},{8,12},{9,13},{10,... | collective-permute-start | bytes 1622024 | tf_op jit(solution)/shard_map/ppermute | solution.py:16
  93.4 1.6 copy-start.8
  95.0 1.0 copy-start.9
  110.5 2.2 collective-permute-start.17
  110.7 2.8 %collective-permute-start.18 = (bf16[64,4224]{1,0:T(8,128)(2,1)}, bf16[64,4224]{1,0:T(8,128)(2,1)S(1)}, u32[]{:S(2)}, u32[]{:S(2)}) collective-permute-start(bf16[64,4224]{1,0:T(8,128)(2,1)} %collective-permute-done.16.refs_1_.refs_17_), channel_id=1, source_target_pairs={{0,1},{1,0},{2,3},{3,2},{4,5},{5,4},{6,7},{7,6},{8,9},{9,8},{10,11... | collective-permute-start | bytes 1622024 | tf_op jit(solution)/shard_map/ppermute | solution.py:16
  112.7 0.8 copy-start.12
  133.8 45.2 %collective-permute-start.20 = (bf16[512,1280]{1,0:T(8,128)(2,1)}, bf16[512,1280]{1,0:T(8,128)(2,1)S(1)}, u32[]{:S(2)}, u32[]{:S(2)}) collective-permute-start(bf16[512,1280]{1,0:T(8,128)(2,1)} %gate_send.1), channel_id=1, source_target_pairs={{0,8},{8,0},{16,24},{24,16},{1,9},{9,1},{17,25},{25,17},{2,10},{10... | collective-permute-start | bytes 3932168 | tf_op jit(solution)/shard_map/ppermute | solution.py:16
  144.0 34.9 %collective-permute-start.19 = (bf16[512,640]{1,0:T(8,128)(2,1)}, bf16[512,640]{1,0:T(8,128)(2,1)S(1)}, u32[]{:S(2)}, u32[]{:S(2)}) collective-permute-start(bf16[512,640]{1,0:T(8,128)(2,1)} %get-tuple-element.136), channel_id=1, source_target_pairs={{0,8},{8,0},{16,24},{24,16},{1,9},{9,1},{17,25},{25,17},{2,10},{10... | collective-permute-start | bytes 1966088 | tf_op jit(solution)/shard_map/ppermute | solution.py:16
  170.2 8.8 %copy-start.20 = (bf16[128,4224]{1,0:T(8,128)(2,1)S(1)}, bf16[128,4224]{1,0:T(8,128)(2,1)}, u32[]{:S(2)}) copy-start(bf16[128,4224]{1,0:T(8,128)(2,1)} %get-tuple-element.140) | copy-start | bytes 3244036
  170.3 12.3 %copy-start.16 = (bf16[128,4224]{1,0:T(8,128)(2,1)S(1)}, bf16[128,4224]{1,0:T(8,128)(2,1)}, u32[]{:S(2)}) copy-start(bf16[128,4224]{1,0:T(8,128)(2,1)} %get-tuple-element.139) | copy-start | bytes 3244036
  179.0 4.9 %copy-start.17 = (bf16[512,640]{1,0:T(8,128)(2,1)}, bf16[512,640]{1,0:T(8,128)(2,1)S(1)}, u32[]{:S(2)}) copy-start(bf16[512,640]{1,0:T(8,128)(2,1)S(1)} %collective-permute-done.19.refs_24_) | copy-start | bytes 1966084
  179.0 4.9 %copy-start.15 = (bf16[512,1280]{1,0:T(8,128)(2,1)}, bf16[512,1280]{1,0:T(8,128)(2,1)S(1)}, u32[]{:S(2)}) copy-start(bf16[512,1280]{1,0:T(8,128)(2,1)S(1)} %collective-permute-done.20.refs_24_) | copy-start | bytes 3932164
  179.0 3.5 %collective-permute-start.21 = (bf16[128,4224]{1,0:T(8,128)(2,1)S(1)}, bf16[128,4224]{1,0:T(8,128)(2,1)S(1)}, u32[]{:S(2)}, u32[]{:S(2)}) collective-permute-start(bf16[128,4224]{1,0:T(8,128)(2,1)S(1)} %copy-done.20), channel_id=1, source_target_pairs={{0,1},{1,0},{2,3},{3,2},{4,5},{5,4},{6,7},{7,6},{8,9},{9,8},{10,11... | collective-permute-start | bytes 3244040 | tf_op jit(solution)/shard_map/ppermute | solution.py:16
  179.1 14.9 %collective-permute-start.25 = (bf16[384,4224]{1,0:T(8,128)(2,1)}, bf16[384,4224]{1,0:T(8,128)(2,1)}, u32[]{:S(2)}, u32[]{:S(2)}) collective-permute-start(bf16[384,4224]{1,0:T(8,128)(2,1)} %get-tuple-element.145), channel_id=1, source_target_pairs={{0,1},{1,0},{2,3},{3,2},{4,5},{5,4},{6,7},{7,6},{8,9},{9,8},{10,11... | collective-permute-start | bytes 9732104 | tf_op jit(solution)/shard_map/ppermute | solution.py:16
  179.6 17.1 %collective-permute-start.24 = (bf16[512,640]{1,0:T(8,128)(2,1)}, bf16[512,640]{1,0:T(8,128)(2,1)S(1)}, u32[]{:S(2)}, u32[]{:S(2)}) collective-permute-start(bf16[512,640]{1,0:T(8,128)(2,1)} %get-tuple-element.143), channel_id=1, source_target_pairs={{0,8},{8,0},{16,24},{24,16},{1,9},{9,1},{17,25},{25,17},{2,10},{10... | collective-permute-start | bytes 1966088 | tf_op jit(solution)/shard_map/ppermute | solution.py:16
  183.9 14.5 %collective-permute-start.23 = (bf16[64,4224]{1,0:T(8,128)(2,1)}, bf16[64,4224]{1,0:T(8,128)(2,1)S(1)}, u32[]{:S(2)}, u32[]{:S(2)}) collective-permute-start(bf16[64,4224]{1,0:T(8,128)(2,1)} %get-tuple-element.180), channel_id=1, source_target_pairs={{0,2},{1,3},{2,0},{3,1},{4,6},{5,7},{6,4},{7,5},{8,10},{9,11},{10,... | collective-permute-start | bytes 1622024 | tf_op jit(solution)/shard_map/ppermute | solution.py:16
  184.4 14.2 %collective-permute-start.22 = (bf16[64,4224]{1,0:T(8,128)(2,1)}, bf16[64,4224]{1,0:T(8,128)(2,1)S(1)}, u32[]{:S(2)}, u32[]{:S(2)}) collective-permute-start(bf16[64,4224]{1,0:T(8,128)(2,1)} %get-tuple-element.181), channel_id=1, source_target_pairs={{0,4},{1,5},{2,6},{3,7},{4,0},{5,1},{6,2},{7,3},{8,12},{9,13},{10,... | collective-permute-start | bytes 1622024 | tf_op jit(solution)/shard_map/ppermute | solution.py:16
  185.3 8.7 %copy-start.14 = (bf16[384,4224]{1,0:T(8,128)(2,1)S(1)}, bf16[384,4224]{1,0:T(8,128)(2,1)}, u32[]{:S(2)}) copy-start(bf16[384,4224]{1,0:T(8,128)(2,1)} %get-tuple-element.144) | copy-start | bytes 9732100
  196.7 2.3 copy-start.18
  199.1 25.4 %collective-permute-start.26 = (bf16[128,4224]{1,0:T(8,128)(2,1)S(1)}, bf16[128,4224]{1,0:T(8,128)(2,1)S(1)}, u32[]{:S(2)}, u32[]{:S(2)}) collective-permute-start(bf16[128,4224]{1,0:T(8,128)(2,1)S(1)} %pad_maximum_fusion.1), channel_id=1, source_target_pairs={{0,2},{1,3},{2,0},{3,1},{4,6},{5,7},{6,4},{7,5},{8,10},{9,11},{10,... | collective-permute-start | bytes 3244040 | tf_op jit(solution)/shard_map/ppermute | solution.py:16
  201.7 24.7 %collective-permute-start.27 = (bf16[128,4224]{1,0:T(8,128)(2,1)}, bf16[128,4224]{1,0:T(8,128)(2,1)S(1)}, u32[]{:S(2)}, u32[]{:S(2)}) collective-permute-start(bf16[128,4224]{1,0:T(8,128)(2,1)} %pad_maximum_fusion.2), channel_id=1, source_target_pairs={{0,4},{1,5},{2,6},{3,7},{4,0},{5,1},{6,2},{7,3},{8,12},{9,13},{10,... | collective-permute-start | bytes 3244040 | tf_op jit(solution)/shard_map/ppermute | solution.py:16
  202.4 22.1 %collective-permute-start.28 = (bf16[512,640]{1,0:T(8,128)(2,1)}, bf16[512,640]{1,0:T(8,128)(2,1)S(1)}, u32[]{:S(2)}, u32[]{:S(2)}) collective-permute-start(bf16[512,640]{1,0:T(8,128)(2,1)} %get-tuple-element.156), channel_id=1, source_target_pairs={{0,8},{8,0},{16,24},{24,16},{1,9},{9,1},{17,25},{25,17},{2,10},{10... | collective-permute-start | bytes 1966088 | tf_op jit(solution)/shard_map/ppermute | solution.py:16
  203.9 27.8 %collective-permute-start.29 = (bf16[512,640]{1,0:T(8,128)(2,1)}, bf16[512,640]{1,0:T(8,128)(2,1)S(1)}, u32[]{:S(2)}, u32[]{:S(2)}) collective-permute-start(bf16[512,640]{1,0:T(8,128)(2,1)} %get-tuple-element.159), channel_id=1, source_target_pairs={{0,8},{8,0},{16,24},{24,16},{1,9},{9,1},{17,25},{25,17},{2,10},{10... | collective-permute-start | bytes 1966088 | tf_op jit(solution)/shard_map/ppermute | solution.py:16
  224.5 3.4 %copy-start.19 = (s32[128,8]{0,1:T(8,128)S(1)}, s32[128,8]{0,1:T(8,128)}, u32[]{:S(2)}) copy-start(s32[128,8]{0,1:T(8,128)} %param.8) | copy-start | bytes 12292
  227.8 3.9 %copy-start = (bf16[512,1280]{1,0:T(8,128)(2,1)S(1)}, bf16[512,1280]{1,0:T(8,128)(2,1)}, u32[]{:S(2)}) copy-start(bf16[512,1280]{1,0:T(8,128)(2,1)} %down_keep.1.keep_ref) | copy-start | bytes 3932164
  (3 other events, 2.4 us)

commit v4 on v3

--- a/solution.py
+++ b/solution.py
@@ -350,22 +350,23 @@
     mate = swap(xc, "dp", 2)
     near_x, near_y = together([swap(xc, "expert", by_x), swap(xc, "expert", by_y)])
     near = [xc, near_x, near_y]
-    first = near + across(*near)
+    own_far, far_near_x, far_near_y = across(*near)
+    first = [xc, near_x, own_far, far_near_x]
     corner = [swap(near_x[:half], "expert", by_y), swap(near_y[half:], "expert", by_x)]
-    made = work([first[:2], first[2:4], first[4:]], True)
+    made = work([first[:2], first[2:]], True)
     corner_x, corner_y, mate, *first_made = together([*corner, mate, *made])
     corner = [corner_x, corner_y]
-    second = corner + across(*corner) + [mate] + across(mate)
-    made = work([second[:4], second[4:]], True)
+    second = [near_y, *corner, far_near_y, *across(*corner), mate, *across(mate)]
+    made = work([second[:3], second[3:6], second[6:]], True)
     far_x, far_y, *second_made = together(
         [swap(mate, "expert", by_x), swap(mate, "expert", by_y), *made]
     )
-    third = [far_x, far_y] + across(far_x, far_y)
+    third, passed = [far_x, far_y], across(far_x, far_y)
     corner = [swap(far_x[:half], "expert", by_y), swap(far_y[half:], "expert", by_x)]
-    made = work([third[:2], third[2:]], False)
+    made = work([third], False)
     corner_x, corner_y, *third_made = together([*corner, *made])
-    fourth = [corner_x, corner_y] + across(corner_x, corner_y)
-    fourth_made = work([fourth], False)
+    fourth = [*passed, corner_x, corner_y, *across(corner_x, corner_y)]
+    fourth_made = work([fourth[:2], fourth[2:]], False)
     arrived = first + second + third + fourth
     units = [first_made, second_made, third_made, fourth_made]
     hws, dgs, dus = [[values[n] for values in units] for n in range(3)]
@@ -377,7 +378,7 @@
 
     gate_send, mates = together([*grad([dgs], mates, False, "gate_send"), mates])
     *up_send, after = together([*grad([dus], mates, False, "up_send", apart=True), mates])
-    shares = out_pass([(first_made, 6 * tok_dev), (second_made, 2 * tok_dev)], wgu, wd, after)
+    shares = out_pass([(first_made, 4 * tok_dev), (second_made, 4 * tok_dev)], wgu, wd, after)
     *shares, mates = together([*shares, after])
     down_send = grad([hws], mates, True, "down_send", apart=True)
     *values, up_last, gate_got, token = together(
@@ -385,9 +386,10 @@
         + [up_send[-1], swap(gate_send, "dp", 1), token]
     )
     shares, down_send, up_got = values[:4], values[4 : 4 + exp_dev], values[4 + exp_dev :]
-    corner = add_to(shares[2], *across(shares[3]))
+    last = add_to(shares[2], *across(shares[3]))
     chip = add_to(shares[0], *across(shares[1]))
-    corner, token = together([corner, token])
+    last, token = together([last, token])
+    of_y, corner = last[:tok_dev], last[tok_dev:]
     (down_keep,) = grad([hws], token, True, "down_keep")
     to_x, to_y, up_last, chip, down_keep, token, *down_send = together(
         [
@@ -401,7 +403,7 @@
         ]
     )
     *down_got, last_got = [swap(send, "dp", 1) for send in down_send]
-    mine_too, of_x, of_y = chip[:tok_dev], chip[tok_dev : 2 * tok_dev], chip[2 * tok_dev :]
+    mine_too, of_x = chip[:tok_dev], chip[tok_dev:]
     of_x = join([add_to(of_x[:half], to_x), of_x[half:]])
     of_y = join([of_y[:half], add_to(of_y[half:], to_y)])
     (gate_grad,) = grad([dgs], token, False, "gate_grad", got=[gate_got])

time: 234 us -> 228 us (0.974)
  local copies, waits for them, and re-layouts: 16.2 us -> 13.3 us
  transfers between devices with their start and end apart: 30 -> 30, of which waited for: 15 -> 17; matrix products, arithmetic and copies ran while one was open for 9% -> 8% of each run, Pallas kernels for 52% -> 52%
where the time goes in v4:
time: 228 us
  Pallas kernels  143 us (63%)
  waiting for transfers between devices  34.6 us (15%)
  starting transfers between devices  25.4 us (11%)
  local copies, waits for them, and re-layouts  13.3 us (6%)
  other arithmetic  10.7 us (5%)
    pallas_call x4, Pallas kernels, routes_pass(): pl.pallas_call(functools.partial(routes_kernel, counts, hid, experts, wit...  61.3 us
    pallas_call x6, Pallas kernels, grad_pass(): pl.pallas_call(functools.partial(grad_kernel, len(srcs), len(sets), len(s...  53.9 us
    ppermute x30, waiting for transfers between devices, swap(): lax.ppermute(value, axis, [(i, i ^ mask) for i in range(lax.axis_size(axi...  34.6 us
    pallas_call x1, Pallas kernels, out_pass(): pl.pallas_call(functools.partial(out_kernel, len(sections)), grid=(2 * st...  25.5 us
    ppermute x30, starting transfers between devices, swap(): lax.ppermute(value, axis, [(i, i ^ mask) for i in range(lax.axis_size(axi...  25.4 us
    concatenate x1, other arithmetic, dense_form(): jnp.concatenate([gate_proj[e] for e in range(exp_dev)] + [up_proj[e] for...  5.5 us
  transfers between devices with their start and end apart: 30, of which 17 were waited for; matrix products, arithmetic and copies ran while one was open for 8% of the time, Pallas kernels for 52%

profile of v4, /device:TPU:0, one launch (start us, length us, event | category | flops | bytes accessed | tf_op | source)
XLA Modules:
  0.0 228.1 jit_solution(2403311422933080889)
XLA Ops:
  1.7 2.3 %concatenate.12.refs_0_ = bf16[128,4224]{1,0:T(8,128)(2,1)S(1)} concatenate(bf16[128,2048]{1,0:T(8,128)(2,1)} %param.7, bf16[128,2048]{1,0:T(8,128)(2,1)} %param.10, bf16[128,16]{1,0:T(8,128)(2,1)S(1)} %copy.20, bf16[128,16]{1,0:T(8,128)(2,1)S(1)} %subtract_convert_fusion, bf16[128,96]{1,0:T(8,128)(2,1)S(1)} %broadcast_in_dim.31), dimensions={1} | concatenate | bytes 2162688 | tf_op jit(solution)/shard_map/concatenate | solution.py:332
  4.1 3.0 %collective-permute-start.1 = (bf16[128,4224]{1,0:T(8,128)(2,1)S(1)}, bf16[128,4224]{1,0:T(8,128)(2,1)S(1)}, u32[]{:S(2)}, u32[]{:S(2)}) collective-permute-start(bf16[128,4224]{1,0:T(8,128)(2,1)S(1)} %concatenate.12.refs_0_), channel_id=1, source_target_pairs={{0,4},{1,5},{2,6},{3,7},{4,0},{5,1},{6,2},{7,3},{8,12},{9,13},{10,... | collective-permute-start | bytes 3244040 | tf_op jit(solution)/shard_map/ppermute | solution.py:16
  7.1 1.5 collective-permute-start
  8.6 2.6 %collective-permute-start.6 = (bf16[128,4224]{1,0:T(8,128)(2,1)S(1)}, bf16[128,4224]{1,0:T(8,128)(2,1)}, u32[]{:S(2)}, u32[]{:S(2)}) collective-permute-start(bf16[128,4224]{1,0:T(8,128)(2,1)S(1)} %concatenate.12.refs_0_), channel_id=1, source_target_pairs={{0,16},{8,24},{16,0},{24,8},{1,17},{9,25},{17,1},{25,9},{2,18},{10... | collective-permute-start | bytes 3244040 | tf_op jit(solution)/shard_map/ppermute | solution.py:16
  11.2 4.5 %slice_bitcast_fusion.1 = (bf16[2048,640]{1,0:T(8,128)(2,1)S(1)}, bf16[2048,640]{1,0:T(8,128)(2,1)S(1)}, bf16[2048,640]{1,0:T(8,128)(2,1)S(1)}, bf16[2048,640]{1,0:T(8,128)(2,1)S(1)}) fusion(bf16[2,2048,640]{2,1,0:T(8,128)(2,1)} %param.12, bf16[2,2048,640]{2,1,0:T(8,128)(2,1)} %param.11), kind=kLoop, calls=%fused_computation.4 | loop fusion | bytes 20971520 | tf_op jit(solution)/shard_map/squeeze | solution.py:338
  15.7 15.3 %collective-permute-done.1.refs_0_.refs_4_ = bf16[128,4224]{1,0:T(8,128)(2,1)S(1)} collective-permute-done((bf16[128,4224]{1,0:T(8,128)(2,1)S(1)}, bf16[128,4224]{1,0:T(8,128)(2,1)S(1)}, u32[]{:S(2)}, u32[]{:S(2)}) %collective-permute-start.1) | collective-permute-done | bytes 1081376 | tf_op jit(solution)/shard_map/ppermute | solution.py:16
  31.0 1.5 collective-permute-done.refs_1_
  32.4 0.9 slice.73
  33.3 0.8 slice.74
  34.7 1.5 collective-permute-start.5
  36.8 5.5 %pad_maximum_fusion.refs_4_.refs_5_.refs_8_.refs_9_.refs_2_.refs_3_.refs_6_.refs_7_ = bf16[2048,2560]{1,0:T(8,128)(2,1)} fusion(bf16[2048,640]{1,0:T(8,128)(2,1)S(1)} %get-tuple-element.173, bf16[2048,640]{1,0:T(8,128)(2,1)S(1)} %get-tuple-element.172, bf16[2048,640]{1,0:T(8,128)(2,1)S(1)} %get-tuple-element.181, bf16[2048,640]{1,0:T(8,128)(2,1)S(1)} %get-tuple-element.182), kind=kLoop, calls=%fused_computation | loop fusion | flops 41943040 | bytes 20971520 | tf_op jit(solution)/shard_map/concatenate | solution.py:337
  42.3 15.3 %routes_pass.4 = (bf16[512,1280]{1,0:T(8,128)(2,1)}, bf16[512,1280]{1,0:T(8,128)(2,1)}, bf16[512,1280]{1,0:T(8,128)(2,1)}, bf16[512,128]{1,0:T(8,128)(2,1)}) custom-call(s32[1]{0:T(128)} %bitcast.1.mine_ref, bf16[128,4224]{1,0:T(8,128)(2,1)} %copy-done.1, bf16[128,4224]{1,0:T(8,128)(2,1)} %copy-done.5, bf16[128,4224]{1,0:T(8,128)(2,1)} %copy-done.7, ...), custom_call_target="tpu_custom_call" | custom-call | flops 7680 | bytes 19 | tf_op jit(solution)/shard_map/routes_pass/pallas_call | solution.py:117
  57.6 1.4 collective-permute-done.6.refs_6_.refs_10_
  60.6 2.1 collective-permute-done.8.refs_4_.refs_8_
  62.7 0.8 collective-permute-done.9.refs_5_.refs_9_
  64.3 1.0 copy-done.6
  65.3 20.7 %routes_pass.5 = (bf16[768,1280]{1,0:T(8,128)(2,1)}, bf16[768,1280]{1,0:T(8,128)(2,1)}, bf16[768,1280]{1,0:T(8,128)(2,1)}, bf16[768,128]{1,0:T(8,128)(2,1)}) custom-call(s32[1]{0:T(128)} %bitcast.1.mine_ref, bf16[128,4224]{1,0:T(8,128)(2,1)} %copy-done.2, bf16[64,4224]{1,0:T(8,128)(2,1)} %collective-permute-done.4.refs_1_.refs_5_, ...), custom_call_target="tpu_custom_call" | custom-call | flops 11520 | bytes 21 | tf_op jit(solution)/shard_map/routes_pass/pallas_call | solution.py:117
  86.1 1.1 collective-permute-start.16
  87.2 1.5 collective-permute-start.15
  89.3 10.9 %routes_pass.6 = (bf16[256,1280]{1,0:T(8,128)(2,1)}, bf16[256,1280]{1,0:T(8,128)(2,1)}, bf16[256,1280]{1,0:T(8,128)(2,1)}) custom-call(s32[1]{0:T(128)} %bitcast.1.mine_ref, bf16[128,4224]{1,0:T(8,128)(2,1)} %copy-done.4, bf16[128,4224]{1,0:T(8,128)(2,1)} %copy-done.3, ...), custom_call_target="tpu_custom_call" | custom-call | flops 3840 | bytes 17 | tf_op jit(solution)/shard_map/routes_pass/pallas_call | solution.py:117
  100.6 0.8 collective-permute-done.15.refs_2_.refs_16_
  101.9 1.8 collective-permute-done.17.refs_4_.refs_18_
  103.7 0.8 collective-permute-done.18.refs_5_.refs_19_
  104.4 14.4 %routes_pass.7 = (bf16[512,1280]{1,0:T(8,128)(2,1)}, bf16[512,1280]{1,0:T(8,128)(2,1)}, bf16[512,1280]{1,0:T(8,128)(2,1)}) custom-call(s32[1]{0:T(128)} %bitcast.1.mine_ref, bf16[128,4224]{1,0:T(8,128)(2,1)} %copy-done.8, bf16[128,4224]{1,0:T(8,128)(2,1)} %collective-permute-done.14.refs_1_.refs_15_, ...), custom_call_target="tpu_custom_call" | custom-call | flops 7680 | bytes 19 | tf_op jit(solution)/shard_map/routes_pass/pallas_call | solution.py:117
  118.9 8.4 %gate_send.1 = bf16[512,1280]{1,0:T(8,128)(2,1)} custom-call(s32[1]{0:T(128)} %bitcast.block_ref.token_ref, bf16[128,4224]{1,0:T(8,128)(2,1)} %copy-done.1, bf16[128,4224]{1,0:T(8,128)(2,1)} %copy-done.5, bf16[128,4224]{1,0:T(8,128)(2,1)} %copy-done.7, bf16[128,4224]{1,0:T(8,128)(2,1)} %collective-permute-done.3.refs_3_, bf16[128,4224]{1,0:T(8,128)(2,1)} %copy-done.2, ...), custom_call_target="tpu_custom_call" | custom-call | flops 2560 | bytes 8 | tf_op jit(solution)/shard_map/gate_send/pallas_call | solution.py:275
  127.3 1.2 collective-permute-start.20
  128.5 8.6 %up_send.1 = (bf16[512,640]{1,0:T(8,128)(2,1)}, bf16[512,640]{1,0:T(8,128)(2,1)}) custom-call(s32[1]{0:T(128)} %bitcast.block_ref.token_ref, bf16[128,4224]{1,0:T(8,128)(2,1)} %copy-done.1, bf16[128,4224]{1,0:T(8,128)(2,1)} %copy-done.5, bf16[128,4224]{1,0:T(8,128)(2,1)} %copy-done.7, bf16[128,4224]{1,0:T(8,128)(2,1)} %collective-permute-done.3.refs_3_, ...), custom_call_target="tpu_custom_call" | custom-call | flops 2560 | bytes 8 | tf_op jit(solution)/shard_map/up_send/pallas_call | solution.py:275
  137.0 1.1 collective-permute-start.19
  138.1 25.5 %out_pass.1 = (bf16[256,4224]{1,0:T(8,128)(2,1)}, bf16[256,4224]{1,0:T(8,128)(2,1)}, bf16[256,4224]{1,0:T(8,128)(2,1)}, bf16[256,4224]{1,0:T(8,128)(2,1)}) custom-call(s32[1]{0:T(128)} %bitcast.block_ref.token_ref, bf16[512,1280]{1,0:T(8,128)(2,1)} %get-tuple-element.119.refs_0_.refs_20_, bf16[512,1280]{1,0:T(8,128)(2,1)} %get-tuple-element.107.refs_20_.refs_1_, ...), custom_call_target="tpu_custom_call" | custom-call | flops 15360 | bytes 23 | tf_op jit(solution)/shard_map/out_pass/pallas_call | solution.py:192
  163.6 8.7 %down_send.1 = (bf16[512,640]{1,0:T(8,128)(2,1)}, bf16[512,640]{1,0:T(8,128)(2,1)}) custom-call(s32[1]{0:T(128)S(6)} %add.27.block_ref, bf16[128,4224]{1,0:T(8,128)(2,1)} %copy-done.1, bf16[128,4224]{1,0:T(8,128)(2,1)} %copy-done.5, bf16[128,4224]{1,0:T(8,128)(2,1)} %copy-done.7, bf16[128,4224]{1,0:T(8,128)(2,1)} %collective-permute-done.3.refs_3_, ...), custom_call_target="tpu_custom_call" | custom-call | flops 2560 | bytes 8 | tf_op jit(solution)/shard_map/down_send/pallas_call | solution.py:275
  172.5 1.2 collective-permute-start.24
  173.8 2.9 %collective-permute-done.21 = bf16[256,4224]{1,0:T(8,128)(2,1)S(1)} collective-permute-done((bf16[256,4224]{1,0:T(8,128)(2,1)S(1)}, bf16[256,4224]{1,0:T(8,128)(2,1)S(1)}, u32[]{:S(2)}, u32[]{:S(2)}) %collective-permute-start.21) | collective-permute-done | bytes 2162720 | tf_op jit(solution)/shard_map/ppermute | solution.py:16
  177.4 1.0 collective-permute-start.23
  178.5 1.1 collective-permute-start.22
  180.6 8.3 %down_keep.1.keep_ref = bf16[512,1280]{1,0:T(8,128)(2,1)} custom-call(s32[1]{0:T(128)S(6)} %add.30.block_ref, bf16[128,4224]{1,0:T(8,128)(2,1)} %copy-done.1, bf16[128,4224]{1,0:T(8,128)(2,1)} %copy-done.5, bf16[128,4224]{1,0:T(8,128)(2,1)} %copy-done.7, bf16[128,4224]{1,0:T(8,128)(2,1)} %collective-permute-done.3.refs_3_, bf16[128,4224]{1,0:T(8,128)(2,1)} %copy-done.2, ...), custom_call_target="tpu_custom_call" | custom-call | flops 2560 | bytes 8 | tf_op jit(solution)/shard_map/down_keep/pallas_call | solution.py:275
  188.8 1.0 collective-permute-done.24.refs_25_
  189.9 1.9 collective-permute-done.23
  192.9 1.1 collective-permute-start.26
  194.0 1.1 pad_maximum_fusion.2
  195.1 1.5 collective-permute-start.27
  197.2 1.4 collective-permute-start.29
  198.7 9.8 %gate_grad.1 = f32[512,2,640]{2,1,0:T(2,128)} custom-call(s32[1]{0:T(128)} %bitcast.7.block_ref, bf16[128,4224]{1,0:T(8,128)(2,1)} %copy-done.1, bf16[128,4224]{1,0:T(8,128)(2,1)} %copy-done.5, bf16[128,4224]{1,0:T(8,128)(2,1)} %copy-done.7, bf16[128,4224]{1,0:T(8,128)(2,1)} %collective-permute-done.3.refs_3_, bf16[128,4224]{1,0:T(8,128)(2,1)} %copy-done.2, ...), custom_call_target="tpu_custom_call" | custom-call | flops 2560 | bytes 8 | tf_op jit(solution)/shard_map/gate_grad/pallas_call | solution.py:275
  208.5 10.1 %up_grad.1 = f32[512,2,640]{2,1,0:T(2,128)} custom-call(s32[1]{0:T(128)} %bitcast.7.block_ref, bf16[128,4224]{1,0:T(8,128)(2,1)} %copy-done.1, bf16[128,4224]{1,0:T(8,128)(2,1)} %copy-done.5, bf16[128,4224]{1,0:T(8,128)(2,1)} %copy-done.7, bf16[128,4224]{1,0:T(8,128)(2,1)} %collective-permute-done.3.refs_3_, bf16[128,4224]{1,0:T(8,128)(2,1)} %copy-done.2, ...), custom_call_target="tpu_custom_call" | custom-call | flops 2560 | bytes 8 | tf_op jit(solution)/shard_map/up_grad/pallas_call | solution.py:275
  218.7 1.1 collective-permute-done.27
  219.8 1.4 fusion
  222.0 2.3 fusion.2
  224.3 1.5 collective-permute-done.29.refs_1_
  225.7 2.3 %sum_pass.1 = f32[512,2,640]{2,1,0:T(2,128)} custom-call(bf16[512,1280]{1,0:T(8,128)(2,1)S(1)} %copy-done, bf16[512,640]{1,0:T(8,128)(2,1)S(1)} %collective-permute-done.28.refs_0_, bf16[512,640]{1,0:T(8,128)(2,1)S(1)} %collective-permute-done.29.refs_1_), custom_call_target="tpu_custom_call" | custom-call | tf_op jit(solution)/shard_map/sum_pass/pallas_call | solution.py:306
  (89 shorter events, 10.6 us)
Async XLA Ops:
  4.1 11.6 %copy-start.1 = (bf16[128,4224]{1,0:T(8,128)(2,1)}, bf16[128,4224]{1,0:T(8,128)(2,1)S(1)}, u32[]{:S(2)}) copy-start(bf16[128,4224]{1,0:T(8,128)(2,1)S(1)} %concatenate.12.refs_0_) | copy-start | bytes 3244036
  4.1 26.9 %collective-permute-start.1 = (bf16[128,4224]{1,0:T(8,128)(2,1)S(1)}, bf16[128,4224]{1,0:T(8,128)(2,1)S(1)}, u32[]{:S(2)}, u32[]{:S(2)}) collective-permute-start(bf16[128,4224]{1,0:T(8,128)(2,1)S(1)} %concatenate.12.refs_0_), channel_id=1, source_target_pairs={{0,4},{1,5},{2,6},{3,7},{4,0},{5,1},{6,2},{7,3},{8,12},{9,13},{10,... | collective-permute-start | bytes 3244040 | tf_op jit(solution)/shard_map/ppermute | solution.py:16
  7.1 25.3 %collective-permute-start = (bf16[128,4224]{1,0:T(8,128)(2,1)S(1)}, bf16[128,4224]{1,0:T(8,128)(2,1)S(1)}, u32[]{:S(2)}, u32[]{:S(2)}) collective-permute-start(bf16[128,4224]{1,0:T(8,128)(2,1)S(1)} %concatenate.12.refs_0_), channel_id=1, source_target_pairs={{0,2},{1,3},{2,0},{3,1},{4,6},{5,7},{6,4},{7,5},{8,10},{9,11},{10,... | collective-permute-start | bytes 3244040 | tf_op jit(solution)/shard_map/ppermute | solution.py:16
  8.6 27.6 %collective-permute-start.2 = (bf16[128,4224]{1,0:T(8,128)(2,1)S(1)}, bf16[128,4224]{1,0:T(8,128)(2,1)S(1)}, u32[]{:S(2)}, u32[]{:S(2)}) collective-permute-start(bf16[128,4224]{1,0:T(8,128)(2,1)S(1)} %concatenate.12.refs_0_), channel_id=1, source_target_pairs={{0,1},{1,0},{2,3},{3,2},{4,5},{5,4},{6,7},{7,6},{8,9},{9,8},{10,11... | collective-permute-start | bytes 3244040 | tf_op jit(solution)/shard_map/ppermute | solution.py:16
  8.6 50.5 %collective-permute-start.6 = (bf16[128,4224]{1,0:T(8,128)(2,1)S(1)}, bf16[128,4224]{1,0:T(8,128)(2,1)}, u32[]{:S(2)}, u32[]{:S(2)}) collective-permute-start(bf16[128,4224]{1,0:T(8,128)(2,1)S(1)} %concatenate.12.refs_0_), channel_id=1, source_target_pairs={{0,16},{8,24},{16,0},{24,8},{1,17},{9,25},{17,1},{25,9},{2,18},{10... | collective-permute-start | bytes 3244040 | tf_op jit(solution)/shard_map/ppermute | solution.py:16
  31.0 11.4 %copy-start.2 = (bf16[128,4224]{1,0:T(8,128)(2,1)}, bf16[128,4224]{1,0:T(8,128)(2,1)S(1)}, u32[]{:S(2)}) copy-start(bf16[128,4224]{1,0:T(8,128)(2,1)S(1)} %collective-permute-done.1.refs_0_.refs_4_) | copy-start | bytes 3244036
  32.4 9.9 %copy-start.5 = (bf16[128,4224]{1,0:T(8,128)(2,1)}, bf16[128,4224]{1,0:T(8,128)(2,1)S(1)}, u32[]{:S(2)}) copy-start(bf16[128,4224]{1,0:T(8,128)(2,1)S(1)} %collective-permute-done.refs_1_) | copy-start | bytes 3244036
  33.3 9.0 %collective-permute-start.3 = (bf16[128,4224]{1,0:T(8,128)(2,1)S(1)}, bf16[128,4224]{1,0:T(8,128)(2,1)}, u32[]{:S(2)}, u32[]{:S(2)}) collective-permute-start(bf16[128,4224]{1,0:T(8,128)(2,1)S(1)} %collective-permute-done.refs_1_), channel_id=1, source_target_pairs={{0,1},{1,0},{2,3},{3,2},{4,5},{5,4},{6,7},{7,6},{8,9},{9,8},{10,11... | collective-permute-start | bytes 3244040 | tf_op jit(solution)/shard_map/ppermute | solution.py:16
  34.2 26.0 %collective-permute-start.7 = (bf16[128,4224]{1,0:T(8,128)(2,1)S(1)}, bf16[128,4224]{1,0:T(8,128)(2,1)}, u32[]{:S(2)}, u32[]{:S(2)}) collective-permute-start(bf16[128,4224]{1,0:T(8,128)(2,1)S(1)} %collective-permute-done.1.refs_0_.refs_4_), channel_id=1, source_target_pairs={{0,1},{1,0},{2,3},{3,2},{4,5},{5,4},{6,7},{7,6},{8,9},{9,8},{10,11... | collective-permute-start | bytes 3244040 | tf_op jit(solution)/shard_map/ppermute | solution.py:16
  34.7 24.4 %collective-permute-start.5 = (bf16[64,4224]{1,0:T(8,128)(2,1)}, bf16[64,4224]{1,0:T(8,128)(2,1)}, u32[]{:S(2)}, u32[]{:S(2)}) collective-permute-start(bf16[64,4224]{1,0:T(8,128)(2,1)} %slice.74), channel_id=1, source_target_pairs={{0,2},{1,3},{2,0},{3,1},{4,6},{5,7},{6,4},{7,5},{8,10},{9,11},{10,... | collective-permute-start | bytes 1622024 | tf_op jit(solution)/shard_map/ppermute | solution.py:16
  36.2 6.2 %copy-start.7 = (bf16[128,4224]{1,0:T(8,128)(2,1)}, bf16[128,4224]{1,0:T(8,128)(2,1)S(1)}, u32[]{:S(2)}) copy-start(bf16[128,4224]{1,0:T(8,128)(2,1)S(1)} %collective-permute-done.2.refs_2_) | copy-start | bytes 3244036
  36.2 22.9 %collective-permute-start.4 = (bf16[64,4224]{1,0:T(8,128)(2,1)}, bf16[64,4224]{1,0:T(8,128)(2,1)}, u32[]{:S(2)}, u32[]{:S(2)}) collective-permute-start(bf16[64,4224]{1,0:T(8,128)(2,1)} %slice.73), channel_id=1, source_target_pairs={{0,4},{1,5},{2,6},{3,7},{4,0},{5,1},{6,2},{7,3},{8,12},{9,13},{10,... | collective-permute-start | bytes 1622024 | tf_op jit(solution)/shard_map/ppermute | solution.py:16
  59.1 4.5 %collective-permute-start.10 = (bf16[128,4224]{1,0:T(8,128)(2,1)}, bf16[128,4224]{1,0:T(8,128)(2,1)S(1)}, u32[]{:S(2)}, u32[]{:S(2)}) collective-permute-start(bf16[128,4224]{1,0:T(8,128)(2,1)} %collective-permute-done.6.refs_6_.refs_10_), channel_id=1, source_target_pairs={{0,1},{1,0},{2,3},{3,2},{4,5},{5,4},{6,7},{7,6},{8,9},{9,8},{10,11... | collective-permute-start | bytes 3244040 | tf_op jit(solution)/shard_map/ppermute | solution.py:16
  59.1 26.9 %collective-permute-start.12 = (bf16[128,4224]{1,0:T(8,128)(2,1)}, bf16[128,4224]{1,0:T(8,128)(2,1)S(1)}, u32[]{:S(2)}, u32[]{:S(2)}) collective-permute-start(bf16[128,4224]{1,0:T(8,128)(2,1)} %collective-permute-done.6.refs_6_.refs_10_), channel_id=1, source_target_pairs={{0,4},{1,5},{2,6},{3,7},{4,0},{5,1},{6,2},{7,3},{8,12},{9,13},{10,... | collective-permute-start | bytes 3244040 | tf_op jit(solution)/shard_map/ppermute | solution.py:16
  59.6 26.4 %collective-permute-start.11 = (bf16[128,4224]{1,0:T(8,128)(2,1)}, bf16[128,4224]{1,0:T(8,128)(2,1)S(1)}, u32[]{:S(2)}, u32[]{:S(2)}) collective-permute-start(bf16[128,4224]{1,0:T(8,128)(2,1)} %collective-permute-done.6.refs_6_.refs_10_), channel_id=1, source_target_pairs={{0,2},{1,3},{2,0},{3,1},{4,6},{5,7},{6,4},{7,5},{8,10},{9,11},{10,... | collective-permute-start | bytes 3244040 | tf_op jit(solution)/shard_map/ppermute | solution.py:16
  60.1 2.6 %collective-permute-start.8 = (bf16[64,4224]{1,0:T(8,128)(2,1)}, bf16[64,4224]{1,0:T(8,128)(2,1)S(1)}, u32[]{:S(2)}, u32[]{:S(2)}) collective-permute-start(bf16[64,4224]{1,0:T(8,128)(2,1)} %collective-permute-done.4.refs_1_.refs_5_), channel_id=1, source_target_pairs={{0,1},{1,0},{2,3},{3,2},{4,5},{5,4},{6,7},{7,6},{8,9},{9,8},{10,11... | collective-permute-start | bytes 1622024 | tf_op jit(solution)/shard_map/ppermute | solution.py:16
  60.1 3.4 %collective-permute-start.9 = (bf16[64,4224]{1,0:T(8,128)(2,1)}, bf16[64,4224]{1,0:T(8,128)(2,1)S(1)}, u32[]{:S(2)}, u32[]{:S(2)}) collective-permute-start(bf16[64,4224]{1,0:T(8,128)(2,1)} %collective-permute-done.5.refs_2_.refs_6_), channel_id=1, source_target_pairs={{0,1},{1,0},{2,3},{3,2},{4,5},{5,4},{6,7},{7,6},{8,9},{9,8},{10,11... | collective-permute-start | bytes 1622024 | tf_op jit(solution)/shard_map/ppermute | solution.py:16
  62.7 0.8 copy-start.9
  64.3 1.0 copy-start.6
  86.0 3.3 %copy-start.3 = (bf16[128,4224]{1,0:T(8,128)(2,1)}, bf16[128,4224]{1,0:T(8,128)(2,1)S(1)}, u32[]{:S(2)}) copy-start(bf16[128,4224]{1,0:T(8,128)(2,1)S(1)} %collective-permute-done.12.refs_1_.refs_13_) | copy-start | bytes 3244036
  86.0 3.3 %copy-start.4 = (bf16[128,4224]{1,0:T(8,128)(2,1)}, bf16[128,4224]{1,0:T(8,128)(2,1)S(1)}, u32[]{:S(2)}) copy-start(bf16[128,4224]{1,0:T(8,128)(2,1)S(1)} %collective-permute-done.11.refs_0_.refs_12_) | copy-start | bytes 3244036
  86.1 14.5 %collective-permute-start.16 = (bf16[64,4224]{1,0:T(8,128)(2,1)S(1)}, bf16[64,4224]{1,0:T(8,128)(2,1)}, u32[]{:S(2)}, u32[]{:S(2)}) collective-permute-start(bf16[64,4224]{1,0:T(8,128)(2,1)S(1)} %slice.80), channel_id=1, source_target_pairs={{0,2},{1,3},{2,0},{3,1},{4,6},{5,7},{6,4},{7,5},{8,10},{9,11},{10,... | collective-permute-start | bytes 1622024 | tf_op jit(solution)/shard_map/ppermute | solution.py:16
  87.2 14.1 %collective-permute-start.15 = (bf16[64,4224]{1,0:T(8,128)(2,1)S(1)}, bf16[64,4224]{1,0:T(8,128)(2,1)}, u32[]{:S(2)}, u32[]{:S(2)}) collective-permute-start(bf16[64,4224]{1,0:T(8,128)(2,1)S(1)} %slice.79), channel_id=1, source_target_pairs={{0,4},{1,5},{2,6},{3,7},{4,0},{5,1},{6,2},{7,3},{8,12},{9,13},{10,... | collective-permute-start | bytes 1622024 | tf_op jit(solution)/shard_map/ppermute | solution.py:16
  88.8 13.1 %collective-permute-start.13 = (bf16[128,4224]{1,0:T(8,128)(2,1)S(1)}, bf16[128,4224]{1,0:T(8,128)(2,1)S(1)}, u32[]{:S(2)}, u32[]{:S(2)}) collective-permute-start(bf16[128,4224]{1,0:T(8,128)(2,1)S(1)} %collective-permute-done.11.refs_0_.refs_12_), channel_id=1, source_target_pairs={{0,1},{1,0},{2,3},{3,2},{4,5},{5,4},{6,7},{7,6},{8,9},{9,8},{10,11... | collective-permute-start | bytes 3244040 | tf_op jit(solution)/shard_map/ppermute | solution.py:16
  88.8 13.1 %collective-permute-start.14 = (bf16[128,4224]{1,0:T(8,128)(2,1)S(1)}, bf16[128,4224]{1,0:T(8,128)(2,1)}, u32[]{:S(2)}, u32[]{:S(2)}) collective-permute-start(bf16[128,4224]{1,0:T(8,128)(2,1)S(1)} %collective-permute-done.12.refs_1_.refs_13_), channel_id=1, source_target_pairs={{0,1},{1,0},{2,3},{3,2},{4,5},{5,4},{6,7},{7,6},{8,9},{9,8},{10,11... | collective-permute-start | bytes 3244040 | tf_op jit(solution)/shard_map/ppermute | solution.py:16
  101.4 2.3 collective-permute-start.17
  101.4 3.0 %collective-permute-start.18 = (bf16[64,4224]{1,0:T(8,128)(2,1)}, bf16[64,4224]{1,0:T(8,128)(2,1)}, u32[]{:S(2)}, u32[]{:S(2)}) collective-permute-start(bf16[64,4224]{1,0:T(8,128)(2,1)} %collective-permute-done.16.refs_3_.refs_17_), channel_id=1, source_target_pairs={{0,1},{1,0},{2,3},{3,2},{4,5},{5,4},{6,7},{7,6},{8,9},{9,8},{10,11... | collective-permute-start | bytes 1622024 | tf_op jit(solution)/shard_map/ppermute | solution.py:16
  101.9 2.5 %copy-start.8 = (bf16[128,4224]{1,0:T(8,128)(2,1)}, bf16[128,4224]{1,0:T(8,128)(2,1)S(1)}, u32[]{:S(2)}) copy-start(bf16[128,4224]{1,0:T(8,128)(2,1)S(1)} %collective-permute-done.13.refs_0_.refs_14_) | copy-start | bytes 3244036
  127.3 45.1 %collective-permute-start.20 = (bf16[512,1280]{1,0:T(8,128)(2,1)}, bf16[512,1280]{1,0:T(8,128)(2,1)S(1)}, u32[]{:S(2)}, u32[]{:S(2)}) collective-permute-start(bf16[512,1280]{1,0:T(8,128)(2,1)} %gate_send.1), channel_id=1, source_target_pairs={{0,8},{8,0},{16,24},{24,16},{1,9},{9,1},{17,25},{25,17},{2,10},{10... | collective-permute-start | bytes 3932168 | tf_op jit(solution)/shard_map/ppermute | solution.py:16
  137.0 35.4 %collective-permute-start.19 = (bf16[512,640]{1,0:T(8,128)(2,1)}, bf16[512,640]{1,0:T(8,128)(2,1)S(1)}, u32[]{:S(2)}, u32[]{:S(2)}) collective-permute-start(bf16[512,640]{1,0:T(8,128)(2,1)} %get-tuple-element.136), channel_id=1, source_target_pairs={{0,8},{8,0},{16,24},{24,16},{1,9},{9,1},{17,25},{25,17},{2,10},{10... | collective-permute-start | bytes 1966088 | tf_op jit(solution)/shard_map/ppermute | solution.py:16
  163.6 8.9 %copy-start.17 = (bf16[256,4224]{1,0:T(8,128)(2,1)S(1)}, bf16[256,4224]{1,0:T(8,128)(2,1)}, u32[]{:S(2)}) copy-start(bf16[256,4224]{1,0:T(8,128)(2,1)} %get-tuple-element.140) | copy-start | bytes 6488068
  163.6 13.2 %copy-start.12 = (bf16[256,4224]{1,0:T(8,128)(2,1)S(1)}, bf16[256,4224]{1,0:T(8,128)(2,1)}, u32[]{:S(2)}) copy-start(bf16[256,4224]{1,0:T(8,128)(2,1)} %get-tuple-element.139) | copy-start | bytes 6488068
  172.4 4.8 %copy-start.14 = (bf16[512,640]{1,0:T(8,128)(2,1)}, bf16[512,640]{1,0:T(8,128)(2,1)S(1)}, u32[]{:S(2)}) copy-start(bf16[512,640]{1,0:T(8,128)(2,1)S(1)} %collective-permute-done.19.refs_24_) | copy-start | bytes 1966084
  172.4 4.8 %copy-start.13 = (bf16[512,1280]{1,0:T(8,128)(2,1)}, bf16[512,1280]{1,0:T(8,128)(2,1)S(1)}, u32[]{:S(2)}) copy-start(bf16[512,1280]{1,0:T(8,128)(2,1)S(1)} %collective-permute-done.20.refs_24_) | copy-start | bytes 3932164
  172.4 4.3 %collective-permute-start.21 = (bf16[256,4224]{1,0:T(8,128)(2,1)S(1)}, bf16[256,4224]{1,0:T(8,128)(2,1)S(1)}, u32[]{:S(2)}, u32[]{:S(2)}) collective-permute-start(bf16[256,4224]{1,0:T(8,128)(2,1)S(1)} %copy-done.17), channel_id=1, source_target_pairs={{0,1},{1,0},{2,3},{3,2},{4,5},{5,4},{6,7},{7,6},{8,9},{9,8},{10,11... | collective-permute-start | bytes 6488072 | tf_op jit(solution)/shard_map/ppermute | solution.py:16
  172.5 17.4 %collective-permute-start.24 = (bf16[512,640]{1,0:T(8,128)(2,1)}, bf16[512,640]{1,0:T(8,128)(2,1)S(1)}, u32[]{:S(2)}, u32[]{:S(2)}) collective-permute-start(bf16[512,640]{1,0:T(8,128)(2,1)} %get-tuple-element.143), channel_id=1, source_target_pairs={{0,8},{8,0},{16,24},{24,16},{1,9},{9,1},{17,25},{25,17},{2,10},{10... | collective-permute-start | bytes 1966088 | tf_op jit(solution)/shard_map/ppermute | solution.py:16
  173.7 6.4 %collective-permute-start.25 = (bf16[256,4224]{1,0:T(8,128)(2,1)}, bf16[256,4224]{1,0:T(8,128)(2,1)S(1)}, u32[]{:S(2)}, u32[]{:S(2)}) collective-permute-start(bf16[256,4224]{1,0:T(8,128)(2,1)} %get-tuple-element.145), channel_id=1, source_target_pairs={{0,1},{1,0},{2,3},{3,2},{4,5},{5,4},{6,7},{7,6},{8,9},{9,8},{10,11... | collective-permute-start | bytes 6488072 | tf_op jit(solution)/shard_map/ppermute | solution.py:16
  177.3 2.8 %copy-start.11 = (bf16[256,4224]{1,0:T(8,128)(2,1)S(1)}, bf16[256,4224]{1,0:T(8,128)(2,1)}, u32[]{:S(2)}) copy-start(bf16[256,4224]{1,0:T(8,128)(2,1)} %get-tuple-element.144) | copy-start | bytes 6488068
  177.4 14.4 %collective-permute-start.23 = (bf16[64,4224]{1,0:T(8,128)(2,1)S(1)}, bf16[64,4224]{1,0:T(8,128)(2,1)S(1)}, u32[]{:S(2)}, u32[]{:S(2)}) collective-permute-start(bf16[64,4224]{1,0:T(8,128)(2,1)S(1)} %get-tuple-element.175), channel_id=1, source_target_pairs={{0,2},{1,3},{2,0},{3,1},{4,6},{5,7},{6,4},{7,5},{8,10},{9,11},{10,... | collective-permute-start | bytes 1622024 | tf_op jit(solution)/shard_map/ppermute | solution.py:16
  178.5 14.0 %collective-permute-start.22 = (bf16[64,4224]{1,0:T(8,128)(2,1)S(1)}, bf16[64,4224]{1,0:T(8,128)(2,1)S(1)}, u32[]{:S(2)}, u32[]{:S(2)}) collective-permute-start(bf16[64,4224]{1,0:T(8,128)(2,1)S(1)} %get-tuple-element.176), channel_id=1, source_target_pairs={{0,4},{1,5},{2,6},{3,7},{4,0},{5,1},{6,2},{7,3},{8,12},{9,13},{10,... | collective-permute-start | bytes 1622024 | tf_op jit(solution)/shard_map/ppermute | solution.py:16
  189.9 2.9 %copy-start.15 = (bf16[512,640]{1,0:T(8,128)(2,1)}, bf16[512,640]{1,0:T(8,128)(2,1)S(1)}, u32[]{:S(2)}) copy-start(bf16[512,640]{1,0:T(8,128)(2,1)S(1)} %collective-permute-done.24.refs_25_) | copy-start | bytes 1966084
  192.8 3.8 %copy-start.18 = (bf16[512,640]{1,0:T(8,128)(2,1)S(1)}, bf16[512,640]{1,0:T(8,128)(2,1)}, u32[]{:S(2)}) copy-start(bf16[512,640]{1,0:T(8,128)(2,1)} %get-tuple-element.156) | copy-start | bytes 1966084
  192.9 25.7 %collective-permute-start.26 = (bf16[128,4224]{1,0:T(8,128)(2,1)S(1)}, bf16[128,4224]{1,0:T(8,128)(2,1)S(1)}, u32[]{:S(2)}, u32[]{:S(2)}) collective-permute-start(bf16[128,4224]{1,0:T(8,128)(2,1)S(1)} %pad_maximum_fusion.1), channel_id=1, source_target_pairs={{0,2},{1,3},{2,0},{3,1},{4,6},{5,7},{6,4},{7,5},{8,10},{9,11},{10,... | collective-permute-start | bytes 3244040 | tf_op jit(solution)/shard_map/ppermute | solution.py:16
  195.1 24.7 %collective-permute-start.27 = (bf16[128,4224]{1,0:T(8,128)(2,1)}, bf16[128,4224]{1,0:T(8,128)(2,1)S(1)}, u32[]{:S(2)}, u32[]{:S(2)}) collective-permute-start(bf16[128,4224]{1,0:T(8,128)(2,1)} %pad_maximum_fusion.2), channel_id=1, source_target_pairs={{0,4},{1,5},{2,6},{3,7},{4,0},{5,1},{6,2},{7,3},{8,12},{9,13},{10,... | collective-permute-start | bytes 3244040 | tf_op jit(solution)/shard_map/ppermute | solution.py:16
  196.6 22.0 %collective-permute-start.28 = (bf16[512,640]{1,0:T(8,128)(2,1)S(1)}, bf16[512,640]{1,0:T(8,128)(2,1)S(1)}, u32[]{:S(2)}, u32[]{:S(2)}) collective-permute-start(bf16[512,640]{1,0:T(8,128)(2,1)S(1)} %copy-done.18), channel_id=1, source_target_pairs={{0,8},{8,0},{16,24},{24,16},{1,9},{9,1},{17,25},{25,17},{2,10},{10... | collective-permute-start | bytes 1966088 | tf_op jit(solution)/shard_map/ppermute | solution.py:16
  197.2 28.5 %collective-permute-start.29 = (bf16[512,640]{1,0:T(8,128)(2,1)}, bf16[512,640]{1,0:T(8,128)(2,1)S(1)}, u32[]{:S(2)}, u32[]{:S(2)}) collective-permute-start(bf16[512,640]{1,0:T(8,128)(2,1)} %get-tuple-element.159), channel_id=1, source_target_pairs={{0,8},{8,0},{16,24},{24,16},{1,9},{9,1},{17,25},{25,17},{2,10},{10... | collective-permute-start | bytes 1966088 | tf_op jit(solution)/shard_map/ppermute | solution.py:16
  218.6 2.7 %copy-start.16 = (s32[128,8]{0,1:T(8,128)S(1)}, s32[128,8]{0,1:T(8,128)}, u32[]{:S(2)}) copy-start(s32[128,8]{0,1:T(8,128)} %param.8) | copy-start | bytes 12292
  221.2 4.5 %copy-start = (bf16[512,1280]{1,0:T(8,128)(2,1)S(1)}, bf16[512,1280]{1,0:T(8,128)(2,1)}, u32[]{:S(2)}) copy-start(bf16[512,1280]{1,0:T(8,128)(2,1)} %down_keep.1.keep_ref) | copy-start | bytes 3932164
  (1 other events, 0.8 us)

commit v5 on v4

--- a/solution.py
+++ b/solution.py
@@ -302,7 +302,7 @@
 
 def sum_pass(keep, gots):
     rows, cols = keep.shape
-    tile, hid = min(128, rows), cols // len(gots)
+    tile, hid = min(256, rows), cols // len(gots)
     return pl.pallas_call(
         sum_kernel,
         grid=(rows // tile,),

time: 228 us -> 228 us (level)
  no operation moved by 1% of the time
where the time goes in v5:
time: 228 us
  Pallas kernels  143 us (63%)
  waiting for transfers between devices  34.6 us (15%)
  starting transfers between devices  25.4 us (11%)
  local copies, waits for them, and re-layouts  13.3 us (6%)
  other arithmetic  10.7 us (5%)
    pallas_call x4, Pallas kernels, routes_pass(): pl.pallas_call(functools.partial(routes_kernel, counts, hid, experts, wit...  61.3 us
    pallas_call x6, Pallas kernels, grad_pass(): pl.pallas_call(functools.partial(grad_kernel, len(srcs), len(sets), len(s...  53.9 us
    ppermute x30, waiting for transfers between devices, swap(): lax.ppermute(value, axis, [(i, i ^ mask) for i in range(lax.axis_size(axi...  34.6 us
    pallas_call x1, Pallas kernels, out_pass(): pl.pallas_call(functools.partial(out_kernel, len(sections)), grid=(2 * st...  25.5 us
    ppermute x30, starting transfers between devices, swap(): lax.ppermute(value, axis, [(i, i ^ mask) for i in range(lax.axis_size(axi...  25.4 us
    concatenate x1, other arithmetic, dense_form(): jnp.concatenate([gate_proj[e] for e in range(exp_dev)] + [up_proj[e] for...  5.5 us
  transfers between devices with their start and end apart: 30, of which 17 were waited for; matrix products, arithmetic and copies ran while one was open for 8% of the time, Pallas kernels for 52%

profile of v5, /device:TPU:0, one launch (start us, length us, event | category | flops | bytes accessed | tf_op | source)
XLA Modules:
  0.0 227.6 jit_solution(7017138771307106200)
XLA Ops:
  1.7 2.3 %concatenate.12.refs_0_ = bf16[128,4224]{1,0:T(8,128)(2,1)S(1)} concatenate(bf16[128,2048]{1,0:T(8,128)(2,1)} %param.7, bf16[128,2048]{1,0:T(8,128)(2,1)} %param.10, bf16[128,16]{1,0:T(8,128)(2,1)S(1)} %copy.20, bf16[128,16]{1,0:T(8,128)(2,1)S(1)} %subtract_convert_fusion, bf16[128,96]{1,0:T(8,128)(2,1)S(1)} %broadcast_in_dim.31), dimensions={1} | concatenate | bytes 2162688 | tf_op jit(solution)/shard_map/concatenate | solution.py:332
  4.1 3.0 %collective-permute-start.1 = (bf16[128,4224]{1,0:T(8,128)(2,1)S(1)}, bf16[128,4224]{1,0:T(8,128)(2,1)S(1)}, u32[]{:S(2)}, u32[]{:S(2)}) collective-permute-start(bf16[128,4224]{1,0:T(8,128)(2,1)S(1)} %concatenate.12.refs_0_), channel_id=1, source_target_pairs={{0,4},{1,5},{2,6},{3,7},{4,0},{5,1},{6,2},{7,3},{8,12},{9,13},{10,... | collective-permute-start | bytes 3244040 | tf_op jit(solution)/shard_map/ppermute | solution.py:16
  7.1 1.5 collective-permute-start
  8.6 2.6 %collective-permute-start.6 = (bf16[128,4224]{1,0:T(8,128)(2,1)S(1)}, bf16[128,4224]{1,0:T(8,128)(2,1)}, u32[]{:S(2)}, u32[]{:S(2)}) collective-permute-start(bf16[128,4224]{1,0:T(8,128)(2,1)S(1)} %concatenate.12.refs_0_), channel_id=1, source_target_pairs={{0,16},{8,24},{16,0},{24,8},{1,17},{9,25},{17,1},{25,9},{2,18},{10... | collective-permute-start | bytes 3244040 | tf_op jit(solution)/shard_map/ppermute | solution.py:16
  11.2 4.5 %slice_bitcast_fusion.1 = (bf16[2048,640]{1,0:T(8,128)(2,1)S(1)}, bf16[2048,640]{1,0:T(8,128)(2,1)S(1)}, bf16[2048,640]{1,0:T(8,128)(2,1)S(1)}, bf16[2048,640]{1,0:T(8,128)(2,1)S(1)}) fusion(bf16[2,2048,640]{2,1,0:T(8,128)(2,1)} %param.12, bf16[2,2048,640]{2,1,0:T(8,128)(2,1)} %param.11), kind=kLoop, calls=%fused_computation.4 | loop fusion | bytes 20971520 | tf_op jit(solution)/shard_map/squeeze | solution.py:338
  15.7 15.3 %collective-permute-done.1.refs_0_.refs_4_ = bf16[128,4224]{1,0:T(8,128)(2,1)S(1)} collective-permute-done((bf16[128,4224]{1,0:T(8,128)(2,1)S(1)}, bf16[128,4224]{1,0:T(8,128)(2,1)S(1)}, u32[]{:S(2)}, u32[]{:S(2)}) %collective-permute-start.1) | collective-permute-done | bytes 1081376 | tf_op jit(solution)/shard_map/ppermute | solution.py:16
  31.0 1.5 collective-permute-done.refs_1_
  32.4 0.9 slice.73
  33.3 0.8 slice.74
  34.7 1.5 collective-permute-start.5
  36.8 5.5 %pad_maximum_fusion.refs_4_.refs_5_.refs_8_.refs_9_.refs_2_.refs_3_.refs_6_.refs_7_ = bf16[2048,2560]{1,0:T(8,128)(2,1)} fusion(bf16[2048,640]{1,0:T(8,128)(2,1)S(1)} %get-tuple-element.173, bf16[2048,640]{1,0:T(8,128)(2,1)S(1)} %get-tuple-element.172, bf16[2048,640]{1,0:T(8,128)(2,1)S(1)} %get-tuple-element.181, bf16[2048,640]{1,0:T(8,128)(2,1)S(1)} %get-tuple-element.182), kind=kLoop, calls=%fused_computation | loop fusion | flops 41943040 | bytes 20971520 | tf_op jit(solution)/shard_map/concatenate | solution.py:337
  42.3 15.3 %routes_pass.4 = (bf16[512,1280]{1,0:T(8,128)(2,1)}, bf16[512,1280]{1,0:T(8,128)(2,1)}, bf16[512,1280]{1,0:T(8,128)(2,1)}, bf16[512,128]{1,0:T(8,128)(2,1)}) custom-call(s32[1]{0:T(128)} %bitcast.1.mine_ref, bf16[128,4224]{1,0:T(8,128)(2,1)} %copy-done.1, bf16[128,4224]{1,0:T(8,128)(2,1)} %copy-done.5, bf16[128,4224]{1,0:T(8,128)(2,1)} %copy-done.7, ...), custom_call_target="tpu_custom_call" | custom-call | flops 7680 | bytes 19 | tf_op jit(solution)/shard_map/routes_pass/pallas_call | solution.py:117
  57.6 1.4 collective-permute-done.6.refs_6_.refs_10_
  60.6 2.1 collective-permute-done.8.refs_4_.refs_8_
  62.7 0.8 collective-permute-done.9.refs_5_.refs_9_
  64.3 1.0 copy-done.6
  65.3 20.7 %routes_pass.5 = (bf16[768,1280]{1,0:T(8,128)(2,1)}, bf16[768,1280]{1,0:T(8,128)(2,1)}, bf16[768,1280]{1,0:T(8,128)(2,1)}, bf16[768,128]{1,0:T(8,128)(2,1)}) custom-call(s32[1]{0:T(128)} %bitcast.1.mine_ref, bf16[128,4224]{1,0:T(8,128)(2,1)} %copy-done.2, bf16[64,4224]{1,0:T(8,128)(2,1)} %collective-permute-done.4.refs_1_.refs_5_, ...), custom_call_target="tpu_custom_call" | custom-call | flops 11520 | bytes 21 | tf_op jit(solution)/shard_map/routes_pass/pallas_call | solution.py:117
  86.1 1.1 collective-permute-start.16
  87.2 1.5 collective-permute-start.15
  89.3 10.9 %routes_pass.6 = (bf16[256,1280]{1,0:T(8,128)(2,1)}, bf16[256,1280]{1,0:T(8,128)(2,1)}, bf16[256,1280]{1,0:T(8,128)(2,1)}) custom-call(s32[1]{0:T(128)} %bitcast.1.mine_ref, bf16[128,4224]{1,0:T(8,128)(2,1)} %copy-done.4, bf16[128,4224]{1,0:T(8,128)(2,1)} %copy-done.3, ...), custom_call_target="tpu_custom_call" | custom-call | flops 3840 | bytes 17 | tf_op jit(solution)/shard_map/routes_pass/pallas_call | solution.py:117
  100.6 0.8 collective-permute-done.15.refs_2_.refs_16_
  101.9 1.8 collective-permute-done.17.refs_4_.refs_18_
  103.7 0.8 collective-permute-done.18.refs_5_.refs_19_
  104.4 14.4 %routes_pass.7 = (bf16[512,1280]{1,0:T(8,128)(2,1)}, bf16[512,1280]{1,0:T(8,128)(2,1)}, bf16[512,1280]{1,0:T(8,128)(2,1)}) custom-call(s32[1]{0:T(128)} %bitcast.1.mine_ref, bf16[128,4224]{1,0:T(8,128)(2,1)} %copy-done.8, bf16[128,4224]{1,0:T(8,128)(2,1)} %collective-permute-done.14.refs_1_.refs_15_, ...), custom_call_target="tpu_custom_call" | custom-call | flops 7680 | bytes 19 | tf_op jit(solution)/shard_map/routes_pass/pallas_call | solution.py:117
  118.9 8.4 %gate_send.1 = bf16[512,1280]{1,0:T(8,128)(2,1)} custom-call(s32[1]{0:T(128)} %bitcast.block_ref.token_ref, bf16[128,4224]{1,0:T(8,128)(2,1)} %copy-done.1, bf16[128,4224]{1,0:T(8,128)(2,1)} %copy-done.5, bf16[128,4224]{1,0:T(8,128)(2,1)} %copy-done.7, bf16[128,4224]{1,0:T(8,128)(2,1)} %collective-permute-done.3.refs_3_, bf16[128,4224]{1,0:T(8,128)(2,1)} %copy-done.2, ...), custom_call_target="tpu_custom_call" | custom-call | flops 2560 | bytes 8 | tf_op jit(solution)/shard_map/gate_send/pallas_call | solution.py:275
  127.3 1.2 collective-permute-start.20
  128.5 8.6 %up_send.1 = (bf16[512,640]{1,0:T(8,128)(2,1)}, bf16[512,640]{1,0:T(8,128)(2,1)}) custom-call(s32[1]{0:T(128)} %bitcast.block_ref.token_ref, bf16[128,4224]{1,0:T(8,128)(2,1)} %copy-done.1, bf16[128,4224]{1,0:T(8,128)(2,1)} %copy-done.5, bf16[128,4224]{1,0:T(8,128)(2,1)} %copy-done.7, bf16[128,4224]{1,0:T(8,128)(2,1)} %collective-permute-done.3.refs_3_, ...), custom_call_target="tpu_custom_call" | custom-call | flops 2560 | bytes 8 | tf_op jit(solution)/shard_map/up_send/pallas_call | solution.py:275
  137.0 1.1 collective-permute-start.19
  138.1 25.5 %out_pass.1 = (bf16[256,4224]{1,0:T(8,128)(2,1)}, bf16[256,4224]{1,0:T(8,128)(2,1)}, bf16[256,4224]{1,0:T(8,128)(2,1)}, bf16[256,4224]{1,0:T(8,128)(2,1)}) custom-call(s32[1]{0:T(128)} %bitcast.block_ref.token_ref, bf16[512,1280]{1,0:T(8,128)(2,1)} %get-tuple-element.119.refs_0_.refs_20_, bf16[512,1280]{1,0:T(8,128)(2,1)} %get-tuple-element.107.refs_20_.refs_1_, ...), custom_call_target="tpu_custom_call" | custom-call | flops 15360 | bytes 23 | tf_op jit(solution)/shard_map/out_pass/pallas_call | solution.py:192
  163.6 8.7 %down_send.1 = (bf16[512,640]{1,0:T(8,128)(2,1)}, bf16[512,640]{1,0:T(8,128)(2,1)}) custom-call(s32[1]{0:T(128)S(6)} %add.27.block_ref, bf16[128,4224]{1,0:T(8,128)(2,1)} %copy-done.1, bf16[128,4224]{1,0:T(8,128)(2,1)} %copy-done.5, bf16[128,4224]{1,0:T(8,128)(2,1)} %copy-done.7, bf16[128,4224]{1,0:T(8,128)(2,1)} %collective-permute-done.3.refs_3_, ...), custom_call_target="tpu_custom_call" | custom-call | flops 2560 | bytes 8 | tf_op jit(solution)/shard_map/down_send/pallas_call | solution.py:275
  172.5 1.2 collective-permute-start.24
  173.8 2.9 %collective-permute-done.21 = bf16[256,4224]{1,0:T(8,128)(2,1)S(1)} collective-permute-done((bf16[256,4224]{1,0:T(8,128)(2,1)S(1)}, bf16[256,4224]{1,0:T(8,128)(2,1)S(1)}, u32[]{:S(2)}, u32[]{:S(2)}) %collective-permute-start.21) | collective-permute-done | bytes 2162720 | tf_op jit(solution)/shard_map/ppermute | solution.py:16
  177.4 1.0 collective-permute-start.23
  178.5 1.1 collective-permute-start.22
  180.6 8.3 %down_keep.1.keep_ref = bf16[512,1280]{1,0:T(8,128)(2,1)} custom-call(s32[1]{0:T(128)S(6)} %add.30.block_ref, bf16[128,4224]{1,0:T(8,128)(2,1)} %copy-done.1, bf16[128,4224]{1,0:T(8,128)(2,1)} %copy-done.5, bf16[128,4224]{1,0:T(8,128)(2,1)} %copy-done.7, bf16[128,4224]{1,0:T(8,128)(2,1)} %collective-permute-done.3.refs_3_, bf16[128,4224]{1,0:T(8,128)(2,1)} %copy-done.2, ...), custom_call_target="tpu_custom_call" | custom-call | flops 2560 | bytes 8 | tf_op jit(solution)/shard_map/down_keep/pallas_call | solution.py:275
  188.8 1.0 collective-permute-done.24.refs_25_
  189.9 1.9 collective-permute-done.23
  192.9 1.1 collective-permute-start.26
  194.0 1.1 pad_maximum_fusion.2
  195.1 1.5 collective-permute-start.27
  197.2 1.4 collective-permute-start.29
  198.7 9.8 %gate_grad.1 = f32[512,2,640]{2,1,0:T(2,128)} custom-call(s32[1]{0:T(128)} %bitcast.7.block_ref, bf16[128,4224]{1,0:T(8,128)(2,1)} %copy-done.1, bf16[128,4224]{1,0:T(8,128)(2,1)} %copy-done.5, bf16[128,4224]{1,0:T(8,128)(2,1)} %copy-done.7, bf16[128,4224]{1,0:T(8,128)(2,1)} %collective-permute-done.3.refs_3_, bf16[128,4224]{1,0:T(8,128)(2,1)} %copy-done.2, ...), custom_call_target="tpu_custom_call" | custom-call | flops 2560 | bytes 8 | tf_op jit(solution)/shard_map/gate_grad/pallas_call | solution.py:275
  208.5 10.1 %up_grad.1 = f32[512,2,640]{2,1,0:T(2,128)} custom-call(s32[1]{0:T(128)} %bitcast.7.block_ref, bf16[128,4224]{1,0:T(8,128)(2,1)} %copy-done.1, bf16[128,4224]{1,0:T(8,128)(2,1)} %copy-done.5, bf16[128,4224]{1,0:T(8,128)(2,1)} %copy-done.7, bf16[128,4224]{1,0:T(8,128)(2,1)} %collective-permute-done.3.refs_3_, bf16[128,4224]{1,0:T(8,128)(2,1)} %copy-done.2, ...), custom_call_target="tpu_custom_call" | custom-call | flops 2560 | bytes 8 | tf_op jit(solution)/shard_map/up_grad/pallas_call | solution.py:275
  218.7 1.1 collective-permute-done.27
  219.8 1.4 fusion
  222.0 2.3 fusion.2
  224.3 1.5 collective-permute-done.29.refs_1_
  225.7 1.9 sum_pass.1
  (89 shorter events, 10.6 us)
Async XLA Ops:
  4.1 11.6 %copy-start.1 = (bf16[128,4224]{1,0:T(8,128)(2,1)}, bf16[128,4224]{1,0:T(8,128)(2,1)S(1)}, u32[]{:S(2)}) copy-start(bf16[128,4224]{1,0:T(8,128)(2,1)S(1)} %concatenate.12.refs_0_) | copy-start | bytes 3244036
  4.1 26.9 %collective-permute-start.1 = (bf16[128,4224]{1,0:T(8,128)(2,1)S(1)}, bf16[128,4224]{1,0:T(8,128)(2,1)S(1)}, u32[]{:S(2)}, u32[]{:S(2)}) collective-permute-start(bf16[128,4224]{1,0:T(8,128)(2,1)S(1)} %concatenate.12.refs_0_), channel_id=1, source_target_pairs={{0,4},{1,5},{2,6},{3,7},{4,0},{5,1},{6,2},{7,3},{8,12},{9,13},{10,... | collective-permute-start | bytes 3244040 | tf_op jit(solution)/shard_map/ppermute | solution.py:16
  7.1 25.3 %collective-permute-start = (bf16[128,4224]{1,0:T(8,128)(2,1)S(1)}, bf16[128,4224]{1,0:T(8,128)(2,1)S(1)}, u32[]{:S(2)}, u32[]{:S(2)}) collective-permute-start(bf16[128,4224]{1,0:T(8,128)(2,1)S(1)} %concatenate.12.refs_0_), channel_id=1, source_target_pairs={{0,2},{1,3},{2,0},{3,1},{4,6},{5,7},{6,4},{7,5},{8,10},{9,11},{10,... | collective-permute-start | bytes 3244040 | tf_op jit(solution)/shard_map/ppermute | solution.py:16
  8.6 27.6 %collective-permute-start.2 = (bf16[128,4224]{1,0:T(8,128)(2,1)S(1)}, bf16[128,4224]{1,0:T(8,128)(2,1)S(1)}, u32[]{:S(2)}, u32[]{:S(2)}) collective-permute-start(bf16[128,4224]{1,0:T(8,128)(2,1)S(1)} %concatenate.12.refs_0_), channel_id=1, source_target_pairs={{0,1},{1,0},{2,3},{3,2},{4,5},{5,4},{6,7},{7,6},{8,9},{9,8},{10,11... | collective-permute-start | bytes 3244040 | tf_op jit(solution)/shard_map/ppermute | solution.py:16
  8.6 50.5 %collective-permute-start.6 = (bf16[128,4224]{1,0:T(8,128)(2,1)S(1)}, bf16[128,4224]{1,0:T(8,128)(2,1)}, u32[]{:S(2)}, u32[]{:S(2)}) collective-permute-start(bf16[128,4224]{1,0:T(8,128)(2,1)S(1)} %concatenate.12.refs_0_), channel_id=1, source_target_pairs={{0,16},{8,24},{16,0},{24,8},{1,17},{9,25},{17,1},{25,9},{2,18},{10... | collective-permute-start | bytes 3244040 | tf_op jit(solution)/shard_map/ppermute | solution.py:16
  31.0 11.4 %copy-start.2 = (bf16[128,4224]{1,0:T(8,128)(2,1)}, bf16[128,4224]{1,0:T(8,128)(2,1)S(1)}, u32[]{:S(2)}) copy-start(bf16[128,4224]{1,0:T(8,128)(2,1)S(1)} %collective-permute-done.1.refs_0_.refs_4_) | copy-start | bytes 3244036
  32.4 9.9 %copy-start.5 = (bf16[128,4224]{1,0:T(8,128)(2,1)}, bf16[128,4224]{1,0:T(8,128)(2,1)S(1)}, u32[]{:S(2)}) copy-start(bf16[128,4224]{1,0:T(8,128)(2,1)S(1)} %collective-permute-done.refs_1_) | copy-start | bytes 3244036
  33.3 9.0 %collective-permute-start.3 = (bf16[128,4224]{1,0:T(8,128)(2,1)S(1)}, bf16[128,4224]{1,0:T(8,128)(2,1)}, u32[]{:S(2)}, u32[]{:S(2)}) collective-permute-start(bf16[128,4224]{1,0:T(8,128)(2,1)S(1)} %collective-permute-done.refs_1_), channel_id=1, source_target_pairs={{0,1},{1,0},{2,3},{3,2},{4,5},{5,4},{6,7},{7,6},{8,9},{9,8},{10,11... | collective-permute-start | bytes 3244040 | tf_op jit(solution)/shard_map/ppermute | solution.py:16
  34.2 26.0 %collective-permute-start.7 = (bf16[128,4224]{1,0:T(8,128)(2,1)S(1)}, bf16[128,4224]{1,0:T(8,128)(2,1)}, u32[]{:S(2)}, u32[]{:S(2)}) collective-permute-start(bf16[128,4224]{1,0:T(8,128)(2,1)S(1)} %collective-permute-done.1.refs_0_.refs_4_), channel_id=1, source_target_pairs={{0,1},{1,0},{2,3},{3,2},{4,5},{5,4},{6,7},{7,6},{8,9},{9,8},{10,11... | collective-permute-start | bytes 3244040 | tf_op jit(solution)/shard_map/ppermute | solution.py:16
  34.7 24.4 %collective-permute-start.5 = (bf16[64,4224]{1,0:T(8,128)(2,1)}, bf16[64,4224]{1,0:T(8,128)(2,1)}, u32[]{:S(2)}, u32[]{:S(2)}) collective-permute-start(bf16[64,4224]{1,0:T(8,128)(2,1)} %slice.74), channel_id=1, source_target_pairs={{0,2},{1,3},{2,0},{3,1},{4,6},{5,7},{6,4},{7,5},{8,10},{9,11},{10,... | collective-permute-start | bytes 1622024 | tf_op jit(solution)/shard_map/ppermute | solution.py:16
  36.2 6.2 %copy-start.7 = (bf16[128,4224]{1,0:T(8,128)(2,1)}, bf16[128,4224]{1,0:T(8,128)(2,1)S(1)}, u32[]{:S(2)}) copy-start(bf16[128,4224]{1,0:T(8,128)(2,1)S(1)} %collective-permute-done.2.refs_2_) | copy-start | bytes 3244036
  36.2 22.9 %collective-permute-start.4 = (bf16[64,4224]{1,0:T(8,128)(2,1)}, bf16[64,4224]{1,0:T(8,128)(2,1)}, u32[]{:S(2)}, u32[]{:S(2)}) collective-permute-start(bf16[64,4224]{1,0:T(8,128)(2,1)} %slice.73), channel_id=1, source_target_pairs={{0,4},{1,5},{2,6},{3,7},{4,0},{5,1},{6,2},{7,3},{8,12},{9,13},{10,... | collective-permute-start | bytes 1622024 | tf_op jit(solution)/shard_map/ppermute | solution.py:16
  59.1 4.5 %collective-permute-start.10 = (bf16[128,4224]{1,0:T(8,128)(2,1)}, bf16[128,4224]{1,0:T(8,128)(2,1)S(1)}, u32[]{:S(2)}, u32[]{:S(2)}) collective-permute-start(bf16[128,4224]{1,0:T(8,128)(2,1)} %collective-permute-done.6.refs_6_.refs_10_), channel_id=1, source_target_pairs={{0,1},{1,0},{2,3},{3,2},{4,5},{5,4},{6,7},{7,6},{8,9},{9,8},{10,11... | collective-permute-start | bytes 3244040 | tf_op jit(solution)/shard_map/ppermute | solution.py:16
  59.1 26.9 %collective-permute-start.12 = (bf16[128,4224]{1,0:T(8,128)(2,1)}, bf16[128,4224]{1,0:T(8,128)(2,1)S(1)}, u32[]{:S(2)}, u32[]{:S(2)}) collective-permute-start(bf16[128,4224]{1,0:T(8,128)(2,1)} %collective-permute-done.6.refs_6_.refs_10_), channel_id=1, source_target_pairs={{0,4},{1,5},{2,6},{3,7},{4,0},{5,1},{6,2},{7,3},{8,12},{9,13},{10,... | collective-permute-start | bytes 3244040 | tf_op jit(solution)/shard_map/ppermute | solution.py:16
  59.6 26.4 %collective-permute-start.11 = (bf16[128,4224]{1,0:T(8,128)(2,1)}, bf16[128,4224]{1,0:T(8,128)(2,1)S(1)}, u32[]{:S(2)}, u32[]{:S(2)}) collective-permute-start(bf16[128,4224]{1,0:T(8,128)(2,1)} %collective-permute-done.6.refs_6_.refs_10_), channel_id=1, source_target_pairs={{0,2},{1,3},{2,0},{3,1},{4,6},{5,7},{6,4},{7,5},{8,10},{9,11},{10,... | collective-permute-start | bytes 3244040 | tf_op jit(solution)/shard_map/ppermute | solution.py:16
  60.1 2.6 %collective-permute-start.8 = (bf16[64,4224]{1,0:T(8,128)(2,1)}, bf16[64,4224]{1,0:T(8,128)(2,1)S(1)}, u32[]{:S(2)}, u32[]{:S(2)}) collective-permute-start(bf16[64,4224]{1,0:T(8,128)(2,1)} %collective-permute-done.4.refs_1_.refs_5_), channel_id=1, source_target_pairs={{0,1},{1,0},{2,3},{3,2},{4,5},{5,4},{6,7},{7,6},{8,9},{9,8},{10,11... | collective-permute-start | bytes 1622024 | tf_op jit(solution)/shard_map/ppermute | solution.py:16
  60.1 3.4 %collective-permute-start.9 = (bf16[64,4224]{1,0:T(8,128)(2,1)}, bf16[64,4224]{1,0:T(8,128)(2,1)S(1)}, u32[]{:S(2)}, u32[]{:S(2)}) collective-permute-start(bf16[64,4224]{1,0:T(8,128)(2,1)} %collective-permute-done.5.refs_2_.refs_6_), channel_id=1, source_target_pairs={{0,1},{1,0},{2,3},{3,2},{4,5},{5,4},{6,7},{7,6},{8,9},{9,8},{10,11... | collective-permute-start | bytes 1622024 | tf_op jit(solution)/shard_map/ppermute | solution.py:16
  62.7 0.8 copy-start.9
  64.3 1.0 copy-start.6
  86.0 3.3 %copy-start.3 = (bf16[128,4224]{1,0:T(8,128)(2,1)}, bf16[128,4224]{1,0:T(8,128)(2,1)S(1)}, u32[]{:S(2)}) copy-start(bf16[128,4224]{1,0:T(8,128)(2,1)S(1)} %collective-permute-done.12.refs_1_.refs_13_) | copy-start | bytes 3244036
  86.0 3.3 %copy-start.4 = (bf16[128,4224]{1,0:T(8,128)(2,1)}, bf16[128,4224]{1,0:T(8,128)(2,1)S(1)}, u32[]{:S(2)}) copy-start(bf16[128,4224]{1,0:T(8,128)(2,1)S(1)} %collective-permute-done.11.refs_0_.refs_12_) | copy-start | bytes 3244036
  86.1 14.5 %collective-permute-start.16 = (bf16[64,4224]{1,0:T(8,128)(2,1)S(1)}, bf16[64,4224]{1,0:T(8,128)(2,1)}, u32[]{:S(2)}, u32[]{:S(2)}) collective-permute-start(bf16[64,4224]{1,0:T(8,128)(2,1)S(1)} %slice.80), channel_id=1, source_target_pairs={{0,2},{1,3},{2,0},{3,1},{4,6},{5,7},{6,4},{7,5},{8,10},{9,11},{10,... | collective-permute-start | bytes 1622024 | tf_op jit(solution)/shard_map/ppermute | solution.py:16
  87.2 14.1 %collective-permute-start.15 = (bf16[64,4224]{1,0:T(8,128)(2,1)S(1)}, bf16[64,4224]{1,0:T(8,128)(2,1)}, u32[]{:S(2)}, u32[]{:S(2)}) collective-permute-start(bf16[64,4224]{1,0:T(8,128)(2,1)S(1)} %slice.79), channel_id=1, source_target_pairs={{0,4},{1,5},{2,6},{3,7},{4,0},{5,1},{6,2},{7,3},{8,12},{9,13},{10,... | collective-permute-start | bytes 1622024 | tf_op jit(solution)/shard_map/ppermute | solution.py:16
  88.8 13.1 %collective-permute-start.13 = (bf16[128,4224]{1,0:T(8,128)(2,1)S(1)}, bf16[128,4224]{1,0:T(8,128)(2,1)S(1)}, u32[]{:S(2)}, u32[]{:S(2)}) collective-permute-start(bf16[128,4224]{1,0:T(8,128)(2,1)S(1)} %collective-permute-done.11.refs_0_.refs_12_), channel_id=1, source_target_pairs={{0,1},{1,0},{2,3},{3,2},{4,5},{5,4},{6,7},{7,6},{8,9},{9,8},{10,11... | collective-permute-start | bytes 3244040 | tf_op jit(solution)/shard_map/ppermute | solution.py:16
  88.8 13.1 %collective-permute-start.14 = (bf16[128,4224]{1,0:T(8,128)(2,1)S(1)}, bf16[128,4224]{1,0:T(8,128)(2,1)}, u32[]{:S(2)}, u32[]{:S(2)}) collective-permute-start(bf16[128,4224]{1,0:T(8,128)(2,1)S(1)} %collective-permute-done.12.refs_1_.refs_13_), channel_id=1, source_target_pairs={{0,1},{1,0},{2,3},{3,2},{4,5},{5,4},{6,7},{7,6},{8,9},{9,8},{10,11... | collective-permute-start | bytes 3244040 | tf_op jit(solution)/shard_map/ppermute | solution.py:16
  101.4 2.3 collective-permute-start.17
  101.4 3.0 %collective-permute-start.18 = (bf16[64,4224]{1,0:T(8,128)(2,1)}, bf16[64,4224]{1,0:T(8,128)(2,1)}, u32[]{:S(2)}, u32[]{:S(2)}) collective-permute-start(bf16[64,4224]{1,0:T(8,128)(2,1)} %collective-permute-done.16.refs_3_.refs_17_), channel_id=1, source_target_pairs={{0,1},{1,0},{2,3},{3,2},{4,5},{5,4},{6,7},{7,6},{8,9},{9,8},{10,11... | collective-permute-start | bytes 1622024 | tf_op jit(solution)/shard_map/ppermute | solution.py:16
  101.9 2.5 %copy-start.8 = (bf16[128,4224]{1,0:T(8,128)(2,1)}, bf16[128,4224]{1,0:T(8,128)(2,1)S(1)}, u32[]{:S(2)}) copy-start(bf16[128,4224]{1,0:T(8,128)(2,1)S(1)} %collective-permute-done.13.refs_0_.refs_14_) | copy-start | bytes 3244036
  127.3 45.1 %collective-permute-start.20 = (bf16[512,1280]{1,0:T(8,128)(2,1)}, bf16[512,1280]{1,0:T(8,128)(2,1)S(1)}, u32[]{:S(2)}, u32[]{:S(2)}) collective-permute-start(bf16[512,1280]{1,0:T(8,128)(2,1)} %gate_send.1), channel_id=1, source_target_pairs={{0,8},{8,0},{16,24},{24,16},{1,9},{9,1},{17,25},{25,17},{2,10},{10... | collective-permute-start | bytes 3932168 | tf_op jit(solution)/shard_map/ppermute | solution.py:16
  137.0 35.4 %collective-permute-start.19 = (bf16[512,640]{1,0:T(8,128)(2,1)}, bf16[512,640]{1,0:T(8,128)(2,1)S(1)}, u32[]{:S(2)}, u32[]{:S(2)}) collective-permute-start(bf16[512,640]{1,0:T(8,128)(2,1)} %get-tuple-element.136), channel_id=1, source_target_pairs={{0,8},{8,0},{16,24},{24,16},{1,9},{9,1},{17,25},{25,17},{2,10},{10... | collective-permute-start | bytes 1966088 | tf_op jit(solution)/shard_map/ppermute | solution.py:16
  163.6 8.9 %copy-start.17 = (bf16[256,4224]{1,0:T(8,128)(2,1)S(1)}, bf16[256,4224]{1,0:T(8,128)(2,1)}, u32[]{:S(2)}) copy-start(bf16[256,4224]{1,0:T(8,128)(2,1)} %get-tuple-element.140) | copy-start | bytes 6488068
  163.6 13.2 %copy-start.12 = (bf16[256,4224]{1,0:T(8,128)(2,1)S(1)}, bf16[256,4224]{1,0:T(8,128)(2,1)}, u32[]{:S(2)}) copy-start(bf16[256,4224]{1,0:T(8,128)(2,1)} %get-tuple-element.139) | copy-start | bytes 6488068
  172.4 4.8 %copy-start.14 = (bf16[512,640]{1,0:T(8,128)(2,1)}, bf16[512,640]{1,0:T(8,128)(2,1)S(1)}, u32[]{:S(2)}) copy-start(bf16[512,640]{1,0:T(8,128)(2,1)S(1)} %collective-permute-done.19.refs_24_) | copy-start | bytes 1966084
  172.4 4.8 %copy-start.13 = (bf16[512,1280]{1,0:T(8,128)(2,1)}, bf16[512,1280]{1,0:T(8,128)(2,1)S(1)}, u32[]{:S(2)}) copy-start(bf16[512,1280]{1,0:T(8,128)(2,1)S(1)} %collective-permute-done.20.refs_24_) | copy-start | bytes 3932164
  172.4 4.3 %collective-permute-start.21 = (bf16[256,4224]{1,0:T(8,128)(2,1)S(1)}, bf16[256,4224]{1,0:T(8,128)(2,1)S(1)}, u32[]{:S(2)}, u32[]{:S(2)}) collective-permute-start(bf16[256,4224]{1,0:T(8,128)(2,1)S(1)} %copy-done.17), channel_id=1, source_target_pairs={{0,1},{1,0},{2,3},{3,2},{4,5},{5,4},{6,7},{7,6},{8,9},{9,8},{10,11... | collective-permute-start | bytes 6488072 | tf_op jit(solution)/shard_map/ppermute | solution.py:16
  172.5 17.4 %collective-permute-start.24 = (bf16[512,640]{1,0:T(8,128)(2,1)}, bf16[512,640]{1,0:T(8,128)(2,1)S(1)}, u32[]{:S(2)}, u32[]{:S(2)}) collective-permute-start(bf16[512,640]{1,0:T(8,128)(2,1)} %get-tuple-element.143), channel_id=1, source_target_pairs={{0,8},{8,0},{16,24},{24,16},{1,9},{9,1},{17,25},{25,17},{2,10},{10... | collective-permute-start | bytes 1966088 | tf_op jit(solution)/shard_map/ppermute | solution.py:16
  173.7 6.4 %collective-permute-start.25 = (bf16[256,4224]{1,0:T(8,128)(2,1)}, bf16[256,4224]{1,0:T(8,128)(2,1)S(1)}, u32[]{:S(2)}, u32[]{:S(2)}) collective-permute-start(bf16[256,4224]{1,0:T(8,128)(2,1)} %get-tuple-element.145), channel_id=1, source_target_pairs={{0,1},{1,0},{2,3},{3,2},{4,5},{5,4},{6,7},{7,6},{8,9},{9,8},{10,11... | collective-permute-start | bytes 6488072 | tf_op jit(solution)/shard_map/ppermute | solution.py:16
  177.3 2.8 %copy-start.11 = (bf16[256,4224]{1,0:T(8,128)(2,1)S(1)}, bf16[256,4224]{1,0:T(8,128)(2,1)}, u32[]{:S(2)}) copy-start(bf16[256,4224]{1,0:T(8,128)(2,1)} %get-tuple-element.144) | copy-start | bytes 6488068
  177.4 14.4 %collective-permute-start.23 = (bf16[64,4224]{1,0:T(8,128)(2,1)S(1)}, bf16[64,4224]{1,0:T(8,128)(2,1)S(1)}, u32[]{:S(2)}, u32[]{:S(2)}) collective-permute-start(bf16[64,4224]{1,0:T(8,128)(2,1)S(1)} %get-tuple-element.175), channel_id=1, source_target_pairs={{0,2},{1,3},{2,0},{3,1},{4,6},{5,7},{6,4},{7,5},{8,10},{9,11},{10,... | collective-permute-start | bytes 1622024 | tf_op jit(solution)/shard_map/ppermute | solution.py:16
  178.5 14.0 %collective-permute-start.22 = (bf16[64,4224]{1,0:T(8,128)(2,1)S(1)}, bf16[64,4224]{1,0:T(8,128)(2,1)S(1)}, u32[]{:S(2)}, u32[]{:S(2)}) collective-permute-start(bf16[64,4224]{1,0:T(8,128)(2,1)S(1)} %get-tuple-element.176), channel_id=1, source_target_pairs={{0,4},{1,5},{2,6},{3,7},{4,0},{5,1},{6,2},{7,3},{8,12},{9,13},{10,... | collective-permute-start | bytes 1622024 | tf_op jit(solution)/shard_map/ppermute | solution.py:16
  189.9 2.9 %copy-start.15 = (bf16[512,640]{1,0:T(8,128)(2,1)}, bf16[512,640]{1,0:T(8,128)(2,1)S(1)}, u32[]{:S(2)}) copy-start(bf16[512,640]{1,0:T(8,128)(2,1)S(1)} %collective-permute-done.24.refs_25_) | copy-start | bytes 1966084
  192.8 3.8 %copy-start.18 = (bf16[512,640]{1,0:T(8,128)(2,1)S(1)}, bf16[512,640]{1,0:T(8,128)(2,1)}, u32[]{:S(2)}) copy-start(bf16[512,640]{1,0:T(8,128)(2,1)} %get-tuple-element.156) | copy-start | bytes 1966084
  192.9 25.7 %collective-permute-start.26 = (bf16[128,4224]{1,0:T(8,128)(2,1)S(1)}, bf16[128,4224]{1,0:T(8,128)(2,1)S(1)}, u32[]{:S(2)}, u32[]{:S(2)}) collective-permute-start(bf16[128,4224]{1,0:T(8,128)(2,1)S(1)} %pad_maximum_fusion.1), channel_id=1, source_target_pairs={{0,2},{1,3},{2,0},{3,1},{4,6},{5,7},{6,4},{7,5},{8,10},{9,11},{10,... | collective-permute-start | bytes 3244040 | tf_op jit(solution)/shard_map/ppermute | solution.py:16
  195.1 24.7 %collective-permute-start.27 = (bf16[128,4224]{1,0:T(8,128)(2,1)}, bf16[128,4224]{1,0:T(8,128)(2,1)S(1)}, u32[]{:S(2)}, u32[]{:S(2)}) collective-permute-start(bf16[128,4224]{1,0:T(8,128)(2,1)} %pad_maximum_fusion.2), channel_id=1, source_target_pairs={{0,4},{1,5},{2,6},{3,7},{4,0},{5,1},{6,2},{7,3},{8,12},{9,13},{10,... | collective-permute-start | bytes 3244040 | tf_op jit(solution)/shard_map/ppermute | solution.py:16
  196.6 22.0 %collective-permute-start.28 = (bf16[512,640]{1,0:T(8,128)(2,1)S(1)}, bf16[512,640]{1,0:T(8,128)(2,1)S(1)}, u32[]{:S(2)}, u32[]{:S(2)}) collective-permute-start(bf16[512,640]{1,0:T(8,128)(2,1)S(1)} %copy-done.18), channel_id=1, source_target_pairs={{0,8},{8,0},{16,24},{24,16},{1,9},{9,1},{17,25},{25,17},{2,10},{10... | collective-permute-start | bytes 1966088 | tf_op jit(solution)/shard_map/ppermute | solution.py:16
  197.2 28.5 %collective-permute-start.29 = (bf16[512,640]{1,0:T(8,128)(2,1)}, bf16[512,640]{1,0:T(8,128)(2,1)S(1)}, u32[]{:S(2)}, u32[]{:S(2)}) collective-permute-start(bf16[512,640]{1,0:T(8,128)(2,1)} %get-tuple-element.159), channel_id=1, source_target_pairs={{0,8},{8,0},{16,24},{24,16},{1,9},{9,1},{17,25},{25,17},{2,10},{10... | collective-permute-start | bytes 1966088 | tf_op jit(solution)/shard_map/ppermute | solution.py:16
  218.6 2.7 %copy-start.16 = (s32[128,8]{0,1:T(8,128)S(1)}, s32[128,8]{0,1:T(8,128)}, u32[]{:S(2)}) copy-start(s32[128,8]{0,1:T(8,128)} %param.8) | copy-start | bytes 12292
  221.2 4.5 %copy-start = (bf16[512,1280]{1,0:T(8,128)(2,1)S(1)}, bf16[512,1280]{1,0:T(8,128)(2,1)}, u32[]{:S(2)}) copy-start(bf16[512,1280]{1,0:T(8,128)(2,1)} %down_keep.1.keep_ref) | copy-start | bytes 3932164
  (1 other events, 0.8 us)
